TPU v7x, 512 devices: a whole 4x8x8 slice. The times are simulated.
512 devices in a mesh: row: 64 (over y, z), col: 8 (over x, core).
Axes of the slice: x: 4, y: 8, z: 8, core: 2. Of those that a mesh axis runs over, the one named last changes fastest.
Arguments:
- hidden: bfloat16 [98304, 7168], P('row', 'col'), may hold values from -60 to 60, as said below
- test_matrix: bfloat16 [7168, 256], P('col'), may hold values from -6 to 6
Outputs:
- basis: float32 [98304, 256], P(('row', 'col'))
- factor: float32 [256, 256], replicated
Inputs may be any that keep to these rules, and one draw needn't show every extreme that they name: `hidden`: hidden states of 98304 tokens.
All inputs are finite; a program needn't handle non-finite values.
Results may differ from a plain program's by a relative error of at most 0.003.
Values may be sent and summed in bfloat16 or wider, within the bound.
No kernel may reach another device: no remote copies, remote signals or barrier semaphores. Data moves between devices by JAX's collectives and lax.ppermute only.
A program may use at most 64 MiB of HBM per device.

v0:
```python
import math

import jax
import jax.numpy as jnp
from jax import lax
from jax.sharding import PartitionSpec as P

D = 7168


def from_partner(block, axis, distance):
    count = lax.axis_size(axis)
    route = []
    for low in range(count):
        high = low | 1 << distance
        if high != low and high < count:
            route += [(low, high), (high, low)]
    return lax.ppermute(block, axis, route)


def gram_of(block, total_rows):
    product = jnp.dot(
        block.T, block, precision=lax.Precision.HIGHEST, preferred_element_type=jnp.float32
    )
    return product * (1.0 / total_rows)


def summed_sketch(hidden, back):
    partial_sketch = jnp.dot(hidden, back, preferred_element_type=jnp.float32)
    return lax.psum(partial_sketch, "col")


def body(hidden, test_matrix):
    tok_rows = hidden.shape[0]
    total_rows = tok_rows * lax.axis_size("row")
    out_rows = tok_rows // lax.axis_size("col")
    partial_first = jnp.dot(hidden, test_matrix, preferred_element_type=jnp.float32)
    first = (lax.psum(partial_first, "col") * (1.0 / math.sqrt(D))).astype(jnp.bfloat16)
    local_back = lax.dot_general(
        hidden, first, (((0,), (0,)), ((), ())), preferred_element_type=jnp.float32
    )
    back = (lax.psum(local_back, "row") * (1.0 / total_rows)).astype(jnp.bfloat16)
    sketch = summed_sketch(hidden, back)
    my_rows = lax.dynamic_slice_in_dim(sketch, lax.axis_index("col") * out_rows, out_rows, 0)
    lower_part = jnp.linalg.cholesky(gram_of(sketch, total_rows))
    levels = lax.axis_size("row").bit_length() - 1
    for level in range(levels):
        partner = from_partner(lower_part, "row", level)
        own_term = jnp.dot(
            lower_part,
            lower_part.T,
            precision=lax.Precision.HIGHEST,
            preferred_element_type=jnp.float32,
        )
        other_term = jnp.dot(
            partner, partner.T, precision=lax.Precision.HIGHEST, preferred_element_type=jnp.float32
        )
        lower_part = jnp.linalg.cholesky(own_term + other_term)
    basis = lax.linalg.triangular_solve(lower_part, my_rows.T, left_side=True, lower=True).T
    return (basis, lower_part.T)


def solution(mesh):
    in_specs = (P("row", "col"), P("col", None))
    out_specs = (P(("row", "col"), None), P())
    return jax.shard_map(body, mesh=mesh, in_specs=in_specs, out_specs=out_specs, check_vma=False)
```

profile of v0, /device:TPU:6, one launch (start us, length us, event | category | flops | bytes accessed | tf_op | source)
XLA Modules:
  0.0 721.2 jit_solution(17614548993673000305)
XLA Ops:
  12.2 77.1 %all-reduce.5.cloned.1.call-done = f32[1536,256]{1,0:T(8,128)} async-done(((f32[1536,256]{1,0:T(8,128)}), f32[1536,256]{1,0:T(8,128)}) %all-reduce.5.cloned.1.call-update) | async-done | bytes 1572880 | tf_op jit(solution)/shard_map/psum | solution.py:38
  92.7 161.7 %all-reduce.7.cloned.1.call-done = f32[896,256]{0,1:T(8,128)} async-done(((f32[896,256]{0,1:T(8,128)}), f32[896,256]{0,1:T(8,128)}) %all-reduce.7.cloned.1.call-update) | async-done | bytes 917520 | tf_op jit(solution)/shard_map/psum | solution.py:42
  257.8 69.0 %all-reduce.9.cloned.1.call-done = f32[1536,256]{0,1:T(8,128)} async-done(((f32[1536,256]{0,1:T(8,128)}), f32[1536,256]{0,1:T(8,128)}) %all-reduce.9.cloned.1.call-update) | async-done | bytes 1572880 | tf_op jit(solution)/shard_map/psum | solution.py:30
  330.3 11.7 %cholesky.340 = f32[128,128]{1,0:T(8,128)S(1)} custom-call(f32[128,128]{1,0:T(8,128)S(1)} %cholesky.574), custom_call_target="Cholesky" | custom-call | tf_op jit(solution)/shard_map/jit(cholesky)/cholesky | solution.py:45
  342.0 9.8 %custom-call.18 = f32[1,128,128]{1,2,0:T(8,128)S(1)} custom-call(f32[1,128,128]{2,1,0:T(8,128)S(1)} %get-tuple-element.52), custom_call_target="InvertDiagBlocksLowerTriangular" | custom-call | tf_op jit(solution)/shard_map/jit(cholesky)/cholesky | solution.py:45
  352.3 12.0 %cholesky.357 = f32[128,128]{1,0:T(8,128)S(1)} custom-call(f32[128,128]{1,0:T(8,128)S(1)} %convolution_subtract_fusion.1), custom_call_target="Cholesky" | custom-call | tf_op jit(solution)/shard_map/jit(cholesky)/cholesky | solution.py:45
  377.6 11.7 %cholesky.374 = f32[128,128]{1,0:T(8,128)S(1)} custom-call(f32[128,128]{1,0:T(8,128)S(1)} %cholesky.577), custom_call_target="Cholesky" | custom-call | tf_op jit(solution)/shard_map/jit(cholesky)/cholesky | solution.py:58
  399.6 11.7 %cholesky.391 = f32[128,128]{1,0:T(8,128)S(1)} custom-call(f32[128,128]{1,0:T(8,128)S(1)} %slice_subtract_fusion.5), custom_call_target="Cholesky" | custom-call | tf_op jit(solution)/shard_map/jit(cholesky)/cholesky | solution.py:58
  419.5 11.6 %collective-permute-done.1 = f32[256,256]{1,0:T(8,128)S(1)} collective-permute-done((f32[256,256]{1,0:T(8,128)S(1)}, f32[256,256]{1,0:T(8,128)S(1)}, u32[]{:S(2)}, u32[]{:S(2)}) %collective-permute-start.1) | collective-permute-done | bytes 262176 | tf_op jit(solution)/shard_map/ppermute | solution.py:18
  431.7 11.7 %cholesky.408 = f32[128,128]{1,0:T(8,128)S(1)} custom-call(f32[128,128]{1,0:T(8,128)S(1)} %cholesky.580), custom_call_target="Cholesky" | custom-call | tf_op jit(solution)/shard_map/jit(cholesky)/cholesky | solution.py:58
  443.5 9.8 %custom-call.20 = f32[1,128,128]{1,2,0:T(8,128)S(1)} custom-call(f32[1,128,128]{2,1,0:T(8,128)S(1)} %get-tuple-element.44), custom_call_target="InvertDiagBlocksLowerTriangular" | custom-call | tf_op jit(solution)/shard_map/jit(cholesky)/cholesky | solution.py:58
  453.8 11.7 %cholesky.425 = f32[128,128]{1,0:T(8,128)S(1)} custom-call(f32[128,128]{1,0:T(8,128)S(1)} %slice_subtract_fusion.4), custom_call_target="Cholesky" | custom-call | tf_op jit(solution)/shard_map/jit(cholesky)/cholesky | solution.py:58
  476.7 11.3 %collective-permute-done.2 = f32[256,256]{1,0:T(8,128)S(1)} collective-permute-done((f32[256,256]{1,0:T(8,128)S(1)}, f32[256,256]{1,0:T(8,128)S(1)}, u32[]{:S(2)}, u32[]{:S(2)}) %collective-permute-start.2) | collective-permute-done | bytes 262176 | tf_op jit(solution)/shard_map/ppermute | solution.py:18
  488.6 11.7 %cholesky.442 = f32[128,128]{1,0:T(8,128)S(1)} custom-call(f32[128,128]{1,0:T(8,128)S(1)} %cholesky.583), custom_call_target="Cholesky" | custom-call | tf_op jit(solution)/shard_map/jit(cholesky)/cholesky | solution.py:58
  510.7 11.7 %cholesky.459 = f32[128,128]{1,0:T(8,128)S(1)} custom-call(f32[128,128]{1,0:T(8,128)S(1)} %slice_subtract_fusion.3), custom_call_target="Cholesky" | custom-call | tf_op jit(solution)/shard_map/jit(cholesky)/cholesky | solution.py:58
  535.0 11.7 %cholesky.476 = f32[128,128]{1,0:T(8,128)S(1)} custom-call(f32[128,128]{1,0:T(8,128)S(1)} %cholesky.586), custom_call_target="Cholesky" | custom-call | tf_op jit(solution)/shard_map/jit(cholesky)/cholesky | solution.py:58
  557.1 11.7 %cholesky.493 = f32[128,128]{1,0:T(8,128)S(1)} custom-call(f32[128,128]{1,0:T(8,128)S(1)} %slice_subtract_fusion.2), custom_call_target="Cholesky" | custom-call | tf_op jit(solution)/shard_map/jit(cholesky)/cholesky | solution.py:58
  576.4 10.0 %collective-permute-done.4 = f32[256,256]{1,0:T(8,128)S(1)} collective-permute-done((f32[256,256]{1,0:T(8,128)S(1)}, f32[256,256]{1,0:T(8,128)S(1)}, u32[]{:S(2)}, u32[]{:S(2)}) %collective-permute-start.4) | collective-permute-done | bytes 262176 | tf_op jit(solution)/shard_map/ppermute | solution.py:18
  587.0 11.7 %cholesky.510 = f32[128,128]{1,0:T(8,128)S(1)} custom-call(f32[128,128]{1,0:T(8,128)S(1)} %cholesky.589), custom_call_target="Cholesky" | custom-call | tf_op jit(solution)/shard_map/jit(cholesky)/cholesky | solution.py:58
  609.1 11.7 %cholesky.527 = f32[128,128]{1,0:T(8,128)S(1)} custom-call(f32[128,128]{1,0:T(8,128)S(1)} %slice_subtract_fusion.1), custom_call_target="Cholesky" | custom-call | tf_op jit(solution)/shard_map/jit(cholesky)/cholesky | solution.py:58
  632.7 10.3 %collective-permute-done.5 = f32[256,256]{1,0:T(8,128)S(1)} collective-permute-done((f32[256,256]{1,0:T(8,128)S(1)}, f32[256,256]{1,0:T(8,128)S(1)}, u32[]{:S(2)}, u32[]{:S(2)}) %collective-permute-start.5) | collective-permute-done | bytes 262176 | tf_op jit(solution)/shard_map/ppermute | solution.py:18
  644.3 11.7 %cholesky.544 = f32[128,128]{1,0:T(8,128)S(1)} custom-call(f32[128,128]{1,0:T(8,128)S(1)} %cholesky.592), custom_call_target="Cholesky" | custom-call | tf_op jit(solution)/shard_map/jit(cholesky)/cholesky | solution.py:58
  668.1 11.7 %cholesky.561 = f32[128,128]{1,0:T(8,128)S(1)} custom-call(f32[128,128]{1,0:T(8,128)S(1)} %slice_subtract_fusion), custom_call_target="Cholesky" | custom-call | tf_op jit(solution)/shard_map/jit(cholesky)/cholesky | solution.py:58
  688.8 21.1 %custom-call.11 = f32[2,128,128]{1,2,0:T(8,128)} custom-call(f32[2,128,128]{2,1,0:T(8,128)} %get-tuple-element.10), custom_call_target="InvertDiagBlocksLowerTriangular" | custom-call | tf_op jit(solution)/shard_map/triangular_solve | solution.py:59
  (133 shorter events, 146.6 us)
Async XLA Ops:
  7.2 1.8 copy-start
  7.2 82.1 %all-reduce.5.cloned.1.call-start = ((), (), s32[]{:S(2)}) async-start(), calls=%async_computation | async-start | bytes 3145728 | tf_op jit(solution)/shard_map/psum | solution.py:38
  12.1 242.3 %all-reduce.7.cloned.1.call-start = ((), (), s32[]{:S(2)}) async-start(), calls=%async_computation.1 | async-start | bytes 1835008 | tf_op jit(solution)/shard_map/psum | solution.py:42
  92.6 234.1 %all-reduce.9.cloned.1.call-start = ((), (), s32[]{:S(2)}) async-start(), calls=%async_computation.2 | async-start | bytes 3145728 | tf_op jit(solution)/shard_map/psum | solution.py:30
  366.4 10.6 %collective-permute-start = (f32[256,256]{1,0:T(8,128)S(1)}, f32[256,256]{1,0:T(8,128)S(1)}, u32[]{:S(2)}, u32[]{:S(2)}) collective-permute-start(f32[256,256]{1,0:T(8,128)S(1)} %select_select_fusion.6), channel_id=1, source_target_pairs={{0,8},{8,0},{16,24},{24,16},{32,40},{40,32},{48,56},{56,48},{64,72... | collective-permute-start | bytes 786440 | tf_op jit(solution)/shard_map/ppermute | solution.py:18
  414.0 17.1 %collective-permute-start.1 = (f32[256,256]{1,0:T(8,128)S(1)}, f32[256,256]{1,0:T(8,128)S(1)}, u32[]{:S(2)}, u32[]{:S(2)}) collective-permute-start(f32[256,256]{1,0:T(8,128)S(1)} %select_select_fusion.5), channel_id=1, source_target_pairs={{0,16},{16,0},{8,24},{24,8},{32,48},{48,32},{40,56},{56,40},{64,80... | collective-permute-start | bytes 786440 | tf_op jit(solution)/shard_map/ppermute | solution.py:18
  468.2 19.9 %collective-permute-start.2 = (f32[256,256]{1,0:T(8,128)S(1)}, f32[256,256]{1,0:T(8,128)S(1)}, u32[]{:S(2)}, u32[]{:S(2)}) collective-permute-start(f32[256,256]{1,0:T(8,128)S(1)} %select_select_fusion.4), channel_id=1, source_target_pairs={{0,32},{32,0},{8,40},{40,8},{16,48},{48,16},{24,56},{56,24},{64,96... | collective-permute-start | bytes 786440 | tf_op jit(solution)/shard_map/ppermute | solution.py:18
  525.1 9.3 %collective-permute-start.3 = (f32[256,256]{1,0:T(8,128)S(1)}, f32[256,256]{1,0:T(8,128)S(1)}, u32[]{:S(2)}, u32[]{:S(2)}) collective-permute-start(f32[256,256]{1,0:T(8,128)S(1)} %select_select_fusion.3), channel_id=1, source_target_pairs={{0,64},{64,0},{8,72},{72,8},{16,80},{80,16},{24,88},{88,24},{32,96... | collective-permute-start | bytes 786440 | tf_op jit(solution)/shard_map/ppermute | solution.py:18
  571.5 14.9 %collective-permute-start.4 = (f32[256,256]{1,0:T(8,128)S(1)}, f32[256,256]{1,0:T(8,128)S(1)}, u32[]{:S(2)}, u32[]{:S(2)}) collective-permute-start(f32[256,256]{1,0:T(8,128)S(1)} %select_select_fusion.2), channel_id=1, source_target_pairs={{0,128},{128,0},{8,136},{136,8},{16,144},{144,16},{24,152},{152,24... | collective-permute-start | bytes 786440 | tf_op jit(solution)/shard_map/ppermute | solution.py:18
  623.5 19.5 %collective-permute-start.5 = (f32[256,256]{1,0:T(8,128)S(1)}, f32[256,256]{1,0:T(8,128)S(1)}, u32[]{:S(2)}, u32[]{:S(2)}) collective-permute-start(f32[256,256]{1,0:T(8,128)S(1)} %select_select_fusion.1), channel_id=1, source_target_pairs={{0,256},{256,0},{8,264},{264,8},{16,272},{272,16},{24,280},{280,24... | collective-permute-start | bytes 786440 | tf_op jit(solution)/shard_map/ppermute | solution.py:18
  643.6 0.7 copy-start.2
  683.2 30.2 %copy-start.1 = (f32[256,256]{0,1:T(8,128)S(1)}, f32[256,256]{0,1:T(8,128)}, u32[]{:S(2)}) copy-start(f32[256,256]{0,1:T(8,128)} %get-tuple-element.23) | copy-start | bytes 786436
Sparse Core Ops, SparseCore 0:
  12.2 76.9 all-reduce.4
  92.7 161.6 all-reduce.6
  257.9 68.7 all-reduce.8
where the time goes:
time: 732 us; the launch traced here: 721 us
  waiting for transfers between devices  363 us (50%)
  other arithmetic  265 us (36%)
  starting transfers between devices  32.8 us (4%)
  matrix products  25.9 us (4%)
  between operations  23.9 us (3%)
  local copies, waits for them, and re-layouts  10.8 us (1%)
    another operation x42, other arithmetic, body(): lower_part = jnp.linalg.cholesky(own_term + other_term)  208 us
    psum x1, waiting for transfers between devices, body(): lax.psum(local_back, 'row') * (1.0 / total_rows)  162 us
    psum x1, waiting for transfers between devices, body(): lax.psum(partial_first, 'col') * (1.0 / math.sqrt(D))  77.1 us
    psum x1, waiting for transfers between devices, summed_sketch(): return lax.psum(partial_sketch, 'col')  69 us
    ppermute x6, waiting for transfers between devices, from_partner(): return lax.ppermute(block, axis, route)  55 us
    another operation x6, other arithmetic, body(): lower_part = jnp.linalg.cholesky(gram_of(sketch, total_rows))  34.3 us
    ppermute x6, starting transfers between devices, from_partner(): return lax.ppermute(block, axis, route)  32.6 us
    another operation x2, other arithmetic, body(): lax.linalg.triangular_solve(lower_part, my_rows.T, left_side=True, lower=...  21.1 us
  transfers between devices with their start and end apart: 9, of which 9 were waited for; matrix products, arithmetic and copies ran while one was open for 1% of the time, Pallas kernels for 0%

commit v1 on v0

v1 whole, which is shorter than its diff:
```python
import math

import jax
import jax.numpy as jnp
from jax import lax
from jax.experimental import pallas as pl
from jax.experimental.pallas import tpu as pltpu
from jax.sharding import Mesh, PartitionSpec as P

D = 7168
K = 256
HIGH = lax.Precision.HIGHEST

def mm(a, b):
    return jnp.dot(a, b, precision=HIGH, preferred_element_type=jnp.float32)

def mtm(a, b):
    return lax.dot_general(a, b, (((0,), (0,)), ((), ())), precision=HIGH, preferred_element_type=jnp.float32)

def low(a, b):
    return jnp.dot(a.astype(jnp.bfloat16), b.astype(jnp.bfloat16), preferred_element_type=jnp.float32)

def low_tm(a, b):
    return lax.dot_general(a.astype(jnp.bfloat16), b.astype(jnp.bfloat16), (((0,), (0,)), ((), ())), preferred_element_type=jnp.float32)


def factor_kernel(gram_ref, rows_ref, basis_ref, factor_ref, g_ref, x_ref, work_ref):
    row = lax.broadcasted_iota(jnp.int32, (K, K), 0)
    col = lax.broadcasted_iota(jnp.int32, (K, K), 1)
    eye = (row == col).astype(jnp.float32)
    upper = jnp.where(row < col, 1.0, jnp.where(row == col, 0.5, 0.0))
    gram = gram_ref[...]
    on_diag = jnp.where(row == col, gram, 0.0)
    s_row = lax.rsqrt(jnp.sum(on_diag, axis=0, keepdims=True))
    s_col = lax.rsqrt(jnp.sum(on_diag, axis=1, keepdims=True))
    g_ref[...] = gram * s_row * s_col
    x_ref[...] = eye * s_row

    def size(e):
        return jnp.sum(e * e)

    def step(state):
        count, _ = state
        g = g_ref[...]
        f = (g - eye) * upper
        a = f - low_tm(f, f) * upper
        t = eye - a + low(a, a)
        new = mtm(t, mm(g, t))
        g_ref[...] = new
        x_ref[...] = mm(x_ref[...], t)
        return count + 1, size(new - eye)

    def more(state):
        count, err = state
        return jnp.logical_and(count < 12, err > 1e-5)

    _, err = lax.while_loop(more, step, (jnp.int32(0), size(g_ref[...] - eye)))
    ok = err <= 1e-5

    @pl.when(ok)
    def _():
        x_ref[...] = mm(x_ref[...], eye - (g_ref[...] - eye) * upper)

    @pl.when(jnp.logical_not(ok))
    def _():
        work_ref[:, :K] = gram
        work_ref[:, K:] = eye
        lane = lax.broadcasted_iota(jnp.int32, (1, 2 * K), 1)

        def eliminate(k, carry):
            line = work_ref[pl.ds(k, 1), :]
            pivot = jnp.sum(jnp.where(lane == k, line, 0.0), axis=1, keepdims=True)
            line = line * lax.rsqrt(pivot)
            coef = jnp.where(lane[:, :K] > k, line[:, :K], 0.0)
            outer = lax.dot_general(coef, line, (((0,), (0,)), ((), ())), precision=HIGH, preferred_element_type=jnp.float32)
            work_ref[...] = work_ref[...] - outer
            work_ref[pl.ds(k, 1), :] = line
            return carry

        lax.fori_loop(0, K, eliminate, 0)
        x_ref[...] = work_ref[:, K:].T

    x = jnp.where(row <= col, x_ref[...], 0.0)
    factor_ref[...] = jnp.where(row <= col, mtm(x, gram), 0.0)
    basis_ref[...] = mm(rows_ref[...], x)


def factor_call(gram, rows):
    n = rows.shape[0]
    return pl.pallas_call(
        factor_kernel,
        out_shape=(jax.ShapeDtypeStruct((n, K), jnp.float32), jax.ShapeDtypeStruct((K, K), jnp.float32)),
        in_specs=[pl.BlockSpec(memory_space=pltpu.VMEM)] * 2,
        out_specs=(pl.BlockSpec(memory_space=pltpu.VMEM),) * 2,
        scratch_shapes=[pltpu.VMEM((K, K), jnp.float32), pltpu.VMEM((K, K), jnp.float32), pltpu.VMEM((K, 2 * K), jnp.float32)],
        compiler_params=pltpu.CompilerParams(vmem_limit_bytes=32 * 1024 * 1024),
    )(gram, rows)


ROW = ("y", "z")
COL = ("x", "core")


def scattered_sum(block, axis, dtype):
    count = lax.axis_size(axis)
    pieces = block.astype(dtype).reshape(count, block.shape[0] // count, K)
    return jnp.sum(lax.all_to_all(pieces, axis, 0, 0).astype(jnp.float32), axis=0)


def gathered(block, axis):
    count = lax.axis_size(axis)
    return lax.all_to_all(jnp.broadcast_to(block[None], (count, *block.shape)), axis, 0, 0)


def gathered_sum(block, axis, dtype):
    return jnp.sum(gathered(block.astype(dtype), axis).astype(jnp.float32), axis=0)


def body(hidden, test_matrix):
    tok_rows, width = hidden.shape
    total_rows = tok_rows * lax.axis_size(ROW)
    partial_first = jnp.dot(hidden, test_matrix, preferred_element_type=jnp.float32)
    my_first = (scattered_sum(partial_first, COL, jnp.bfloat16) * (1.0 / math.sqrt(D))).astype(jnp.bfloat16)
    first = gathered(my_first, COL).reshape(tok_rows, K)
    local_back = lax.dot_general(
        hidden, first, (((0,), (0,)), ((), ())), preferred_element_type=jnp.float32
    )
    my_back = scattered_sum(local_back, "z", jnp.bfloat16)
    my_back = (gathered_sum(my_back, "y", jnp.bfloat16) * (1.0 / total_rows)).astype(jnp.bfloat16)
    back = gathered(my_back, "z").reshape(width, K)
    partial_sketch = jnp.dot(hidden, back, preferred_element_type=jnp.float32)
    my_rows = scattered_sum(partial_sketch, COL, jnp.bfloat16)
    my_gram = jnp.dot(
        my_rows.T, my_rows, precision=lax.Precision.HIGHEST, preferred_element_type=jnp.float32
    )
    my_gram = scattered_sum(my_gram * (1.0 / total_rows), COL, jnp.float32)
    my_gram = gathered_sum(my_gram, "z", jnp.float32)
    my_gram = gathered_sum(my_gram, "y", jnp.float32)
    gram = gathered(my_gram, COL).reshape(K, K)
    return factor_call(gram, my_rows)


def solution(mesh):
    rows, cols = mesh.devices.shape
    side = math.isqrt(rows)
    grid = Mesh(mesh.devices.reshape(side, rows // side, cols // 2, 2), (*ROW, *COL))
    in_specs = (P(ROW, COL), P(COL, None))
    out_specs = (P((*ROW, *COL), None), P())
    return jax.shard_map(body, mesh=grid, in_specs=in_specs, out_specs=out_specs, check_vma=False)
```

time: 732 us -> 359 us (0.49); the launches traced: 721 us -> 356 us
  waiting for transfers between devices: 363 us -> 0 us
  other arithmetic: 265 us -> 0.42 us
  Pallas kernels: 0 us -> 186 us
  blocking collectives: 0 us -> 159 us
  starting transfers between devices: 32.8 us -> 0 us
  between operations: 23.9 us -> 0.75 us
  matrix products: 25.9 us -> 5.6 us
    psum x3 -> x0, waiting for transfers between devices: 308 us -> none  [the longest x1 162 us: body(): lax.psum(local_back, 'row') * (1.0 / total_rows)]
    another operation x50 -> x0, other arithmetic: 263 us -> none  [the longest x42 208 us: body(): lower_part = jnp.linalg.cholesky(own_term + other_term)]
    pallas_call x0 -> x1, Pallas kernels: none -> 186 us  [factor_call(): pl.pallas_call(factor_kernel, out_shape=(jax.ShapeDtypeStruct((n, K), jnp...]
    all_to_all x0 -> x10, blocking collectives: none -> 159 us  [the longest x6 91.3 us: gathered(): lax.all_to_all(jnp.broadcast_to(block[None], (count, *block.shape)), axis...]
    ppermute x6 -> x0, waiting for transfers between devices: 55 us -> none  [from_partner(): return lax.ppermute(block, axis, route)]
    ppermute x6 -> x0, starting transfers between devices: 32.6 us -> none  [from_partner(): return lax.ppermute(block, axis, route)]
    dot_general x14 -> x2, matrix products: 11.6 us -> 2.6 us  [the longest x1 1.94 us: body(): partial_sketch = jnp.dot(hidden, back, preferred_element_type=jnp.float32)]
    another operation x17 -> x0, matrix products: 7.76 us -> none  [the longest x12 4.52 us: body(): lower_part = jnp.linalg.cholesky(own_term + other_term)]
  transfers between devices with their start and end apart: 9 -> 0, of which waited for: 9 -> 0; matrix products, arithmetic and copies ran while one was open for 1% -> 0% of each run, Pallas kernels for 0% -> 0%
where the time goes in v1:
time: 359 us; the launch traced here: 356 us
  Pallas kernels  186 us (52%)
  blocking collectives  159 us (44%)
  matrix products  5.6 us (2%)
  local copies, waits for them, and re-layouts  4.34 us (1%)
    pallas_call x1, Pallas kernels, factor_call(): pl.pallas_call(factor_kernel, out_shape=(jax.ShapeDtypeStruct((n, K), jnp...  186 us
    all_to_all x6, blocking collectives, gathered(): lax.all_to_all(jnp.broadcast_to(block[None], (count, *block.shape)), axis...  91.3 us
    all_to_all x4, blocking collectives, scattered_sum(): lax.all_to_all(pieces, axis, 0, 0).astype(jnp.float32)  67.4 us

profile of v1, /device:TPU:6, one launch (start us, length us, event | category | flops | bytes accessed | tf_op | source)
XLA Modules:
  0.0 356.1 jit_solution(11379034581262992603)
XLA Ops:
  0.6 0.0 copy-start
  0.6 1.8 copy-done
  2.4 2.0 convolution_convert_fusion.1
  4.4 19.4 %all_to_all.50 = bf16[8,192,256]{2,1,0:T(8,128)(2,1)S(1)} all-to-all(bf16[8,192,256]{2,1,0:T(8,128)(2,1)S(1)} %bitcast.24), channel_id=1, replica_groups=mesh['y'=8,'z'=8,'x'=4,'core'=2] {'x','core'}, dimensions={0} | all-to-all | bytes 1572864 | tf_op jit(solution)/shard_map/all_to_all | solution.py:107
  23.8 0.1 convert_reduce_fusion.1
  24.0 0.1 broadcast_in_dim.12
  24.0 15.7 %all_to_all.51 = bf16[8,192,256]{2,1,0:T(8,128)(2,1)S(1)} all-to-all(bf16[8,192,256]{2,1,0:T(8,128)(2,1)S(1)} %broadcast_in_dim.12), channel_id=1, replica_groups=mesh['y'=8,'z'=8,'x'=4,'core'=2] {'x','core'}, dimensions={0} | all-to-all | bytes 1572864 | tf_op jit(solution)/shard_map/all_to_all | solution.py:112
  39.7 1.0 fusion.1
  40.7 1.0 copy.6
  41.7 22.4 %all_to_all.52 = bf16[8,112,256]{2,1,0:T(8,128)(2,1)S(1)} all-to-all(bf16[8,112,256]{2,1,0:T(8,128)(2,1)} %bitcast.21), channel_id=1, replica_groups=mesh['y'=8,'z'=8,'x'=4,'core'=2] {'z'}, dimensions={0} | all-to-all | bytes 917504 | tf_op jit(solution)/shard_map/all_to_all | solution.py:107
  64.0 0.1 reduce_sum.67
  64.2 20.8 %all_to_all.53 = bf16[8,112,256]{2,1,0:T(8,128)(2,1)S(1)} all-to-all(bf16[8,112,256]{2,1,0:T(8,128)(2,1)S(1)} %broadcast_in_dim.13), channel_id=1, replica_groups=mesh['y'=8,'z'=8,'x'=4,'core'=2] {'y'}, dimensions={0} | all-to-all | bytes 917504 | tf_op jit(solution)/shard_map/all_to_all | solution.py:112
  85.0 0.1 convert_reduce_fusion.2
  85.1 16.9 %all_to_all.54 = bf16[8,112,256]{2,1,0:T(8,128)(2,1)S(1)} all-to-all(bf16[8,112,256]{2,1,0:T(8,128)(2,1)S(1)} %broadcast_in_dim.14), channel_id=1, replica_groups=mesh['y'=8,'z'=8,'x'=4,'core'=2] {'z'}, dimensions={0} | all-to-all | bytes 917504 | tf_op jit(solution)/shard_map/all_to_all | solution.py:112
  102.0 1.9 fusion
  103.9 1.4 copy.7
  105.4 15.7 %all_to_all.55 = bf16[8,192,256]{2,1,0:T(8,128)(2,1)S(1)} all-to-all(bf16[8,192,256]{2,1,0:T(8,128)(2,1)S(1)} %bitcast.20), channel_id=1, replica_groups=mesh['y'=8,'z'=8,'x'=4,'core'=2] {'x','core'}, dimensions={0} | all-to-all | bytes 1572864 | tf_op jit(solution)/shard_map/all_to_all | solution.py:107
  121.0 0.1 convert_reduce_fusion.rows_ref
  121.1 0.7 convolution_multiply_fusion
  121.8 9.9 %all_to_all.56 = f32[8,32,256]{2,1,0:T(8,128)S(1)} all-to-all(f32[8,32,256]{2,1,0:T(8,128)S(1)} %bitcast.22), channel_id=1, replica_groups=mesh['y'=8,'z'=8,'x'=4,'core'=2] {'x','core'}, dimensions={0} | all-to-all | bytes 524288 | tf_op jit(solution)/shard_map/all_to_all | solution.py:107
  131.8 14.2 %all_to_all.57 = f32[8,32,256]{2,1,0:T(8,128)S(1)} all-to-all(f32[8,32,256]{2,1,0:T(8,128)S(1)} %broadcast_in_dim.15), channel_id=1, replica_groups=mesh['y'=8,'z'=8,'x'=4,'core'=2] {'z'}, dimensions={0} | all-to-all | bytes 524288 | tf_op jit(solution)/shard_map/all_to_all | solution.py:112
  146.0 13.4 %all_to_all.58 = f32[8,32,256]{2,1,0:T(8,128)S(1)} all-to-all(f32[8,32,256]{2,1,0:T(8,128)S(1)} %broadcast_in_dim.16), channel_id=1, replica_groups=mesh['y'=8,'z'=8,'x'=4,'core'=2] {'y'}, dimensions={0} | all-to-all | bytes 524288 | tf_op jit(solution)/shard_map/all_to_all | solution.py:112
  159.5 10.3 %all_to_all.59 = f32[8,32,256]{2,1,0:T(8,128)S(1)} all-to-all(f32[8,32,256]{2,1,0:T(8,128)S(1)} %broadcast_in_dim.17), channel_id=1, replica_groups=mesh['y'=8,'z'=8,'x'=4,'core'=2] {'x','core'}, dimensions={0} | all-to-all | bytes 524288 | tf_op jit(solution)/shard_map/all_to_all | solution.py:112
  169.7 186.3 %shard_map.41 = (f32[192,256]{1,0:T(8,128)}, f32[256,256]{1,0:T(8,128)}) custom-call(f32[256,256]{1,0:T(8,128)S(1)} %bitcast.19, f32[192,256]{1,0:T(8,128)S(1)} %convert_reduce_fusion.rows_ref), custom_call_target="tpu_custom_call" | custom-call | tf_op jit(solution)/shard_map/pallas_call | solution.py:90
  (10 shorter events, 0.2 us)
Async XLA Ops:
  0.6 1.8 copy-start

commit v2 on v1

v2 whole, which is shorter than its diff:
```python
import math

import jax
import jax.numpy as jnp
from jax import lax
from jax.experimental import pallas as pl
from jax.experimental.pallas import tpu as pltpu
from jax.sharding import Mesh, PartitionSpec as P

D = 7168
K = 256
HALF = K // 2
HIGH = lax.Precision.HIGHEST

def mm(a, b):
    return jnp.dot(a, b, precision=HIGH, preferred_element_type=jnp.float32)

def mtm(a, b):
    return lax.dot_general(a, b, (((0,), (0,)), ((), ())), precision=HIGH, preferred_element_type=jnp.float32)

def low(a, b):
    return jnp.dot(a.astype(jnp.bfloat16), b.astype(jnp.bfloat16), preferred_element_type=jnp.float32)

def low_tm(a, b):
    return lax.dot_general(a.astype(jnp.bfloat16), b.astype(jnp.bfloat16), (((0,), (0,)), ((), ())), preferred_element_type=jnp.float32)


def factor_kernel(packed_ref, rows_ref, basis_ref, factor_ref, gram_ref, g_ref, x_ref, work_ref):
    corner = packed_ref[HALF : 2 * HALF, :]
    gram_ref[:HALF, :HALF] = packed_ref[:HALF, :]
    gram_ref[:HALF, HALF:] = corner
    gram_ref[HALF:, :HALF] = corner.T
    gram_ref[HALF:, HALF:] = packed_ref[2 * HALF :, :]
    row = lax.broadcasted_iota(jnp.int32, (K, K), 0)
    col = lax.broadcasted_iota(jnp.int32, (K, K), 1)
    eye = (row == col).astype(jnp.float32)
    upper = jnp.where(row < col, 1.0, jnp.where(row == col, 0.5, 0.0))
    gram = gram_ref[...]
    on_diag = jnp.where(row == col, gram, 0.0)
    s_row = lax.rsqrt(jnp.sum(on_diag, axis=0, keepdims=True))
    s_col = lax.rsqrt(jnp.sum(on_diag, axis=1, keepdims=True))
    g_ref[...] = gram * s_row * s_col
    x_ref[...] = eye * s_row

    def size(e):
        return jnp.sum(e * e)

    def step(state):
        count, _ = state
        g = g_ref[...]
        f = (g - eye) * upper
        a = f - low_tm(f, f) * upper
        t = eye - a + low(a, a)
        new = mtm(t, mm(g, t))
        g_ref[...] = new
        x_ref[...] = mm(x_ref[...], t)
        return count + 1, size(new - eye)

    def more(state):
        count, err = state
        return jnp.logical_and(count < 12, err > 1e-5)

    _, err = lax.while_loop(more, step, (jnp.int32(0), size(g_ref[...] - eye)))
    ok = err <= 1e-5

    @pl.when(ok)
    def _():
        x_ref[...] = mm(x_ref[...], eye - (g_ref[...] - eye) * upper)

    @pl.when(jnp.logical_not(ok))
    def _():
        work_ref[:, :K] = gram
        work_ref[:, K:] = eye
        lane = lax.broadcasted_iota(jnp.int32, (1, 2 * K), 1)

        def eliminate(k, carry):
            line = work_ref[pl.ds(k, 1), :]
            pivot = jnp.sum(jnp.where(lane == k, line, 0.0), axis=1, keepdims=True)
            line = line * lax.rsqrt(pivot)
            coef = jnp.where(lane[:, :K] > k, line[:, :K], 0.0)
            outer = lax.dot_general(coef, line, (((0,), (0,)), ((), ())), precision=HIGH, preferred_element_type=jnp.float32)
            work_ref[...] = work_ref[...] - outer
            work_ref[pl.ds(k, 1), :] = line
            return carry

        lax.fori_loop(0, K, eliminate, 0)
        x_ref[...] = work_ref[:, K:].T

    x = jnp.where(row <= col, x_ref[...], 0.0)
    factor_ref[...] = jnp.where(row <= col, mtm(x, gram), 0.0)
    basis_ref[...] = mm(rows_ref[...], x)


def factor_call(packed, rows):
    square = pltpu.VMEM((K, K), jnp.float32)
    return pl.pallas_call(
        factor_kernel,
        out_shape=(jax.ShapeDtypeStruct(rows.shape, jnp.float32), jax.ShapeDtypeStruct((K, K), jnp.float32)),
        in_specs=[WHOLE] * 2,
        out_specs=(WHOLE, WHOLE),
        scratch_shapes=[square, square, square, pltpu.VMEM((K, 2 * K), jnp.float32)],
        compiler_params=PARAMS,
        name="factor",
    )(packed, rows)


WHOLE = pl.BlockSpec(memory_space=pltpu.VMEM)
PARAMS = pltpu.CompilerParams(vmem_limit_bytes=32 * 1024 * 1024)


def rows_kernel(over_rows, which_ref, left_ref, right_ref, out_ref):
    dims = (((1,), (0 if over_rows else 1,)), ((), ()))
    out_ref[...] = lax.dot_general(left_ref[...], right_ref[...], dims, preferred_element_type=jnp.float32)


def half_product(hidden, right, half, over_rows):
    rows, width = hidden.shape
    tile = rows // 8
    spec = pltpu.PrefetchScalarGridSpec(
        num_scalar_prefetch=1,
        grid=(4,),
        in_specs=[
            pl.BlockSpec((tile, width), lambda i, which: (2 * i + which[0], 0)),
            pl.BlockSpec(right.shape, lambda i, which: (0, 0)),
        ],
        out_specs=pl.BlockSpec((tile, K), lambda i, which: (i, 0)),
    )
    return pl.pallas_call(
        lambda *refs: rows_kernel(over_rows, *refs),
        out_shape=jax.ShapeDtypeStruct((rows // 2, K), jnp.float32),
        grid_spec=spec,
        compiler_params=PARAMS,
        name="half_product",
    )(half, hidden, right)


def back_kernel(which_ref, first_ref, hidden_ref, out_ref):
    part = lax.dot_general(first_ref[...], hidden_ref[...], (((0,), (0,)), ((), ())), preferred_element_type=jnp.float32)

    @pl.when(pl.program_id(0) == 0)
    def _():
        out_ref[...] = part

    @pl.when(pl.program_id(0) > 0)
    def _():
        out_ref[...] = out_ref[...] + part


def half_back(hidden, first, half):
    rows, width = hidden.shape
    tile = rows // 8
    spec = pltpu.PrefetchScalarGridSpec(
        num_scalar_prefetch=1,
        grid=(4,),
        in_specs=[
            pl.BlockSpec((tile, K), lambda i, which: (i, 0)),
            pl.BlockSpec((tile, width), lambda i, which: (2 * i + which[0], 0)),
        ],
        out_specs=pl.BlockSpec((K, width), lambda i, which: (0, 0)),
    )
    return pl.pallas_call(
        back_kernel,
        out_shape=jax.ShapeDtypeStruct((K, width), jnp.float32),
        grid_spec=spec,
        compiler_params=PARAMS,
        name="half_back",
    )(half, first, hidden)


def gram_kernel(rows_ref, packed_ref):
    left, right = rows_ref[:, :HALF], rows_ref[:, HALF:]
    packed_ref[:HALF, :] = mtm(left, left)
    packed_ref[HALF : 2 * HALF, :] = mtm(left, right)
    packed_ref[2 * HALF :, :] = mtm(right, right)


def packed_gram(rows):
    return pl.pallas_call(
        gram_kernel,
        out_shape=jax.ShapeDtypeStruct((3 * HALF, HALF), jnp.float32),
        in_specs=[WHOLE],
        out_specs=WHOLE,
        compiler_params=PARAMS,
        name="packed_gram",
    )(rows)


ROW = ("y", "z")
COL = ("x", "core")
ALL = (*ROW, *COL)


def swapped(block):
    return lax.ppermute(block, "core", [(0, 1), (1, 0)])


def line_groups(sizes, along):
    ys, zs, xs = sizes
    groups = []
    for core in range(2):
        y_steps, z_steps = along[core]
        for y in range(ys):
            for z in range(zs):
                if any(y // s % n for s, n in y_steps) or any(z // s % n for s, n in z_steps):
                    continue
                spots = [(y, z)]
                for s, n in y_steps:
                    spots = [(a + s * k, b) for a, b in spots for k in range(n)]
                for s, n in z_steps:
                    spots = [(a, b + s * k) for a, b in spots for k in range(n)]
                for x in range(xs):
                    groups.append([((a * zs + b) * xs + x) * 2 + core for a, b in spots])
    return groups


def exchanged(pieces, axis, groups=None):
    return lax.all_to_all(pieces, axis, 0, 0, axis_index_groups=groups)


def spread(block, count):
    return jnp.broadcast_to(block[None], (count, *block.shape))


def total(pieces):
    return jnp.sum(pieces.astype(jnp.float32), axis=0)


def body(sizes, hidden, test_matrix):
    bf16 = jnp.bfloat16
    tok_rows, width = hidden.shape
    tile = tok_rows // 8
    ys, zs, xs = sizes
    total_rows = tok_rows * ys * zs
    core = lax.axis_index("core")
    mine, other = core.reshape(1), (1 - core).reshape(1)

    landed = swapped(half_product(hidden, test_matrix, other, True))
    pieces = (half_product(hidden, test_matrix, mine, True) + landed).astype(bf16).reshape(xs, tile, K)
    my_first = (total(exchanged(pieces, "x")) * (1.0 / math.sqrt(D))).astype(bf16)
    my_half = exchanged(spread(my_first, xs), "x").reshape(tok_rows // 2, K)
    other_half = swapped(my_half)
    local_back = half_back(hidden, my_half, mine) + half_back(hidden, other_half, other)

    wide = line_groups(sizes, ((((1, 2),), ((1, zs),)), (((1, ys),), ((1, 2),))))
    rest = line_groups(sizes, ((((2, ys // 2),), ()), ((), ((2, zs // 2),))))
    n_wide, n_rest = len(wide[0]), len(rest[0])
    pieces = local_back.astype(bf16).reshape(n_wide, K // n_wide, width)
    my_back = total(exchanged(pieces, ALL, wide))
    my_back = total(exchanged(spread(my_back, n_rest), ALL, rest))
    my_back = (my_back * (1.0 / total_rows)).astype(bf16)
    back = exchanged(spread(my_back, n_wide), ALL, wide).reshape(K, width)

    landed = swapped(half_product(hidden, back, other, False))
    own = half_product(hidden, back, mine, False) + landed
    pieces = own.reshape(xs, tile, K)
    landed = exchanged(pieces.astype(bf16), "x").astype(jnp.float32)
    mine_of_x = lax.broadcasted_iota(jnp.int32, (xs, 1, 1), 0) == lax.axis_index("x")
    my_rows = jnp.sum(jnp.where(mine_of_x, pieces, landed), axis=0)

    gram = packed_gram(my_rows) * (1.0 / total_rows)
    gram = total(exchanged(gram.reshape(8, 3 * HALF // 8, HALF), COL))
    lines = [((), ((1, zs),)), (((1, ys),), ())]
    for along in (lines, lines[::-1]):
        groups = line_groups(sizes, along)
        gram = total(exchanged(spread(gram, len(groups[0])), ALL, groups))
    gram = exchanged(spread(gram, 8), COL).reshape(3 * HALF, HALF)
    return factor_call(gram, my_rows)


def solution(mesh):
    rows, cols = mesh.devices.shape
    side = math.isqrt(rows)
    sizes = (side, rows // side, cols // 2)
    grid = Mesh(mesh.devices.reshape(*sizes, 2), ALL)
    in_specs = (P(ROW, COL), P(COL, None))
    out_specs = (P(ALL, None), P())
    return jax.shard_map(
        lambda *args: body(sizes, *args), mesh=grid, in_specs=in_specs, out_specs=out_specs, check_vma=False
    )
```

time: 359 us -> 345 us (0.961)
  blocking collectives: 159 us -> 122 us
  starting transfers between devices: 0 us -> 11.2 us
  Pallas kernels: 186 us -> 195 us
  waiting for transfers between devices: 0 us -> 8.61 us
  matrix products: 5.6 us -> 0 us
    all_to_all x10 -> x9, blocking collectives: 159 us -> 122 us  [exchanged(): return lax.all_to_all(pieces, axis, 0, 0, axis_index_groups=groups)]
    pallas_call x1 -> x8, Pallas kernels: 186 us -> 195 us  [the longest x1 186 us: factor_call(): pl.pallas_call(factor_kernel, out_shape=(jax.ShapeDtypeStruct(rows.shape,...]
    all_to_all x0 -> x1, waiting for transfers between devices: none -> 6.58 us  [exchanged(): return lax.all_to_all(pieces, axis, 0, 0, axis_index_groups=groups)]
    ppermute x0 -> x3, starting transfers between devices: none -> 5.75 us  [swapped(): return lax.ppermute(block, 'core', [(0, 1), (1, 0)])]
    dot_general x4 -> x0, matrix products: 5.6 us -> none  [the longest x1 1.99 us: body(): jnp.dot(hidden, test_matrix, preferred_element_type=jnp.float32)]
    all_to_all x0 -> x1, starting transfers between devices: none -> 5.5 us  [exchanged(): return lax.all_to_all(pieces, axis, 0, 0, axis_index_groups=groups)]
  transfers between devices with their start and end apart: 0 -> 4, of which waited for: 0 -> 3; matrix products, arithmetic and copies ran while one was open for 0% -> 0% of each run, Pallas kernels for 0% -> 1%
where the time goes in v2:
time: 345 us; the launch traced here: 342 us
  Pallas kernels  195 us (57%)
  blocking collectives  122 us (35%)
  starting transfers between devices  11.2 us (3%)
  waiting for transfers between devices  8.61 us (2%)
    pallas_call x1, Pallas kernels, factor_call(): pl.pallas_call(factor_kernel, out_shape=(jax.ShapeDtypeStruct(rows.shape,...  186 us
    all_to_all x9, blocking collectives, exchanged(): return lax.all_to_all(pieces, axis, 0, 0, axis_index_groups=groups)  122 us
  transfers between devices with their start and end apart: 4, of which 3 were waited for; matrix products, arithmetic and copies ran while one was open for 0% of the time, Pallas kernels for 1%

profile of v2, /device:TPU:6, one launch (start us, length us, event | category | flops | bytes accessed | tf_op | source)
XLA Modules:
  0.0 342.2 jit_solution(13724081918798178042)
XLA Ops:
  0.6 1.8 copy-done
  2.4 1.0 copy-done.2
  3.4 1.1 half_product.5
  4.5 1.9 collective-permute-start
  6.5 1.1 half_product.4
  7.6 1.1 collective-permute-done
  8.9 14.8 %all_to_all.50 = bf16[4,192,256]{2,1,0:T(8,128)(2,1)S(1)} all-to-all(bf16[4,192,256]{2,1,0:T(8,128)(2,1)S(1)} %bitcast.17), channel_id=1, replica_groups=mesh['y'=8,'z'=8,'x'=4,'core'=2] {'x'}, dimensions={0} | all-to-all | bytes 786432 | tf_op jit(solution)/shard_map/all_to_all | solution.py:217
  23.8 10.2 %all_to_all.51 = bf16[4,192,256]{2,1,0:T(8,128)(2,1)S(1)} all-to-all(bf16[4,192,256]{2,1,0:T(8,128)(2,1)S(1)} %broadcast_in_dim.21), channel_id=1, replica_groups=mesh['y'=8,'z'=8,'x'=4,'core'=2] {'x'}, dimensions={0} | all-to-all | bytes 786432 | tf_op jit(solution)/shard_map/all_to_all | solution.py:217
  34.0 1.9 collective-permute-start.1
  35.9 1.7 half_back.2
  37.6 1.7 half_back.3
  39.4 18.9 %all_to_all.52 = bf16[16,16,896]{2,1,0:T(8,128)(2,1)S(1)} all-to-all(bf16[16,16,896]{2,1,0:T(8,128)(2,1)S(1)} %bitcast.16), channel_id=1, replica_groups={{0,8,16,24,32,40,48,56,64,72,80,88,96,104,112,120},{2,10,18,26,34,42,50..., dimensions={0} | all-to-all | bytes 917504 | tf_op jit(solution)/shard_map/all_to_all | solution.py:217
  58.5 16.9 %all_to_all.53 = f32[4,16,896]{2,1,0:T(8,128)S(1)} all-to-all(f32[4,16,896]{2,1,0:T(8,128)S(1)} %broadcast_in_dim.22), channel_id=1, replica_groups={{0,128,256,384},{2,130,258,386},{4,132,260,388},{6,134,262,390},{8,136,..., dimensions={0} | all-to-all | bytes 458752 | tf_op jit(solution)/shard_map/all_to_all | solution.py:217
  75.4 15.3 %all_to_all.54 = bf16[16,16,896]{2,1,0:T(8,128)(2,1)S(1)} all-to-all(bf16[16,16,896]{2,1,0:T(8,128)(2,1)S(1)} %broadcast_in_dim.23), channel_id=1, replica_groups={{0,8,16,24,32,40,48,56,64,72,80,88,96,104,112,120},{2,10,18,26,34,42,50..., dimensions={0} | all-to-all | bytes 917504 | tf_op jit(solution)/shard_map/all_to_all | solution.py:217
  90.7 1.3 half_product.7
  92.0 1.9 collective-permute-start.2
  93.9 1.3 half_product.6
  97.1 5.5 %all-to-all-start.5 = ((bf16[4,192,256]{2,1,0:T(8,128)(2,1)}), bf16[4,192,256]{2,1,0:T(8,128)(2,1)S(1)}, u32[]{:S(2)}, u32[]{:S(2)}) async-start(bf16[4,192,256]{2,1,0:T(8,128)(2,1)} %convert_element_type.38), calls=%async_computation.5 | async-start | bytes 786432 | tf_op jit(solution)/shard_map/all_to_all | solution.py:217
  102.6 6.6 %all-to-all-done.5 = bf16[4,192,256]{2,1,0:T(8,128)(2,1)S(1)} async-done(((bf16[4,192,256]{2,1,0:T(8,128)(2,1)}), bf16[4,192,256]{2,1,0:T(8,128)(2,1)S(1)}, u32[]{:S(2)}, u32[]{:S(2)}) %all-to-all-start.5) | async-done | bytes 393248 | tf_op jit(solution)/shard_map/all_to_all | solution.py:217
  109.8 9.2 %all_to_all.55 = f32[8,48,128]{2,1,0:T(8,128)S(1)} all-to-all(f32[8,48,128]{2,1,0:T(8,128)S(1)} %bitcast.18), channel_id=1, replica_groups=mesh['y'=8,'z'=8,'x'=4,'core'=2] {'x','core'}, dimensions={0} | all-to-all | bytes 393216 | tf_op jit(solution)/shard_map/all_to_all | solution.py:217
  119.1 14.2 %all_to_all.56 = f32[8,48,128]{2,1,0:T(8,128)S(1)} all-to-all(f32[8,48,128]{2,1,0:T(8,128)S(1)} %broadcast_in_dim.24), channel_id=1, replica_groups={{0,8,16,24,32,40,48,56},{2,10,18,26,34,42,50,58},{4,12,20,28,36,44,52,6..., dimensions={0} | all-to-all | bytes 393216 | tf_op jit(solution)/shard_map/all_to_all | solution.py:217
  133.3 13.3 %all_to_all.57 = f32[8,48,128]{2,1,0:T(8,128)S(1)} all-to-all(f32[8,48,128]{2,1,0:T(8,128)S(1)} %broadcast_in_dim.25), channel_id=1, replica_groups={{0,64,128,192,256,320,384,448},{2,66,130,194,258,322,386,450},{4,68,132..., dimensions={0} | all-to-all | bytes 393216 | tf_op jit(solution)/shard_map/all_to_all | solution.py:217
  146.6 9.2 %all_to_all.58 = f32[8,48,128]{2,1,0:T(8,128)S(1)} all-to-all(f32[8,48,128]{2,1,0:T(8,128)S(1)} %broadcast_in_dim.26), channel_id=1, replica_groups=mesh['y'=8,'z'=8,'x'=4,'core'=2] {'x','core'}, dimensions={0} | all-to-all | bytes 393216 | tf_op jit(solution)/shard_map/all_to_all | solution.py:217
  155.9 186.3 %factor.1 = (f32[192,256]{1,0:T(8,128)}, f32[256,256]{1,0:T(8,128)}) custom-call(f32[384,128]{1,0:T(8,128)S(1)} %bitcast.13, f32[192,256]{1,0:T(8,128)S(1)} %select_reduce_fusion.rows_ref), custom_call_target="tpu_custom_call" | custom-call | tf_op jit(solution)/shard_map/factor/pallas_call | solution.py:96
  (28 shorter events, 3.0 us)
Async XLA Ops:
  0.6 1.8 copy-start
  2.4 1.0 copy-start.2
  3.4 3.0 copy-start.1
  4.5 4.2 %collective-permute-start = (f32[768,256]{1,0:T(8,128)S(1)}, f32[768,256]{1,0:T(8,128)S(1)}, u32[]{:S(2)}, u32[]{:S(2)}) collective-permute-start(f32[768,256]{1,0:T(8,128)S(1)} %half_product.5), channel_id=1, source_target_pairs={{0,1},{1,0},{2,3},{3,2},{4,5},{5,4},{6,7},{7,6},{8,9},{9,8},{10,11... | collective-permute-start | bytes 2359304 | tf_op jit(solution)/shard_map/ppermute | solution.py:194
  34.0 3.6 %collective-permute-start.1 = (bf16[768,256]{1,0:T(8,128)(2,1)S(1)}, bf16[768,256]{1,0:T(8,128)(2,1)S(1)}, u32[]{:S(2)}, u32[]{:S(2)}) collective-permute-start(bf16[768,256]{1,0:T(8,128)(2,1)S(1)} %bitcast.11), channel_id=1, source_target_pairs={{0,1},{1,0},{2,3},{3,2},{4,5},{5,4},{6,7},{7,6},{8,9},{9,8},{10,11... | collective-permute-start | bytes 1179656 | tf_op jit(solution)/shard_map/ppermute | solution.py:194
  92.0 4.2 %collective-permute-start.2 = (f32[768,256]{1,0:T(8,128)S(1)}, f32[768,256]{1,0:T(8,128)S(1)}, u32[]{:S(2)}, u32[]{:S(2)}) collective-permute-start(f32[768,256]{1,0:T(8,128)S(1)} %half_product.7), channel_id=1, source_target_pairs={{0,1},{1,0},{2,3},{3,2},{4,5},{5,4},{6,7},{7,6},{8,9},{9,8},{10,11... | collective-permute-start | bytes 2359304 | tf_op jit(solution)/shard_map/ppermute | solution.py:194
  97.1 12.1 %all-to-all-start.5 = ((bf16[4,192,256]{2,1,0:T(8,128)(2,1)}), bf16[4,192,256]{2,1,0:T(8,128)(2,1)S(1)}, u32[]{:S(2)}, u32[]{:S(2)}) async-start(bf16[4,192,256]{2,1,0:T(8,128)(2,1)} %convert_element_type.38), calls=%async_computation.5 | async-start | bytes 786432 | tf_op jit(solution)/shard_map/all_to_all | solution.py:217

commit v3 on v2

v3 whole, which is shorter than its diff:
```python
import math

import jax
import jax.numpy as jnp
from jax import lax
from jax.experimental import pallas as pl
from jax.experimental.pallas import tpu as pltpu
from jax.sharding import Mesh, PartitionSpec as P

D = 7168
K = 256
HALF = K // 2
HIGH = lax.Precision.HIGHEST

def dot(a, b, over_a=1, over_b=0, precision=None):
    return lax.dot_general(
        a, b, (((over_a,), (over_b,)), ((), ())), precision=precision, preferred_element_type=jnp.float32
    )


def terms(a, count):
    parts = []
    for _ in range(count):
        parts.append(a.astype(jnp.bfloat16))
        a = a - parts[-1].astype(jnp.float32)
    return parts


def factor_kernel(packed_ref, rows_ref, basis_ref, factor_ref, gram_ref, g_ref, x_ref, work_ref):
    bf16 = jnp.bfloat16
    corner = packed_ref[HALF : 2 * HALF, :]
    gram_ref[:HALF, :HALF] = packed_ref[:HALF, :]
    gram_ref[:HALF, HALF:] = corner
    gram_ref[HALF:, :HALF] = corner.T
    gram_ref[HALF:, HALF:] = packed_ref[2 * HALF :, :]
    row = lax.broadcasted_iota(jnp.int32, (K, K), 0)
    col = lax.broadcasted_iota(jnp.int32, (K, K), 1)
    eye = (row == col).astype(jnp.float32)
    upper = jnp.where(row < col, 1.0, jnp.where(row == col, 0.5, 0.0))
    on_diag = jnp.where(row == col, gram_ref[...], 0.0)
    s_row = lax.rsqrt(jnp.sum(on_diag, axis=0, keepdims=True))
    s_col = lax.rsqrt(jnp.sum(on_diag, axis=1, keepdims=True))

    def change_for(g):
        f = (g - eye) * upper
        fb = f.astype(bf16)
        a = f - dot(fb, fb, 0, 0) * upper
        ab = a.astype(bf16)
        return (dot(ab, ab) - a).astype(bf16)

    def moved(g, n):
        y = g + sum(dot(part, n) for part in terms(g, 3))
        return y + sum(dot(n, part, 0, 0) for part in terms(y, 3))

    def size(e):
        return jnp.sum(e * e)

    g = gram_ref[...] * s_row * s_col
    n = change_for(g)
    x_ref[...] = s_col * (eye + n.astype(jnp.float32))
    g_ref[...] = moved(g, n)

    def step(state):
        count, _ = state
        g = g_ref[...]
        n = change_for(g)
        g = moved(g, n)
        g_ref[...] = g
        x = x_ref[...]
        x_ref[...] = x + sum(dot(part, n) for part in terms(x, 3))
        return count + 1, size(g - eye)

    def more(state):
        count, err = state
        return jnp.logical_and(count < 12, err > 1e-5)

    _, err = lax.while_loop(more, step, (jnp.int32(0), jnp.float32(1.0)))
    ok = err <= 1e-5

    @pl.when(ok)
    def _():
        x = x_ref[...]
        last = ((g_ref[...] - eye) * upper).astype(bf16)
        x_ref[...] = x - sum(dot(part, last) for part in terms(x, 2))

    @pl.when(jnp.logical_not(ok))
    def _():
        work_ref[:, :K] = gram_ref[...]
        work_ref[:, K:] = eye
        lane = lax.broadcasted_iota(jnp.int32, (1, 2 * K), 1)

        def eliminate(k, carry):
            line = work_ref[pl.ds(k, 1), :]
            pivot = jnp.sum(jnp.where(lane == k, line, 0.0), axis=1, keepdims=True)
            line = line * lax.rsqrt(pivot)
            coef = jnp.where(lane[:, :K] > k, line[:, :K], 0.0)
            work_ref[...] = work_ref[...] - dot(coef, line, 0, 0, HIGH)
            work_ref[pl.ds(k, 1), :] = line
            return carry

        lax.fori_loop(0, K, eliminate, 0)
        x_ref[...] = work_ref[:, K:].T

    x = jnp.where(row <= col, x_ref[...], 0.0)
    basis_ref[...] = dot(rows_ref[...], x, precision=HIGH)
    factor_ref[...] = jnp.where(row <= col, dot(x, gram_ref[...], 0, 0, HIGH), 0.0)


def factor_call(packed, rows):
    square = pltpu.VMEM((K, K), jnp.float32)
    return pl.pallas_call(
        factor_kernel,
        out_shape=(jax.ShapeDtypeStruct(rows.shape, jnp.float32), jax.ShapeDtypeStruct((K, K), jnp.float32)),
        in_specs=[WHOLE] * 2,
        out_specs=(WHOLE, WHOLE),
        scratch_shapes=[square, square, square, pltpu.VMEM((K, 2 * K), jnp.float32)],
        compiler_params=PARAMS,
        name="factor",
    )(packed, rows)


WHOLE = pl.BlockSpec(memory_space=pltpu.VMEM)
PARAMS = pltpu.CompilerParams(vmem_limit_bytes=32 * 1024 * 1024)


def streamed_kernel(which_ref, left_ref, right_ref, out_ref):
    out_ref[...] = dot(left_ref[...], right_ref[...])


def streamed_half(hidden, right, half):
    rows, width = hidden.shape
    steps = 2
    tile = rows // 2 // steps
    spec = pltpu.PrefetchScalarGridSpec(
        num_scalar_prefetch=1,
        grid=(steps,),
        in_specs=[
            pl.BlockSpec((tile, width), lambda i, which: (steps * which[0] + i, 0)),
            pl.BlockSpec(right.shape, lambda i, which: (0, 0)),
        ],
        out_specs=pl.BlockSpec((tile, K), lambda i, which: (i, 0)),
    )
    return pl.pallas_call(
        streamed_kernel,
        out_shape=jax.ShapeDtypeStruct((rows // 2, K), jnp.float32),
        grid_spec=spec,
        compiler_params=pltpu.CompilerParams(vmem_limit_bytes=56 * 1024 * 1024),
        name="streamed_half",
    )(half, hidden, right)


SCALAR = pl.BlockSpec(memory_space=pltpu.SMEM)


def half_kernel(which_ref, hidden_ref, right_ref, out_ref):
    rows = out_ref.shape[0]
    out_ref[...] = dot(hidden_ref[pl.ds(pl.multiple_of(which_ref[0] * rows, rows), rows), :], right_ref[...])


def striped_kernel(which_ref, hidden_ref, back_ref, out_ref):
    rows = out_ref.shape[0]
    tile = rows // 4
    blocks = [hidden_ref[pl.ds(pl.multiple_of((2 * i + which_ref[0]) * tile, tile), tile), :] for i in range(4)]
    out_ref[...] = dot(jnp.concatenate(blocks, axis=0), back_ref[...], 1, 1)


def half_product(kernel, hidden, right, half):
    return pl.pallas_call(
        kernel,
        out_shape=jax.ShapeDtypeStruct((hidden.shape[0] // 2, K), jnp.float32),
        in_specs=[SCALAR, WHOLE, WHOLE],
        out_specs=WHOLE,
        compiler_params=PARAMS,
        name="half_product",
    )(half, hidden, right)


def back_kernel(which_ref, hidden_ref, first_ref, *refs):
    *so_far, out_ref = refs
    rows = first_ref.shape[0]
    part = dot(first_ref[...], hidden_ref[pl.ds(pl.multiple_of(which_ref[0] * rows, rows), rows), :], 0, 0)
    for ref in so_far:
        part = part + ref[...]
    out_ref[...] = part.astype(out_ref.dtype)


def half_back(hidden, first, half, dtype, *so_far):
    return pl.pallas_call(
        back_kernel,
        out_shape=jax.ShapeDtypeStruct((K, hidden.shape[1]), dtype),
        in_specs=[SCALAR, *[WHOLE] * (2 + len(so_far))],
        out_specs=WHOLE,
        compiler_params=PARAMS,
        name="half_back",
    )(half, hidden, first, *so_far)


def gram_kernel(scale, x_ref, landed_ref, kept_ref, other_ref, rows_ref, packed_ref):
    count, tile, _ = landed_ref.shape
    own = pl.ds(pl.multiple_of(x_ref[0] * tile, tile), tile)
    rows = kept_ref[own, :] + other_ref[own, :]
    for i in range(count):
        rows = rows + jnp.where(x_ref[0] == i, 0.0, landed_ref[i].astype(jnp.float32))
    rows_ref[...] = rows
    left, right = rows[:, :HALF], rows[:, HALF:]
    packed_ref[:HALF, :] = dot(left, left, 0, 0, HIGH) * scale
    packed_ref[HALF : 2 * HALF, :] = dot(left, right, 0, 0, HIGH) * scale
    packed_ref[2 * HALF :, :] = dot(right, right, 0, 0, HIGH) * scale


def rows_and_gram(x, landed, kept, other, scale):
    return pl.pallas_call(
        lambda *refs: gram_kernel(scale, *refs),
        out_shape=(
            jax.ShapeDtypeStruct(landed.shape[1:], jnp.float32),
            jax.ShapeDtypeStruct((3 * HALF, HALF), jnp.float32),
        ),
        in_specs=[SCALAR, WHOLE, WHOLE, WHOLE],
        out_specs=(WHOLE, WHOLE),
        compiler_params=PARAMS,
        name="rows_and_gram",
    )(x, landed, kept, other)


ROW = ("y", "z")
COL = ("x", "core")
ALL = (*ROW, *COL)


def swapped(block):
    return lax.ppermute(block, "core", [(0, 1), (1, 0)])


def line_groups(sizes, along):
    ys, zs, xs = sizes
    groups = []
    for core in range(2):
        y_steps, z_steps = along[core]
        for y in range(ys):
            for z in range(zs):
                if any(y // s % n for s, n in y_steps) or any(z // s % n for s, n in z_steps):
                    continue
                spots = [(y, z)]
                for s, n in y_steps:
                    spots = [(a + s * k, b) for a, b in spots for k in range(n)]
                for s, n in z_steps:
                    spots = [(a, b + s * k) for a, b in spots for k in range(n)]
                for x in range(xs):
                    groups.append([((a * zs + b) * xs + x) * 2 + core for a, b in spots])
    return groups


def exchanged(pieces, axis, groups=None):
    return lax.all_to_all(pieces, axis, 0, 0, axis_index_groups=groups)


def spread(block, count):
    return jnp.broadcast_to(block[None], (count, *block.shape))


def total(pieces):
    return jnp.sum(pieces.astype(jnp.float32), axis=0)


def body(sizes, hidden, test_matrix):
    bf16 = jnp.bfloat16
    tok_rows, width = hidden.shape
    tile = tok_rows // 8
    ys, zs, xs = sizes
    total_rows = tok_rows * ys * zs
    core = lax.axis_index("core")
    mine, other = core.reshape(1), (1 - core).reshape(1)

    landed = swapped(streamed_half(hidden, test_matrix, other))
    pieces = (half_product(half_kernel, hidden, test_matrix, mine) + landed).astype(bf16).reshape(xs, tile, K)
    my_first = (total(exchanged(pieces, "x")) * (1.0 / math.sqrt(D))).astype(bf16)
    my_half = exchanged(spread(my_first, xs), "x").reshape(tok_rows // 2, K)
    other_half = swapped(my_half)
    local_back = half_back(hidden, my_half, mine, jnp.float32)
    local_back = half_back(hidden, other_half, other, bf16, local_back)

    pieces = local_back.reshape(ys * zs, K // (ys * zs), width)
    my_back = (total(exchanged(pieces, ROW)) * (1.0 / total_rows)).astype(bf16)
    back = exchanged(spread(my_back, ys * zs), ROW).reshape(K, width)

    landed = swapped(half_product(striped_kernel, hidden, back, other))
    kept = half_product(striped_kernel, hidden, back, mine)
    pieces = exchanged((kept + landed).astype(bf16).reshape(xs, tile, K), "x")
    my_rows, gram = rows_and_gram(lax.axis_index("x").reshape(1), pieces, kept, landed, 1.0 / total_rows)
    gram = total(exchanged(gram.reshape(8, 3 * HALF // 8, HALF), COL))
    lines = [((), ((1, zs),)), (((1, ys),), ())]
    for along in (lines, lines[::-1]):
        groups = line_groups(sizes, along)
        gram = total(exchanged(spread(gram, len(groups[0])), ALL, groups))
    gram = exchanged(spread(gram, 8), COL).reshape(3 * HALF, HALF)
    return factor_call(gram, my_rows)


def solution(mesh):
    rows, cols = mesh.devices.shape
    side = math.isqrt(rows)
    sizes = (side, rows // side, cols // 2)
    grid = Mesh(mesh.devices.reshape(*sizes, 2), ALL)
    in_specs = (P(ROW, COL), P(COL, None))
    out_specs = (P(ALL, None), P())
    return jax.shard_map(
        lambda *args: body(sizes, *args), mesh=grid, in_specs=in_specs, out_specs=out_specs, check_vma=False
    )
```

time: 345 us -> 346 us (level)
    all_to_all x9 -> x8, blocking collectives: 122 us -> 123 us  [exchanged(): return lax.all_to_all(pieces, axis, 0, 0, axis_index_groups=groups)]
  transfers between devices with their start and end apart: 4 -> 4, of which waited for: 3 -> 4; matrix products, arithmetic and copies ran while one was open for 0% -> 0% of each run, Pallas kernels for 1% -> 1%
where the time goes in v3:
time: 346 us; the launch traced here: 343 us
  Pallas kernels  192 us (55%)
  blocking collectives  123 us (36%)
  starting transfers between devices  11.2 us (3%)
  waiting for transfers between devices  10.2 us (3%)
  local copies, waits for them, and re-layouts  5.38 us (2%)
    pallas_call x1, Pallas kernels, factor_call(): pl.pallas_call(factor_kernel, out_shape=(jax.ShapeDtypeStruct(rows.shape,...  185 us
    all_to_all x8, blocking collectives, exchanged(): return lax.all_to_all(pieces, axis, 0, 0, axis_index_groups=groups)  123 us
  transfers between devices with their start and end apart: 4, of which 4 were waited for; matrix products, arithmetic and copies ran while one was open for 0% of the time, Pallas kernels for 1%

profile of v3, /device:TPU:6, one launch (start us, length us, event | category | flops | bytes accessed | tf_op | source)
XLA Modules:
  0.0 343.5 jit_solution(1383574065772761313)
XLA Ops:
  0.7 2.9 streamed_half.1
  3.6 1.9 collective-permute-start
  6.1 1.9 collective-permute-done
  8.1 14.8 %all_to_all.45 = bf16[4,192,256]{2,1,0:T(8,128)(2,1)S(1)} all-to-all(bf16[4,192,256]{2,1,0:T(8,128)(2,1)S(1)} %bitcast.12), channel_id=1, replica_groups=mesh['y'=8,'z'=8,'x'=4,'core'=2] {'x'}, dimensions={0} | all-to-all | bytes 786432 | tf_op jit(solution)/shard_map/all_to_all | solution.py:254
  23.0 10.2 %all_to_all.46 = bf16[4,192,256]{2,1,0:T(8,128)(2,1)S(1)} all-to-all(bf16[4,192,256]{2,1,0:T(8,128)(2,1)S(1)} %broadcast_in_dim.10), channel_id=1, replica_groups=mesh['y'=8,'z'=8,'x'=4,'core'=2] {'x'}, dimensions={0} | all-to-all | bytes 786432 | tf_op jit(solution)/shard_map/all_to_all | solution.py:254
  33.2 1.9 collective-permute-start.1
  35.7 1.1 collective-permute-done.1.first_ref
  37.4 0.9 reshape.50
  38.3 30.4 %all_to_all.47 = bf16[64,4,896]{2,1,0:T(4,128)(2,1)S(1)} all-to-all(bf16[64,4,896]{2,1,0:T(4,128)(2,1)} %reshape.50), channel_id=1, replica_groups=mesh['y'=8,'z'=8,'x'=4,'core'=2] {'y','z'}, dimensions={0} | all-to-all | bytes 917504 | tf_op jit(solution)/shard_map/all_to_all | solution.py:254
  69.1 23.1 %all_to_all.48 = bf16[64,4,896]{2,1,0:T(4,128)(2,1)} all-to-all(bf16[64,4,896]{2,1,0:T(4,128)(2,1)S(1)} %broadcast_in_dim.11), channel_id=1, replica_groups=mesh['y'=8,'z'=8,'x'=4,'core'=2] {'y','z'}, dimensions={0} | all-to-all | bytes 917504 | tf_op jit(solution)/shard_map/all_to_all | solution.py:254
  92.2 1.1 reshape.51.back_ref
  94.1 1.9 collective-permute-start.2
  96.0 1.0 copy-done.2
  97.6 0.6 collective-permute-done.2.refs_3_
  98.3 0.8 add_convert_fusion
  99.1 0.9 copy-done.3
  100.0 5.5 %all-to-all-start.4 = ((bf16[4,192,256]{2,1,0:T(8,128)(2,1)}), bf16[4,192,256]{2,1,0:T(8,128)(2,1)S(1)}, u32[]{:S(2)}, u32[]{:S(2)}) async-start(bf16[4,192,256]{2,1,0:T(8,128)(2,1)} %bitcast.5), calls=%async_computation.4 | async-start | bytes 786432 | tf_op jit(solution)/shard_map/all_to_all | solution.py:254
  105.5 6.6 %all-to-all-done.4.refs_1_ = bf16[4,192,256]{2,1,0:T(8,128)(2,1)S(1)} async-done(((bf16[4,192,256]{2,1,0:T(8,128)(2,1)}), bf16[4,192,256]{2,1,0:T(8,128)(2,1)S(1)}, u32[]{:S(2)}, u32[]{:S(2)}) %all-to-all-start.4) | async-done | bytes 393248 | tf_op jit(solution)/shard_map/all_to_all | solution.py:254
  112.1 1.1 copy-done.4
  113.7 9.2 %all_to_all.49 = f32[8,48,128]{2,1,0:T(8,128)S(1)} all-to-all(f32[8,48,128]{2,1,0:T(8,128)S(1)} %bitcast.11), channel_id=1, replica_groups=mesh['y'=8,'z'=8,'x'=4,'core'=2] {'x','core'}, dimensions={0} | all-to-all | bytes 393216 | tf_op jit(solution)/shard_map/all_to_all | solution.py:254
  123.0 13.5 %all_to_all.50 = f32[8,48,128]{2,1,0:T(8,128)S(1)} all-to-all(f32[8,48,128]{2,1,0:T(8,128)S(1)} %broadcast_in_dim.12), channel_id=1, replica_groups={{0,8,16,24,32,40,48,56},{2,10,18,26,34,42,50,58},{4,12,20,28,36,44,52,6..., dimensions={0} | all-to-all | bytes 393216 | tf_op jit(solution)/shard_map/all_to_all | solution.py:254
  136.5 12.2 %all_to_all.51 = f32[8,48,128]{2,1,0:T(8,128)S(1)} all-to-all(f32[8,48,128]{2,1,0:T(8,128)S(1)} %broadcast_in_dim.13), channel_id=1, replica_groups={{0,64,128,192,256,320,384,448},{2,66,130,194,258,322,386,450},{4,68,132..., dimensions={0} | all-to-all | bytes 393216 | tf_op jit(solution)/shard_map/all_to_all | solution.py:254
  148.7 9.2 %all_to_all.52 = f32[8,48,128]{2,1,0:T(8,128)S(1)} all-to-all(f32[8,48,128]{2,1,0:T(8,128)S(1)} %broadcast_in_dim.14), channel_id=1, replica_groups=mesh['y'=8,'z'=8,'x'=4,'core'=2] {'x','core'}, dimensions={0} | all-to-all | bytes 393216 | tf_op jit(solution)/shard_map/all_to_all | solution.py:254
  158.0 185.5 %factor.1 = (f32[192,256]{1,0:T(8,128)}, f32[256,256]{1,0:T(8,128)}) custom-call(f32[384,128]{1,0:T(8,128)S(1)} %bitcast.10, f32[192,256]{1,0:T(8,128)S(1)} %get-tuple-element.5.rows_ref), custom_call_target="tpu_custom_call" | custom-call | tf_op jit(solution)/shard_map/factor/pallas_call | solution.py:111
  (28 shorter events, 4.3 us)
Async XLA Ops:
  0.6 4.9 %copy-start = (bf16[1536,896]{1,0:T(8,128)(2,1)S(1)}, bf16[1536,896]{1,0:T(8,128)(2,1)}, u32[]{:S(2)}) copy-start(bf16[1536,896]{1,0:T(8,128)(2,1)} %hidden_ref.9) | copy-start | bytes 8257540
  0.6 4.9 %copy-start.5 = (bf16[896,256]{1,0:T(8,128)(2,1)S(1)}, bf16[896,256]{1,0:T(8,128)(2,1)}, u32[]{:S(2)}) copy-start(bf16[896,256]{1,0:T(8,128)(2,1)} %right_ref.3) | copy-start | bytes 1376260
  3.6 4.4 %collective-permute-start = (f32[768,256]{1,0:T(8,128)}, f32[768,256]{1,0:T(8,128)S(1)}, u32[]{:S(2)}, u32[]{:S(2)}) collective-permute-start(f32[768,256]{1,0:T(8,128)} %streamed_half.1), channel_id=1, source_target_pairs={{0,1},{1,0},{2,3},{3,2},{4,5},{5,4},{6,7},{7,6},{8,9},{9,8},{10,11... | collective-permute-start | bytes 2359304 | tf_op jit(solution)/shard_map/ppermute | solution.py:231
  33.2 3.6 %collective-permute-start.1 = (bf16[768,256]{1,0:T(8,128)(2,1)S(1)}, bf16[768,256]{1,0:T(8,128)(2,1)S(1)}, u32[]{:S(2)}, u32[]{:S(2)}) collective-permute-start(bf16[768,256]{1,0:T(8,128)(2,1)S(1)} %bitcast.8), channel_id=1, source_target_pairs={{0,1},{1,0},{2,3},{3,2},{4,5},{5,4},{6,7},{7,6},{8,9},{9,8},{10,11... | collective-permute-start | bytes 1179656 | tf_op jit(solution)/shard_map/ppermute | solution.py:231
  93.3 0.8 copy-start.1
  94.1 4.2 %collective-permute-start.2 = (f32[768,256]{1,0:T(8,128)S(1)}, f32[768,256]{1,0:T(8,128)S(1)}, u32[]{:S(2)}, u32[]{:S(2)}) collective-permute-start(f32[768,256]{1,0:T(8,128)S(1)} %half_product.5), channel_id=1, source_target_pairs={{0,1},{1,0},{2,3},{3,2},{4,5},{5,4},{6,7},{7,6},{8,9},{9,8},{10,11... | collective-permute-start | bytes 2359304 | tf_op jit(solution)/shard_map/ppermute | solution.py:231
  96.0 1.0 copy-start.2
  99.1 0.9 copy-start.3
  100.0 12.1 %all-to-all-start.4 = ((bf16[4,192,256]{2,1,0:T(8,128)(2,1)}), bf16[4,192,256]{2,1,0:T(8,128)(2,1)S(1)}, u32[]{:S(2)}, u32[]{:S(2)}) async-start(bf16[4,192,256]{2,1,0:T(8,128)(2,1)} %bitcast.5), calls=%async_computation.4 | async-start | bytes 786432 | tf_op jit(solution)/shard_map/all_to_all | solution.py:254
  112.1 1.1 copy-start.4

commit v4 on v3

--- a/solution.py
+++ b/solution.py
@@ -120,35 +120,43 @@
 
 
 WHOLE = pl.BlockSpec(memory_space=pltpu.VMEM)
-PARAMS = pltpu.CompilerParams(vmem_limit_bytes=32 * 1024 * 1024)
-
-
-def streamed_kernel(which_ref, left_ref, right_ref, out_ref):
-    out_ref[...] = dot(left_ref[...], right_ref[...])
+PARAMS = pltpu.CompilerParams(vmem_limit_bytes=12 * 1024 * 1024)
+
+
+def streamed_kernel(which_ref, left_ref, right_ref, out_ref, left_buf, right_buf, sems):
+    rows = out_ref.shape[0]
+    tile = rows // STEPS
+    copies = [pltpu.make_async_copy(right_ref, right_buf, sems.at[STEPS])]
+    for i in range(STEPS):
+        start = pl.multiple_of(which_ref[0] * rows + i * tile, tile)
+        copies.append(pltpu.make_async_copy(left_ref.at[pl.ds(start, tile), :], left_buf.at[i], sems.at[i]))
+    for copy in copies:
+        copy.start()
+    copies[0].wait()
+    for i in range(STEPS):
+        copies[1 + i].wait()
+        out_ref[i * tile : (i + 1) * tile, :] = dot(left_buf[i], right_buf[...])
 
 
 def streamed_half(hidden, right, half):
     rows, width = hidden.shape
-    steps = 2
-    tile = rows // 2 // steps
-    spec = pltpu.PrefetchScalarGridSpec(
-        num_scalar_prefetch=1,
-        grid=(steps,),
-        in_specs=[
-            pl.BlockSpec((tile, width), lambda i, which: (steps * which[0] + i, 0)),
-            pl.BlockSpec(right.shape, lambda i, which: (0, 0)),
-        ],
-        out_specs=pl.BlockSpec((tile, K), lambda i, which: (i, 0)),
-    )
+    in_hbm = pl.BlockSpec(memory_space=pltpu.HBM)
     return pl.pallas_call(
         streamed_kernel,
         out_shape=jax.ShapeDtypeStruct((rows // 2, K), jnp.float32),
-        grid_spec=spec,
-        compiler_params=pltpu.CompilerParams(vmem_limit_bytes=56 * 1024 * 1024),
+        in_specs=[SCALAR, in_hbm, in_hbm],
+        out_specs=WHOLE,
+        scratch_shapes=[
+            pltpu.VMEM((STEPS, rows // 2 // STEPS, width), hidden.dtype),
+            pltpu.VMEM(right.shape, right.dtype),
+            pltpu.SemaphoreType.DMA((STEPS + 1,)),
+        ],
+        compiler_params=pltpu.CompilerParams(vmem_limit_bytes=60 * 1024 * 1024),
         name="streamed_half",
     )(half, hidden, right)
 
 
+STEPS = 2
 SCALAR = pl.BlockSpec(memory_space=pltpu.SMEM)
 
 
@@ -271,10 +279,11 @@
     core = lax.axis_index("core")
     mine, other = core.reshape(1), (1 - core).reshape(1)
 
-    landed = swapped(streamed_half(hidden, test_matrix, other))
-    pieces = (half_product(half_kernel, hidden, test_matrix, mine) + landed).astype(bf16).reshape(xs, tile, K)
-    my_first = (total(exchanged(pieces, "x")) * (1.0 / math.sqrt(D))).astype(bf16)
-    my_half = exchanged(spread(my_first, xs), "x").reshape(tok_rows // 2, K)
+    send = streamed_half(hidden, test_matrix, other)
+    send, hidden, test_matrix = lax.optimization_barrier((send, hidden, test_matrix))
+    landed = swapped(send)
+    half_first = (half_product(half_kernel, hidden, test_matrix, mine) + landed).astype(bf16)
+    my_half = (total(exchanged(spread(half_first, xs), "x")) * (1.0 / math.sqrt(D))).astype(bf16)
     other_half = swapped(my_half)
     local_back = half_back(hidden, my_half, mine, jnp.float32)
     local_back = half_back(hidden, other_half, other, bf16, local_back)

time: 346 us -> 350 us (1.012)
    all_to_all x8 -> x7, blocking collectives: 123 us -> 126 us  [exchanged(): return lax.all_to_all(pieces, axis, 0, 0, axis_index_groups=groups)]
where the time goes in v4:
time: 350 us; the launch traced here: 347 us
  Pallas kernels  192 us (55%)
  blocking collectives  126 us (36%)
  starting transfers between devices  11.2 us (3%)
  waiting for transfers between devices  10.1 us (3%)
  local copies, waits for them, and re-layouts  5.46 us (2%)
    pallas_call x1, Pallas kernels, factor_call(): pl.pallas_call(factor_kernel, out_shape=(jax.ShapeDtypeStruct(rows.shape,...  185 us
    all_to_all x7, blocking collectives, exchanged(): return lax.all_to_all(pieces, axis, 0, 0, axis_index_groups=groups)  126 us
  transfers between devices with their start and end apart: 4, of which 4 were waited for; matrix products, arithmetic and copies ran while one was open for 0% of the time, Pallas kernels for 1%

profile of v4, /device:TPU:6, one launch (start us, length us, event | category | flops | bytes accessed | tf_op | source)
XLA Modules:
  0.0 347.2 jit_solution(15609094120644631792)
XLA Ops:
  0.7 3.4 streamed_half.1
  4.1 1.9 collective-permute-start
  6.6 1.9 collective-permute-done
  8.7 27.5 %all_to_all.40 = bf16[4,768,256]{2,1,0:T(8,128)(2,1)S(1)} all-to-all(bf16[4,768,256]{2,1,0:T(8,128)(2,1)S(1)} %broadcast_in_dim.10), channel_id=1, replica_groups=mesh['y'=8,'z'=8,'x'=4,'core'=2] {'x'}, dimensions={0} | all-to-all | bytes 3145728 | tf_op jit(solution)/shard_map/all_to_all | solution.py:262
  36.5 1.9 collective-permute-start.1
  38.5 0.6 half_back.2.refs_0_
  39.1 1.1 collective-permute-done.1.first_ref
  40.1 0.6 half_back.3
  40.8 0.9 reshape.39
  41.7 30.8 %all_to_all.41 = bf16[64,4,896]{2,1,0:T(4,128)(2,1)S(1)} all-to-all(bf16[64,4,896]{2,1,0:T(4,128)(2,1)} %reshape.39), channel_id=1, replica_groups=mesh['y'=8,'z'=8,'x'=4,'core'=2] {'y','z'}, dimensions={0} | all-to-all | bytes 917504 | tf_op jit(solution)/shard_map/all_to_all | solution.py:262
  72.8 23.1 %all_to_all.42 = bf16[64,4,896]{2,1,0:T(4,128)(2,1)} all-to-all(bf16[64,4,896]{2,1,0:T(4,128)(2,1)S(1)} %broadcast_in_dim.11), channel_id=1, replica_groups=mesh['y'=8,'z'=8,'x'=4,'core'=2] {'y','z'}, dimensions={0} | all-to-all | bytes 917504 | tf_op jit(solution)/shard_map/all_to_all | solution.py:262
  95.9 1.1 reshape.40.back_ref
  97.8 1.9 collective-permute-start.2
  99.8 1.0 copy-done.2
  102.0 0.8 add_convert_fusion
  102.8 0.9 copy-done.3
  103.7 5.5 %all-to-all-start.3 = ((bf16[4,192,256]{2,1,0:T(8,128)(2,1)}), bf16[4,192,256]{2,1,0:T(8,128)(2,1)S(1)}, u32[]{:S(2)}, u32[]{:S(2)}) async-start(bf16[4,192,256]{2,1,0:T(8,128)(2,1)} %bitcast.3), calls=%async_computation.3 | async-start | bytes 786432 | tf_op jit(solution)/shard_map/all_to_all | solution.py:262
  109.2 6.6 %all-to-all-done.3.refs_1_ = bf16[4,192,256]{2,1,0:T(8,128)(2,1)S(1)} async-done(((bf16[4,192,256]{2,1,0:T(8,128)(2,1)}), bf16[4,192,256]{2,1,0:T(8,128)(2,1)S(1)}, u32[]{:S(2)}, u32[]{:S(2)}) %all-to-all-start.3) | async-done | bytes 393248 | tf_op jit(solution)/shard_map/all_to_all | solution.py:262
  115.8 1.1 copy-done.4
  117.4 9.2 %all_to_all.43 = f32[8,48,128]{2,1,0:T(8,128)S(1)} all-to-all(f32[8,48,128]{2,1,0:T(8,128)S(1)} %bitcast.7), channel_id=1, replica_groups=mesh['y'=8,'z'=8,'x'=4,'core'=2] {'x','core'}, dimensions={0} | all-to-all | bytes 393216 | tf_op jit(solution)/shard_map/all_to_all | solution.py:262
  126.7 13.4 %all_to_all.44 = f32[8,48,128]{2,1,0:T(8,128)S(1)} all-to-all(f32[8,48,128]{2,1,0:T(8,128)S(1)} %broadcast_in_dim.12), channel_id=1, replica_groups={{0,8,16,24,32,40,48,56},{2,10,18,26,34,42,50,58},{4,12,20,28,36,44,52,6..., dimensions={0} | all-to-all | bytes 393216 | tf_op jit(solution)/shard_map/all_to_all | solution.py:262
  140.2 12.2 %all_to_all.45 = f32[8,48,128]{2,1,0:T(8,128)S(1)} all-to-all(f32[8,48,128]{2,1,0:T(8,128)S(1)} %broadcast_in_dim.13), channel_id=1, replica_groups={{0,64,128,192,256,320,384,448},{2,66,130,194,258,322,386,450},{4,68,132..., dimensions={0} | all-to-all | bytes 393216 | tf_op jit(solution)/shard_map/all_to_all | solution.py:262
  152.5 9.2 %all_to_all.46 = f32[8,48,128]{2,1,0:T(8,128)S(1)} all-to-all(f32[8,48,128]{2,1,0:T(8,128)S(1)} %broadcast_in_dim.14), channel_id=1, replica_groups=mesh['y'=8,'z'=8,'x'=4,'core'=2] {'x','core'}, dimensions={0} | all-to-all | bytes 393216 | tf_op jit(solution)/shard_map/all_to_all | solution.py:262
  161.7 185.5 %factor.1 = (f32[192,256]{1,0:T(8,128)}, f32[256,256]{1,0:T(8,128)}) custom-call(f32[384,128]{1,0:T(8,128)S(1)} %bitcast.6, f32[192,256]{1,0:T(8,128)S(1)} %get-tuple-element.11.rows_ref), custom_call_target="tpu_custom_call" | custom-call | tf_op jit(solution)/shard_map/factor/pallas_call | solution.py:111
  (27 shorter events, 4.1 us)
Async XLA Ops:
  0.6 5.4 %copy-start = (bf16[1536,896]{1,0:T(8,128)(2,1)S(1)}, bf16[1536,896]{1,0:T(8,128)(2,1)}, u32[]{:S(2)}) copy-start(bf16[1536,896]{1,0:T(8,128)(2,1)} %hidden_ref.4) | copy-start | bytes 8257540
  0.6 5.4 %copy-start.5 = (bf16[896,256]{1,0:T(8,128)(2,1)S(1)}, bf16[896,256]{1,0:T(8,128)(2,1)}, u32[]{:S(2)}) copy-start(bf16[896,256]{1,0:T(8,128)(2,1)} %right_ref.2) | copy-start | bytes 1376260
  4.1 4.4 %collective-permute-start = (f32[768,256]{1,0:T(8,128)}, f32[768,256]{1,0:T(8,128)S(1)}, u32[]{:S(2)}, u32[]{:S(2)}) collective-permute-start(f32[768,256]{1,0:T(8,128)} %streamed_half.1), channel_id=1, source_target_pairs={{0,1},{1,0},{2,3},{3,2},{4,5},{5,4},{6,7},{7,6},{8,9},{9,8},{10,11... | collective-permute-start | bytes 2359304 | tf_op jit(solution)/shard_map/ppermute | solution.py:239
  36.5 3.6 %collective-permute-start.1 = (bf16[768,256]{1,0:T(8,128)(2,1)S(1)}, bf16[768,256]{1,0:T(8,128)(2,1)S(1)}, u32[]{:S(2)}, u32[]{:S(2)}) collective-permute-start(bf16[768,256]{1,0:T(8,128)(2,1)S(1)} %multiply_convert_fusion.first_ref), channel_id=1, source_target_pairs={{0,1},{1,0},{2,3},{3,2},{4,5},{5,4},{6,7},{7,6},{8,9},{9,8},{10,11... | collective-permute-start | bytes 1179656 | tf_op jit(solution)/shard_map/ppermute | solution.py:239
  97.1 0.8 copy-start.1
  97.8 4.2 %collective-permute-start.2 = (f32[768,256]{1,0:T(8,128)S(1)}, f32[768,256]{1,0:T(8,128)S(1)}, u32[]{:S(2)}, u32[]{:S(2)}) collective-permute-start(f32[768,256]{1,0:T(8,128)S(1)} %half_product.5), channel_id=1, source_target_pairs={{0,1},{1,0},{2,3},{3,2},{4,5},{5,4},{6,7},{7,6},{8,9},{9,8},{10,11... | collective-permute-start | bytes 2359304 | tf_op jit(solution)/shard_map/ppermute | solution.py:239
  99.7 1.0 copy-start.2
  102.8 0.9 copy-start.3
  103.7 12.1 %all-to-all-start.3 = ((bf16[4,192,256]{2,1,0:T(8,128)(2,1)}), bf16[4,192,256]{2,1,0:T(8,128)(2,1)S(1)}, u32[]{:S(2)}, u32[]{:S(2)}) async-start(bf16[4,192,256]{2,1,0:T(8,128)(2,1)} %bitcast.3), calls=%async_computation.3 | async-start | bytes 786432 | tf_op jit(solution)/shard_map/all_to_all | solution.py:262
  115.8 1.1 copy-start.4

commit v5 on v3

--- a/solution.py
+++ b/solution.py
@@ -120,32 +120,34 @@
 
 
 WHOLE = pl.BlockSpec(memory_space=pltpu.VMEM)
-PARAMS = pltpu.CompilerParams(vmem_limit_bytes=32 * 1024 * 1024)
-
-
-def streamed_kernel(which_ref, left_ref, right_ref, out_ref):
-    out_ref[...] = dot(left_ref[...], right_ref[...])
-
-
-def streamed_half(hidden, right, half):
-    rows, width = hidden.shape
-    steps = 2
-    tile = rows // 2 // steps
-    spec = pltpu.PrefetchScalarGridSpec(
-        num_scalar_prefetch=1,
-        grid=(steps,),
-        in_specs=[
-            pl.BlockSpec((tile, width), lambda i, which: (steps * which[0] + i, 0)),
-            pl.BlockSpec(right.shape, lambda i, which: (0, 0)),
-        ],
-        out_specs=pl.BlockSpec((tile, K), lambda i, which: (i, 0)),
-    )
-    return pl.pallas_call(
-        streamed_kernel,
-        out_shape=jax.ShapeDtypeStruct((rows // 2, K), jnp.float32),
-        grid_spec=spec,
-        compiler_params=pltpu.CompilerParams(vmem_limit_bytes=56 * 1024 * 1024),
-        name="streamed_half",
+PARAMS = pltpu.CompilerParams(vmem_limit_bytes=12 * 1024 * 1024)
+
+
+def opening_kernel(which_ref, hidden_ref, right_ref, send_ref, hidden_out, sems):
+    rows = send_ref.shape[0]
+    halves = [pl.ds(pl.multiple_of(half * rows, rows), rows) for half in (which_ref[0], 1 - which_ref[0])]
+    copies = [
+        pltpu.make_async_copy(hidden_ref.at[half, :], hidden_out.at[half, :], sems.at[i]) for i, half in enumerate(halves)
+    ]
+    for copy in copies:
+        copy.start()
+    copies[0].wait()
+    send_ref[...] = dot(hidden_out[halves[0], :], right_ref[...])
+    copies[1].wait()
+
+
+def opening(hidden, right, half):
+    return pl.pallas_call(
+        opening_kernel,
+        out_shape=(
+            jax.ShapeDtypeStruct((hidden.shape[0] // 2, K), jnp.float32),
+            jax.ShapeDtypeStruct(hidden.shape, hidden.dtype),
+        ),
+        in_specs=[SCALAR, pl.BlockSpec(memory_space=pltpu.HBM), WHOLE],
+        out_specs=(WHOLE, WHOLE),
+        scratch_shapes=[pltpu.SemaphoreType.DMA((2,))],
+        compiler_params=pltpu.CompilerParams(vmem_limit_bytes=49 * 1024 * 1024),
+        name="opening",
     )(half, hidden, right)
 
 
@@ -181,13 +183,18 @@
     part = dot(first_ref[...], hidden_ref[pl.ds(pl.multiple_of(which_ref[0] * rows, rows), rows), :], 0, 0)
     for ref in so_far:
         part = part + ref[...]
-    out_ref[...] = part.astype(out_ref.dtype)
-
-
-def half_back(hidden, first, half, dtype, *so_far):
+    if len(out_ref.shape) == 2:
+        out_ref[...] = part
+        return
+    count, rows, _ = out_ref.shape
+    for i in range(count):
+        out_ref[i] = part[i * rows : (i + 1) * rows, :].astype(out_ref.dtype)
+
+
+def half_back(hidden, first, half, shape, dtype, *so_far):
     return pl.pallas_call(
         back_kernel,
-        out_shape=jax.ShapeDtypeStruct((K, hidden.shape[1]), dtype),
+        out_shape=jax.ShapeDtypeStruct(shape, dtype),
         in_specs=[SCALAR, *[WHOLE] * (2 + len(so_far))],
         out_specs=WHOLE,
         compiler_params=PARAMS,
@@ -195,11 +202,53 @@
     )(half, hidden, first, *so_far)
 
 
-def gram_kernel(scale, x_ref, landed_ref, kept_ref, other_ref, rows_ref, packed_ref):
-    count, tile, _ = landed_ref.shape
+def join_kernel(pieces_ref, out_ref):
+    count, rows, _ = pieces_ref.shape
+    step = 16 // rows
+    for i in range(0, count, step):
+        parts = [pieces_ref[i + j].astype(jnp.float32) for j in range(step)]
+        out_ref[i * rows : (i + step) * rows, :] = jnp.concatenate(parts, axis=0).astype(out_ref.dtype)
+
+
+def joined(pieces):
+    count, rows, width = pieces.shape
+    return pl.pallas_call(
+        join_kernel,
+        out_shape=jax.ShapeDtypeStruct((count * rows, width), pieces.dtype),
+        in_specs=[WHOLE],
+        out_specs=WHOLE,
+        compiler_params=PARAMS,
+        name="joined",
+    )(pieces)
+
+
+def sum_kernel(x_ref, kept_ref, landed_ref, own_ref, pieces_ref):
+    count, tile, _ = pieces_ref.shape
     own = pl.ds(pl.multiple_of(x_ref[0] * tile, tile), tile)
-    rows = kept_ref[own, :] + other_ref[own, :]
+    own_ref[...] = kept_ref[own, :] + landed_ref[own, :]
     for i in range(count):
+        block = slice(i * tile, (i + 1) * tile)
+        pieces_ref[i] = (kept_ref[block, :] + landed_ref[block, :]).astype(pieces_ref.dtype)
+
+
+def sum_of_halves(x, kept, landed, count):
+    tile = kept.shape[0] // count
+    return pl.pallas_call(
+        sum_kernel,
+        out_shape=(
+            jax.ShapeDtypeStruct((tile, K), jnp.float32),
+            jax.ShapeDtypeStruct((count, tile, K), jnp.bfloat16),
+        ),
+        in_specs=[SCALAR, WHOLE, WHOLE],
+        out_specs=(WHOLE, WHOLE),
+        compiler_params=PARAMS,
+        name="sum_of_halves",
+    )(x, kept, landed)
+
+
+def gram_kernel(scale, x_ref, landed_ref, own_ref, rows_ref, packed_ref):
+    rows = own_ref[...]
+    for i in range(landed_ref.shape[0]):
         rows = rows + jnp.where(x_ref[0] == i, 0.0, landed_ref[i].astype(jnp.float32))
     rows_ref[...] = rows
     left, right = rows[:, :HALF], rows[:, HALF:]
@@ -208,18 +257,18 @@
     packed_ref[2 * HALF :, :] = dot(right, right, 0, 0, HIGH) * scale
 
 
-def rows_and_gram(x, landed, kept, other, scale):
+def rows_and_gram(x, landed, own, scale):
     return pl.pallas_call(
         lambda *refs: gram_kernel(scale, *refs),
         out_shape=(
             jax.ShapeDtypeStruct(landed.shape[1:], jnp.float32),
             jax.ShapeDtypeStruct((3 * HALF, HALF), jnp.float32),
         ),
-        in_specs=[SCALAR, WHOLE, WHOLE, WHOLE],
+        in_specs=[SCALAR, WHOLE, WHOLE],
         out_specs=(WHOLE, WHOLE),
         compiler_params=PARAMS,
         name="rows_and_gram",
-    )(x, landed, kept, other)
+    )(x, landed, own)
 
 
 ROW = ("y", "z")
@@ -271,22 +320,24 @@
     core = lax.axis_index("core")
     mine, other = core.reshape(1), (1 - core).reshape(1)
 
-    landed = swapped(streamed_half(hidden, test_matrix, other))
+    send, hidden = opening(hidden, test_matrix, other)
+    landed = swapped(send)
     pieces = (half_product(half_kernel, hidden, test_matrix, mine) + landed).astype(bf16).reshape(xs, tile, K)
     my_first = (total(exchanged(pieces, "x")) * (1.0 / math.sqrt(D))).astype(bf16)
     my_half = exchanged(spread(my_first, xs), "x").reshape(tok_rows // 2, K)
     other_half = swapped(my_half)
-    local_back = half_back(hidden, my_half, mine, jnp.float32)
-    local_back = half_back(hidden, other_half, other, bf16, local_back)
-
-    pieces = local_back.reshape(ys * zs, K // (ys * zs), width)
+    local_back = half_back(hidden, my_half, mine, (K, width), jnp.float32)
+    shape = (ys * zs, K // (ys * zs), width)
+    pieces = half_back(hidden, other_half, other, shape, bf16, local_back)
+
     my_back = (total(exchanged(pieces, ROW)) * (1.0 / total_rows)).astype(bf16)
-    back = exchanged(spread(my_back, ys * zs), ROW).reshape(K, width)
+    back = joined(exchanged(spread(my_back, ys * zs), ROW))
 
     landed = swapped(half_product(striped_kernel, hidden, back, other))
     kept = half_product(striped_kernel, hidden, back, mine)
-    pieces = exchanged((kept + landed).astype(bf16).reshape(xs, tile, K), "x")
-    my_rows, gram = rows_and_gram(lax.axis_index("x").reshape(1), pieces, kept, landed, 1.0 / total_rows)
+    x = lax.axis_index("x").reshape(1)
+    own, pieces = sum_of_halves(x, kept, landed, xs)
+    my_rows, gram = rows_and_gram(x, exchanged(pieces, "x"), own, 1.0 / total_rows)
     gram = total(exchanged(gram.reshape(8, 3 * HALF // 8, HALF), COL))
     lines = [((), ((1, zs),)), (((1, ys),), ())]
     for along in (lines, lines[::-1]):

time: 346 us -> 342 us (0.988)
  blocking collectives: 123 us -> 133 us
  waiting for transfers between devices: 10.2 us -> 4.71 us
  starting transfers between devices: 11.2 us -> 5.74 us
  local copies, waits for them, and re-layouts: 5.38 us -> 1.21 us
    all_to_all x8 -> x9, blocking collectives: 123 us -> 133 us  [exchanged(): return lax.all_to_all(pieces, axis, 0, 0, axis_index_groups=groups)]
    all_to_all x1 -> x0, waiting for transfers between devices: 6.58 us -> none  [exchanged(): return lax.all_to_all(pieces, axis, 0, 0, axis_index_groups=groups)]
    all_to_all x1 -> x0, starting transfers between devices: 5.5 us -> none  [exchanged(): return lax.all_to_all(pieces, axis, 0, 0, axis_index_groups=groups)]
  transfers between devices with their start and end apart: 4 -> 3, of which waited for: 4 -> 3; matrix products, arithmetic and copies ran while one was open for 0% -> 0% of each run, Pallas kernels for 1% -> 1%
where the time goes in v5:
time: 342 us; the launch traced here: 339 us
  Pallas kernels  193 us (56%)
  blocking collectives  133 us (39%)
  starting transfers between devices  5.74 us (2%)
  waiting for transfers between devices  4.71 us (1%)
    pallas_call x1, Pallas kernels, factor_call(): pl.pallas_call(factor_kernel, out_shape=(jax.ShapeDtypeStruct(rows.shape,...  185 us
    all_to_all x9, blocking collectives, exchanged(): return lax.all_to_all(pieces, axis, 0, 0, axis_index_groups=groups)  133 us
  transfers between devices with their start and end apart: 3, of which 3 were waited for; matrix products, arithmetic and copies ran while one was open for 0% of the time, Pallas kernels for 1%

profile of v5, /device:TPU:6, one launch (start us, length us, event | category | flops | bytes accessed | tf_op | source)
XLA Modules:
  0.0 339.5 jit_solution(7663818462589923688)
XLA Ops:
  0.6 1.0 copy-done
  1.7 1.9 opening.1
  3.6 1.9 collective-permute-start
  5.5 0.6 half_product.3
  6.1 1.7 collective-permute-done
  7.9 14.8 %all_to_all.45 = bf16[4,192,256]{2,1,0:T(8,128)(2,1)S(1)} all-to-all(bf16[4,192,256]{2,1,0:T(8,128)(2,1)S(1)} %bitcast.11), channel_id=1, replica_groups=mesh['y'=8,'z'=8,'x'=4,'core'=2] {'x'}, dimensions={0} | all-to-all | bytes 786432 | tf_op jit(solution)/shard_map/all_to_all | solution.py:303
  22.8 10.2 %all_to_all.46 = bf16[4,192,256]{2,1,0:T(8,128)(2,1)S(1)} all-to-all(bf16[4,192,256]{2,1,0:T(8,128)(2,1)S(1)} %broadcast_in_dim.10), channel_id=1, replica_groups=mesh['y'=8,'z'=8,'x'=4,'core'=2] {'x'}, dimensions={0} | all-to-all | bytes 786432 | tf_op jit(solution)/shard_map/all_to_all | solution.py:303
  33.1 1.9 collective-permute-start.1
  35.0 0.6 half_back.2.refs_0_
  35.6 1.1 collective-permute-done.1.first_ref
  36.7 0.6 half_back.3
  37.3 30.2 %all_to_all.47 = bf16[64,4,896]{2,1,0:T(4,128)(2,1)S(1)} all-to-all(bf16[64,4,896]{2,1,0:T(4,128)(2,1)S(1)} %half_back.3), channel_id=1, replica_groups=mesh['y'=8,'z'=8,'x'=4,'core'=2] {'y','z'}, dimensions={0} | all-to-all | bytes 917504 | tf_op jit(solution)/shard_map/all_to_all | solution.py:303
  67.9 23.0 %all_to_all.48.pieces_ref = bf16[64,4,896]{2,1,0:T(4,128)(2,1)S(1)} all-to-all(bf16[64,4,896]{2,1,0:T(4,128)(2,1)S(1)} %broadcast_in_dim.11), channel_id=1, replica_groups=mesh['y'=8,'z'=8,'x'=4,'core'=2] {'y','z'}, dimensions={0} | all-to-all | bytes 917504 | tf_op jit(solution)/shard_map/all_to_all | solution.py:303
  91.0 1.5 half_product.5
  92.5 1.9 collective-permute-start.2
  94.4 0.6 half_product.4.kept_ref
  95.0 2.0 collective-permute-done.2.landed_ref
  97.0 1.2 sum_of_halves.1
  98.2 11.1 %all_to_all.49.refs_1_ = bf16[4,192,256]{2,1,0:T(8,128)(2,1)S(1)} all-to-all(bf16[4,192,256]{2,1,0:T(8,128)(2,1)S(1)} %get-tuple-element.10), channel_id=1, replica_groups=mesh['y'=8,'z'=8,'x'=4,'core'=2] {'x'}, dimensions={0} | all-to-all | bytes 786432 | tf_op jit(solution)/shard_map/all_to_all | solution.py:303
  109.8 9.2 %all_to_all.50 = f32[8,48,128]{2,1,0:T(8,128)S(1)} all-to-all(f32[8,48,128]{2,1,0:T(8,128)S(1)} %bitcast.10), channel_id=1, replica_groups=mesh['y'=8,'z'=8,'x'=4,'core'=2] {'x','core'}, dimensions={0} | all-to-all | bytes 393216 | tf_op jit(solution)/shard_map/all_to_all | solution.py:303
  119.1 13.4 %all_to_all.51 = f32[8,48,128]{2,1,0:T(8,128)S(1)} all-to-all(f32[8,48,128]{2,1,0:T(8,128)S(1)} %broadcast_in_dim.12), channel_id=1, replica_groups={{0,8,16,24,32,40,48,56},{2,10,18,26,34,42,50,58},{4,12,20,28,36,44,52,6..., dimensions={0} | all-to-all | bytes 393216 | tf_op jit(solution)/shard_map/all_to_all | solution.py:303
  132.5 12.2 %all_to_all.52 = f32[8,48,128]{2,1,0:T(8,128)S(1)} all-to-all(f32[8,48,128]{2,1,0:T(8,128)S(1)} %broadcast_in_dim.13), channel_id=1, replica_groups={{0,64,128,192,256,320,384,448},{2,66,130,194,258,322,386,450},{4,68,132..., dimensions={0} | all-to-all | bytes 393216 | tf_op jit(solution)/shard_map/all_to_all | solution.py:303
  144.8 9.2 %all_to_all.53 = f32[8,48,128]{2,1,0:T(8,128)S(1)} all-to-all(f32[8,48,128]{2,1,0:T(8,128)S(1)} %broadcast_in_dim.14), channel_id=1, replica_groups=mesh['y'=8,'z'=8,'x'=4,'core'=2] {'x','core'}, dimensions={0} | all-to-all | bytes 393216 | tf_op jit(solution)/shard_map/all_to_all | solution.py:303
  154.0 185.5 %factor.1 = (f32[192,256]{1,0:T(8,128)}, f32[256,256]{1,0:T(8,128)}) custom-call(f32[384,128]{1,0:T(8,128)S(1)} %bitcast.9, f32[192,256]{1,0:T(8,128)S(1)} %get-tuple-element.13.rows_ref), custom_call_target="tpu_custom_call" | custom-call | tf_op jit(solution)/shard_map/factor/pallas_call | solution.py:111
  (16 shorter events, 1.3 us)
Async XLA Ops:
  0.6 1.0 copy-start
  3.6 4.2 %collective-permute-start = (f32[768,256]{1,0:T(8,128)S(1)}, f32[768,256]{1,0:T(8,128)S(1)}, u32[]{:S(2)}, u32[]{:S(2)}) collective-permute-start(f32[768,256]{1,0:T(8,128)S(1)} %get-tuple-element.9), channel_id=1, source_target_pairs={{0,1},{1,0},{2,3},{3,2},{4,5},{5,4},{6,7},{7,6},{8,9},{9,8},{10,11... | collective-permute-start | bytes 2359304 | tf_op jit(solution)/shard_map/ppermute | solution.py:280
  33.1 3.6 %collective-permute-start.1 = (bf16[768,256]{1,0:T(8,128)(2,1)S(1)}, bf16[768,256]{1,0:T(8,128)(2,1)S(1)}, u32[]{:S(2)}, u32[]{:S(2)}) collective-permute-start(bf16[768,256]{1,0:T(8,128)(2,1)S(1)} %bitcast.7), channel_id=1, source_target_pairs={{0,1},{1,0},{2,3},{3,2},{4,5},{5,4},{6,7},{7,6},{8,9},{9,8},{10,11... | collective-permute-start | bytes 1179656 | tf_op jit(solution)/shard_map/ppermute | solution.py:280
  92.5 4.5 %collective-permute-start.2 = (f32[768,256]{1,0:T(8,128)}, f32[768,256]{1,0:T(8,128)}, u32[]{:S(2)}, u32[]{:S(2)}) collective-permute-start(f32[768,256]{1,0:T(8,128)} %half_product.5), channel_id=1, source_target_pairs={{0,1},{1,0},{2,3},{3,2},{4,5},{5,4},{6,7},{7,6},{8,9},{9,8},{10,11... | collective-permute-start | bytes 2359304 | tf_op jit(solution)/shard_map/ppermute | solution.py:280

commit v6 on v3

--- a/solution.py
+++ b/solution.py
@@ -120,32 +120,34 @@
 
 
 WHOLE = pl.BlockSpec(memory_space=pltpu.VMEM)
-PARAMS = pltpu.CompilerParams(vmem_limit_bytes=32 * 1024 * 1024)
-
-
-def streamed_kernel(which_ref, left_ref, right_ref, out_ref):
-    out_ref[...] = dot(left_ref[...], right_ref[...])
-
-
-def streamed_half(hidden, right, half):
-    rows, width = hidden.shape
-    steps = 2
-    tile = rows // 2 // steps
-    spec = pltpu.PrefetchScalarGridSpec(
-        num_scalar_prefetch=1,
-        grid=(steps,),
-        in_specs=[
-            pl.BlockSpec((tile, width), lambda i, which: (steps * which[0] + i, 0)),
-            pl.BlockSpec(right.shape, lambda i, which: (0, 0)),
-        ],
-        out_specs=pl.BlockSpec((tile, K), lambda i, which: (i, 0)),
-    )
-    return pl.pallas_call(
-        streamed_kernel,
-        out_shape=jax.ShapeDtypeStruct((rows // 2, K), jnp.float32),
-        grid_spec=spec,
-        compiler_params=pltpu.CompilerParams(vmem_limit_bytes=56 * 1024 * 1024),
-        name="streamed_half",
+PARAMS = pltpu.CompilerParams(vmem_limit_bytes=12 * 1024 * 1024)
+
+
+def opening_kernel(which_ref, hidden_ref, right_ref, send_ref, hidden_out, sems):
+    rows = send_ref.shape[0]
+    halves = [pl.ds(pl.multiple_of(half * rows, rows), rows) for half in (which_ref[0], 1 - which_ref[0])]
+    copies = [
+        pltpu.make_async_copy(hidden_ref.at[half, :], hidden_out.at[half, :], sems.at[i]) for i, half in enumerate(halves)
+    ]
+    for copy in copies:
+        copy.start()
+    copies[0].wait()
+    send_ref[...] = dot(hidden_out[halves[0], :], right_ref[...])
+    copies[1].wait()
+
+
+def opening(hidden, right, half):
+    return pl.pallas_call(
+        opening_kernel,
+        out_shape=(
+            jax.ShapeDtypeStruct((hidden.shape[0] // 2, K), jnp.float32),
+            jax.ShapeDtypeStruct(hidden.shape, hidden.dtype),
+        ),
+        in_specs=[SCALAR, pl.BlockSpec(memory_space=pltpu.HBM), WHOLE],
+        out_specs=(WHOLE, WHOLE),
+        scratch_shapes=[pltpu.SemaphoreType.DMA((2,))],
+        compiler_params=pltpu.CompilerParams(vmem_limit_bytes=49 * 1024 * 1024),
+        name="opening",
     )(half, hidden, right)
 
 
@@ -195,12 +197,10 @@
     )(half, hidden, first, *so_far)
 
 
-def gram_kernel(scale, x_ref, landed_ref, kept_ref, other_ref, rows_ref, packed_ref):
-    count, tile, _ = landed_ref.shape
-    own = pl.ds(pl.multiple_of(x_ref[0] * tile, tile), tile)
-    rows = kept_ref[own, :] + other_ref[own, :]
-    for i in range(count):
-        rows = rows + jnp.where(x_ref[0] == i, 0.0, landed_ref[i].astype(jnp.float32))
+def gram_kernel(scale, landed_ref, rows_ref, packed_ref):
+    rows = landed_ref[0]
+    for i in range(1, landed_ref.shape[0]):
+        rows = rows + landed_ref[i]
     rows_ref[...] = rows
     left, right = rows[:, :HALF], rows[:, HALF:]
     packed_ref[:HALF, :] = dot(left, left, 0, 0, HIGH) * scale
@@ -208,18 +208,18 @@
     packed_ref[2 * HALF :, :] = dot(right, right, 0, 0, HIGH) * scale
 
 
-def rows_and_gram(x, landed, kept, other, scale):
+def rows_and_gram(landed, scale):
     return pl.pallas_call(
         lambda *refs: gram_kernel(scale, *refs),
         out_shape=(
             jax.ShapeDtypeStruct(landed.shape[1:], jnp.float32),
             jax.ShapeDtypeStruct((3 * HALF, HALF), jnp.float32),
         ),
-        in_specs=[SCALAR, WHOLE, WHOLE, WHOLE],
+        in_specs=[WHOLE],
         out_specs=(WHOLE, WHOLE),
         compiler_params=PARAMS,
         name="rows_and_gram",
-    )(x, landed, kept, other)
+    )(landed)
 
 
 ROW = ("y", "z")
@@ -271,7 +271,8 @@
     core = lax.axis_index("core")
     mine, other = core.reshape(1), (1 - core).reshape(1)
 
-    landed = swapped(streamed_half(hidden, test_matrix, other))
+    send, hidden = opening(hidden, test_matrix, other)
+    landed = swapped(send)
     pieces = (half_product(half_kernel, hidden, test_matrix, mine) + landed).astype(bf16).reshape(xs, tile, K)
     my_first = (total(exchanged(pieces, "x")) * (1.0 / math.sqrt(D))).astype(bf16)
     my_half = exchanged(spread(my_first, xs), "x").reshape(tok_rows // 2, K)
@@ -279,18 +280,20 @@
     local_back = half_back(hidden, my_half, mine, jnp.float32)
     local_back = half_back(hidden, other_half, other, bf16, local_back)
 
-    pieces = local_back.reshape(ys * zs, K // (ys * zs), width)
-    my_back = (total(exchanged(pieces, ROW)) * (1.0 / total_rows)).astype(bf16)
-    back = exchanged(spread(my_back, ys * zs), ROW).reshape(K, width)
+    lines = ((), ((1, zs),)), (((1, ys),), ())
+    this_way, that_way = line_groups(sizes, lines), line_groups(sizes, lines[::-1])
+    count = len(this_way[0])
+    pieces = local_back.reshape(count, K // count, width)
+    my_back = total(exchanged(pieces, ALL, this_way)).astype(bf16)
+    my_back = total(exchanged(spread(my_back, len(that_way[0])), ALL, that_way))
+    my_back = (my_back * (1.0 / total_rows)).astype(bf16)
+    back = exchanged(spread(my_back, count), ALL, this_way).reshape(K, width)
 
     landed = swapped(half_product(striped_kernel, hidden, back, other))
-    kept = half_product(striped_kernel, hidden, back, mine)
-    pieces = exchanged((kept + landed).astype(bf16).reshape(xs, tile, K), "x")
-    my_rows, gram = rows_and_gram(lax.axis_index("x").reshape(1), pieces, kept, landed, 1.0 / total_rows)
+    pieces = (half_product(striped_kernel, hidden, back, mine) + landed).reshape(xs, tile, K)
+    my_rows, gram = rows_and_gram(exchanged(pieces, "x"), 1.0 / total_rows)
     gram = total(exchanged(gram.reshape(8, 3 * HALF // 8, HALF), COL))
-    lines = [((), ((1, zs),)), (((1, ys),), ())]
-    for along in (lines, lines[::-1]):
-        groups = line_groups(sizes, along)
+    for groups in (this_way, that_way):
         gram = total(exchanged(spread(gram, len(groups[0])), ALL, groups))
     gram = exchanged(spread(gram, 8), COL).reshape(3 * HALF, HALF)
     return factor_call(gram, my_rows)

time: 346 us -> 342 us (0.988)
  blocking collectives: 123 us -> 136 us
  waiting for transfers between devices: 10.2 us -> 4.37 us
  starting transfers between devices: 11.2 us -> 5.75 us
  local copies, waits for them, and re-layouts: 5.38 us -> 1.15 us
    all_to_all x8 -> x10, blocking collectives: 123 us -> 136 us  [exchanged(): return lax.all_to_all(pieces, axis, 0, 0, axis_index_groups=groups)]
    all_to_all x1 -> x0, waiting for transfers between devices: 6.58 us -> none  [exchanged(): return lax.all_to_all(pieces, axis, 0, 0, axis_index_groups=groups)]
    all_to_all x1 -> x0, starting transfers between devices: 5.5 us -> none  [exchanged(): return lax.all_to_all(pieces, axis, 0, 0, axis_index_groups=groups)]
  transfers between devices with their start and end apart: 4 -> 3, of which waited for: 4 -> 3; matrix products, arithmetic and copies ran while one was open for 0% -> 0% of each run, Pallas kernels for 1% -> 1%
where the time goes in v6:
time: 342 us; the launch traced here: 339 us
  Pallas kernels  191 us (56%)
  blocking collectives  136 us (40%)
  starting transfers between devices  5.75 us (2%)
  waiting for transfers between devices  4.37 us (1%)
    pallas_call x1, Pallas kernels, factor_call(): pl.pallas_call(factor_kernel, out_shape=(jax.ShapeDtypeStruct(rows.shape,...  185 us
    all_to_all x10, blocking collectives, exchanged(): return lax.all_to_all(pieces, axis, 0, 0, axis_index_groups=groups)  136 us
  transfers between devices with their start and end apart: 3, of which 3 were waited for; matrix products, arithmetic and copies ran while one was open for 0% of the time, Pallas kernels for 1%

profile of v6, /device:TPU:6, one launch (start us, length us, event | category | flops | bytes accessed | tf_op | source)
XLA Modules:
  0.0 339.4 jit_solution(14504335212458334353)
XLA Ops:
  0.6 1.0 copy-done
  1.7 1.9 opening.1
  3.6 1.9 collective-permute-start
  5.5 0.6 half_product.3
  6.1 1.7 collective-permute-done
  7.9 14.8 %all_to_all.50 = bf16[4,192,256]{2,1,0:T(8,128)(2,1)S(1)} all-to-all(bf16[4,192,256]{2,1,0:T(8,128)(2,1)S(1)} %bitcast.17), channel_id=1, replica_groups=mesh['y'=8,'z'=8,'x'=4,'core'=2] {'x'}, dimensions={0} | all-to-all | bytes 786432 | tf_op jit(solution)/shard_map/all_to_all | solution.py:254
  22.8 10.2 %all_to_all.51 = bf16[4,192,256]{2,1,0:T(8,128)(2,1)S(1)} all-to-all(bf16[4,192,256]{2,1,0:T(8,128)(2,1)S(1)} %broadcast_in_dim.12), channel_id=1, replica_groups=mesh['y'=8,'z'=8,'x'=4,'core'=2] {'x'}, dimensions={0} | all-to-all | bytes 786432 | tf_op jit(solution)/shard_map/all_to_all | solution.py:254
  33.1 1.9 collective-permute-start.1
  35.0 0.6 half_back.2.refs_0_
  35.6 1.1 collective-permute-done.1.first_ref
  36.7 0.6 half_back.3
  37.3 18.3 %all_to_all.52 = bf16[8,32,896]{2,1,0:T(8,128)(2,1)S(1)} all-to-all(bf16[8,32,896]{2,1,0:T(8,128)(2,1)S(1)} %bitcast.11), channel_id=1, replica_groups={{0,8,16,24,32,40,48,56},{2,10,18,26,34,42,50,58},{4,12,20,28,36,44,52,6..., dimensions={0} | all-to-all | bytes 917504 | tf_op jit(solution)/shard_map/all_to_all | solution.py:254
  55.7 19.5 %all_to_all.53 = bf16[8,32,896]{2,1,0:T(8,128)(2,1)S(1)} all-to-all(bf16[8,32,896]{2,1,0:T(8,128)(2,1)S(1)} %broadcast_in_dim.13), channel_id=1, replica_groups={{0,64,128,192,256,320,384,448},{2,66,130,194,258,322,386,450},{4,68,132..., dimensions={0} | all-to-all | bytes 917504 | tf_op jit(solution)/shard_map/all_to_all | solution.py:254
  75.3 15.0 %all_to_all.54 = bf16[8,32,896]{2,1,0:T(8,128)(2,1)S(1)} all-to-all(bf16[8,32,896]{2,1,0:T(8,128)(2,1)S(1)} %broadcast_in_dim.14), channel_id=1, replica_groups={{0,8,16,24,32,40,48,56},{2,10,18,26,34,42,50,58},{4,12,20,28,36,44,52,6..., dimensions={0} | all-to-all | bytes 917504 | tf_op jit(solution)/shard_map/all_to_all | solution.py:254
  90.3 0.6 half_product.5
  90.9 1.9 collective-permute-start.2
  92.9 0.6 half_product.4
  93.5 1.6 collective-permute-done.2
  95.2 15.3 %all_to_all.55.refs_0_ = f32[4,192,256]{2,1,0:T(8,128)S(1)} all-to-all(f32[4,192,256]{2,1,0:T(8,128)S(1)} %bitcast.16), channel_id=1, replica_groups=mesh['y'=8,'z'=8,'x'=4,'core'=2] {'x'}, dimensions={0} | all-to-all | bytes 1572864 | tf_op jit(solution)/shard_map/all_to_all | solution.py:254
  111.0 9.2 %all_to_all.56 = f32[8,48,128]{2,1,0:T(8,128)S(1)} all-to-all(f32[8,48,128]{2,1,0:T(8,128)S(1)} %bitcast.15), channel_id=1, replica_groups=mesh['y'=8,'z'=8,'x'=4,'core'=2] {'x','core'}, dimensions={0} | all-to-all | bytes 393216 | tf_op jit(solution)/shard_map/all_to_all | solution.py:254
  120.3 12.2 %all_to_all.57 = f32[8,48,128]{2,1,0:T(8,128)S(1)} all-to-all(f32[8,48,128]{2,1,0:T(8,128)S(1)} %broadcast_in_dim.15), channel_id=1, replica_groups={{0,8,16,24,32,40,48,56},{2,10,18,26,34,42,50,58},{4,12,20,28,36,44,52,6..., dimensions={0} | all-to-all | bytes 393216 | tf_op jit(solution)/shard_map/all_to_all | solution.py:254
  132.5 12.2 %all_to_all.58 = f32[8,48,128]{2,1,0:T(8,128)S(1)} all-to-all(f32[8,48,128]{2,1,0:T(8,128)S(1)} %broadcast_in_dim.16), channel_id=1, replica_groups={{0,64,128,192,256,320,384,448},{2,66,130,194,258,322,386,450},{4,68,132..., dimensions={0} | all-to-all | bytes 393216 | tf_op jit(solution)/shard_map/all_to_all | solution.py:254
  144.7 9.2 %all_to_all.59 = f32[8,48,128]{2,1,0:T(8,128)S(1)} all-to-all(f32[8,48,128]{2,1,0:T(8,128)S(1)} %broadcast_in_dim.17), channel_id=1, replica_groups=mesh['y'=8,'z'=8,'x'=4,'core'=2] {'x','core'}, dimensions={0} | all-to-all | bytes 393216 | tf_op jit(solution)/shard_map/all_to_all | solution.py:254
  153.9 185.5 %factor.1 = (f32[192,256]{1,0:T(8,128)}, f32[256,256]{1,0:T(8,128)}) custom-call(f32[384,128]{1,0:T(8,128)S(1)} %bitcast.14, f32[192,256]{1,0:T(8,128)S(1)} %get-tuple-element.9.rows_ref), custom_call_target="tpu_custom_call" | custom-call | tf_op jit(solution)/shard_map/factor/pallas_call | solution.py:111
  (18 shorter events, 1.2 us)
Async XLA Ops:
  0.6 1.0 copy-start
  3.6 4.2 %collective-permute-start = (f32[768,256]{1,0:T(8,128)S(1)}, f32[768,256]{1,0:T(8,128)S(1)}, u32[]{:S(2)}, u32[]{:S(2)}) collective-permute-start(f32[768,256]{1,0:T(8,128)S(1)} %get-tuple-element.7), channel_id=1, source_target_pairs={{0,1},{1,0},{2,3},{3,2},{4,5},{5,4},{6,7},{7,6},{8,9},{9,8},{10,11... | collective-permute-start | bytes 2359304 | tf_op jit(solution)/shard_map/ppermute | solution.py:231
  33.1 3.6 %collective-permute-start.1 = (bf16[768,256]{1,0:T(8,128)(2,1)S(1)}, bf16[768,256]{1,0:T(8,128)(2,1)S(1)}, u32[]{:S(2)}, u32[]{:S(2)}) collective-permute-start(bf16[768,256]{1,0:T(8,128)(2,1)S(1)} %bitcast.12), channel_id=1, source_target_pairs={{0,1},{1,0},{2,3},{3,2},{4,5},{5,4},{6,7},{7,6},{8,9},{9,8},{10,11... | collective-permute-start | bytes 1179656 | tf_op jit(solution)/shard_map/ppermute | solution.py:231
  90.9 4.2 %collective-permute-start.2 = (f32[768,256]{1,0:T(8,128)S(1)}, f32[768,256]{1,0:T(8,128)S(1)}, u32[]{:S(2)}, u32[]{:S(2)}) collective-permute-start(f32[768,256]{1,0:T(8,128)S(1)} %half_product.5), channel_id=1, source_target_pairs={{0,1},{1,0},{2,3},{3,2},{4,5},{5,4},{6,7},{7,6},{8,9},{9,8},{10,11... | collective-permute-start | bytes 2359304 | tf_op jit(solution)/shard_map/ppermute | solution.py:231

commit v7 on v6

--- a/solution.py
+++ b/solution.py
@@ -18,12 +18,9 @@
     )
 
 
-def terms(a, count):
-    parts = []
-    for _ in range(count):
-        parts.append(a.astype(jnp.bfloat16))
-        a = a - parts[-1].astype(jnp.float32)
-    return parts
+def terms(a):
+    high = a.astype(jnp.bfloat16)
+    return high, (a - high.astype(jnp.float32)).astype(jnp.bfloat16)
 
 
 def factor_kernel(packed_ref, rows_ref, basis_ref, factor_ref, gram_ref, g_ref, x_ref, work_ref):
@@ -49,8 +46,8 @@
         return (dot(ab, ab) - a).astype(bf16)
 
     def moved(g, n):
-        y = g + sum(dot(part, n) for part in terms(g, 3))
-        return y + sum(dot(n, part, 0, 0) for part in terms(y, 3))
+        y = g + sum(dot(part, n) for part in terms(g))
+        return y + sum(dot(n, part, 0, 0) for part in terms(y))
 
     def size(e):
         return jnp.sum(e * e)
@@ -67,7 +64,7 @@
         g = moved(g, n)
         g_ref[...] = g
         x = x_ref[...]
-        x_ref[...] = x + sum(dot(part, n) for part in terms(x, 3))
+        x_ref[...] = x + sum(dot(part, n) for part in terms(x))
         return count + 1, size(g - eye)
 
     def more(state):
@@ -81,7 +78,7 @@
     def _():
         x = x_ref[...]
         last = ((g_ref[...] - eye) * upper).astype(bf16)
-        x_ref[...] = x - sum(dot(part, last) for part in terms(x, 2))
+        x_ref[...] = x - dot(x.astype(bf16), last)
 
     @pl.when(jnp.logical_not(ok))
     def _():
@@ -132,7 +129,7 @@
     for copy in copies:
         copy.start()
     copies[0].wait()
-    send_ref[...] = dot(hidden_out[halves[0], :], right_ref[...])
+    send_ref[...] = dot(hidden_out[halves[0], :], right_ref[...]).astype(send_ref.dtype)
     copies[1].wait()
 
 
@@ -140,7 +137,7 @@
     return pl.pallas_call(
         opening_kernel,
         out_shape=(
-            jax.ShapeDtypeStruct((hidden.shape[0] // 2, K), jnp.float32),
+            jax.ShapeDtypeStruct((hidden.shape[0] // 2, K), jnp.bfloat16),
             jax.ShapeDtypeStruct(hidden.shape, hidden.dtype),
         ),
         in_specs=[SCALAR, pl.BlockSpec(memory_space=pltpu.HBM), WHOLE],
@@ -197,10 +194,32 @@
     )(half, hidden, first, *so_far)
 
 
-def gram_kernel(scale, landed_ref, rows_ref, packed_ref):
-    rows = landed_ref[0]
-    for i in range(1, landed_ref.shape[0]):
-        rows = rows + landed_ref[i]
+def split_kernel(x_ref, whole_ref, own_ref, pieces_ref):
+    count, tile, _ = pieces_ref.shape
+    own_ref[...] = whole_ref[pl.ds(pl.multiple_of(x_ref[0] * tile, tile), tile), :]
+    for i in range(count):
+        pieces_ref[i] = whole_ref[i * tile : (i + 1) * tile, :].astype(pieces_ref.dtype)
+
+
+def own_and_pieces(x, whole, count):
+    tile = whole.shape[0] // count
+    return pl.pallas_call(
+        split_kernel,
+        out_shape=(
+            jax.ShapeDtypeStruct((tile, K), jnp.float32),
+            jax.ShapeDtypeStruct((count, tile, K), jnp.bfloat16),
+        ),
+        in_specs=[SCALAR, WHOLE],
+        out_specs=(WHOLE, WHOLE),
+        compiler_params=PARAMS,
+        name="own_and_pieces",
+    )(x, whole)
+
+
+def gram_kernel(scale, x_ref, landed_ref, own_ref, rows_ref, packed_ref):
+    rows = own_ref[...]
+    for i in range(landed_ref.shape[0]):
+        rows = rows + jnp.where(x_ref[0] == i, 0.0, landed_ref[i].astype(jnp.float32))
     rows_ref[...] = rows
     left, right = rows[:, :HALF], rows[:, HALF:]
     packed_ref[:HALF, :] = dot(left, left, 0, 0, HIGH) * scale
@@ -208,18 +227,18 @@
     packed_ref[2 * HALF :, :] = dot(right, right, 0, 0, HIGH) * scale
 
 
-def rows_and_gram(landed, scale):
+def rows_and_gram(x, landed, own, scale):
     return pl.pallas_call(
         lambda *refs: gram_kernel(scale, *refs),
         out_shape=(
             jax.ShapeDtypeStruct(landed.shape[1:], jnp.float32),
             jax.ShapeDtypeStruct((3 * HALF, HALF), jnp.float32),
         ),
-        in_specs=[WHOLE],
+        in_specs=[SCALAR, WHOLE, WHOLE],
         out_specs=(WHOLE, WHOLE),
         compiler_params=PARAMS,
         name="rows_and_gram",
-    )(landed)
+    )(x, landed, own)
 
 
 ROW = ("y", "z")
@@ -290,8 +309,10 @@
     back = exchanged(spread(my_back, count), ALL, this_way).reshape(K, width)
 
     landed = swapped(half_product(striped_kernel, hidden, back, other))
-    pieces = (half_product(striped_kernel, hidden, back, mine) + landed).reshape(xs, tile, K)
-    my_rows, gram = rows_and_gram(exchanged(pieces, "x"), 1.0 / total_rows)
+    whole = half_product(striped_kernel, hidden, back, mine) + landed
+    x = lax.axis_index("x").reshape(1)
+    own, pieces = own_and_pieces(x, whole, xs)
+    my_rows, gram = rows_and_gram(x, exchanged(pieces, "x"), own, 1.0 / total_rows)
     gram = total(exchanged(gram.reshape(8, 3 * HALF // 8, HALF), COL))
     for groups in (this_way, that_way):
         gram = total(exchanged(spread(gram, len(groups[0])), ALL, groups))

time: 342 us -> 340 us (level)
  blocking collectives: 136 us -> 132 us
    all_to_all x10, blocking collectives: 136 us -> 132 us  [exchanged(): return lax.all_to_all(pieces, axis, 0, 0, axis_index_groups=groups)]
where the time goes in v7:
time: 340 us; the launch traced here: 337 us
  Pallas kernels  192 us (56%)
  blocking collectives  132 us (39%)
  starting transfers between devices  5.74 us (2%)
  waiting for transfers between devices  4.14 us (1%)
    pallas_call x1, Pallas kernels, factor_call(): pl.pallas_call(factor_kernel, out_shape=(jax.ShapeDtypeStruct(rows.shape,...  185 us
    all_to_all x10, blocking collectives, exchanged(): return lax.all_to_all(pieces, axis, 0, 0, axis_index_groups=groups)  132 us
  transfers between devices with their start and end apart: 3, of which 3 were waited for; matrix products, arithmetic and copies ran while one was open for 0% of the time, Pallas kernels for 1%

profile of v7, /device:TPU:6, one launch (start us, length us, event | category | flops | bytes accessed | tf_op | source)
XLA Modules:
  0.0 336.8 jit_solution(3005458339870518500)
XLA Ops:
  0.6 1.0 copy-done
  1.7 1.9 opening.1
  3.6 1.9 collective-permute-start
  6.1 1.1 collective-permute-done
  7.3 14.8 %all_to_all.50 = bf16[4,192,256]{2,1,0:T(8,128)(2,1)S(1)} all-to-all(bf16[4,192,256]{2,1,0:T(8,128)(2,1)S(1)} %bitcast.16), channel_id=1, replica_groups=mesh['y'=8,'z'=8,'x'=4,'core'=2] {'x'}, dimensions={0} | all-to-all | bytes 786432 | tf_op jit(solution)/shard_map/all_to_all | solution.py:273
  22.3 10.2 %all_to_all.51 = bf16[4,192,256]{2,1,0:T(8,128)(2,1)S(1)} all-to-all(bf16[4,192,256]{2,1,0:T(8,128)(2,1)S(1)} %broadcast_in_dim.12), channel_id=1, replica_groups=mesh['y'=8,'z'=8,'x'=4,'core'=2] {'x'}, dimensions={0} | all-to-all | bytes 786432 | tf_op jit(solution)/shard_map/all_to_all | solution.py:273
  32.5 1.9 collective-permute-start.1
  34.4 0.6 half_back.2.refs_0_
  35.0 1.1 collective-permute-done.1.first_ref
  36.1 0.6 half_back.3
  36.7 18.3 %all_to_all.52 = bf16[8,32,896]{2,1,0:T(8,128)(2,1)S(1)} all-to-all(bf16[8,32,896]{2,1,0:T(8,128)(2,1)S(1)} %bitcast.11), channel_id=1, replica_groups={{0,8,16,24,32,40,48,56},{2,10,18,26,34,42,50,58},{4,12,20,28,36,44,52,6..., dimensions={0} | all-to-all | bytes 917504 | tf_op jit(solution)/shard_map/all_to_all | solution.py:273
  55.1 19.5 %all_to_all.53 = bf16[8,32,896]{2,1,0:T(8,128)(2,1)S(1)} all-to-all(bf16[8,32,896]{2,1,0:T(8,128)(2,1)S(1)} %broadcast_in_dim.13), channel_id=1, replica_groups={{0,64,128,192,256,320,384,448},{2,66,130,194,258,322,386,450},{4,68,132..., dimensions={0} | all-to-all | bytes 917504 | tf_op jit(solution)/shard_map/all_to_all | solution.py:273
  74.8 15.0 %all_to_all.54 = bf16[8,32,896]{2,1,0:T(8,128)(2,1)S(1)} all-to-all(bf16[8,32,896]{2,1,0:T(8,128)(2,1)S(1)} %broadcast_in_dim.14), channel_id=1, replica_groups={{0,8,16,24,32,40,48,56},{2,10,18,26,34,42,50,58},{4,12,20,28,36,44,52,6..., dimensions={0} | all-to-all | bytes 917504 | tf_op jit(solution)/shard_map/all_to_all | solution.py:273
  89.7 1.5 half_product.5
  91.2 1.9 collective-permute-start.2
  93.2 0.6 half_product.4
  93.8 2.0 collective-permute-done.2
  95.7 1.2 add.7.whole_ref
  97.0 11.0 %all_to_all.55.refs_1_ = bf16[4,192,256]{2,1,0:T(8,128)(2,1)S(1)} all-to-all(bf16[4,192,256]{2,1,0:T(8,128)(2,1)S(1)} %get-tuple-element.10), channel_id=1, replica_groups=mesh['y'=8,'z'=8,'x'=4,'core'=2] {'x'}, dimensions={0} | all-to-all | bytes 786432 | tf_op jit(solution)/shard_map/all_to_all | solution.py:273
  108.6 9.2 %all_to_all.56 = f32[8,48,128]{2,1,0:T(8,128)S(1)} all-to-all(f32[8,48,128]{2,1,0:T(8,128)S(1)} %bitcast.15), channel_id=1, replica_groups=mesh['y'=8,'z'=8,'x'=4,'core'=2] {'x','core'}, dimensions={0} | all-to-all | bytes 393216 | tf_op jit(solution)/shard_map/all_to_all | solution.py:273
  117.9 12.2 %all_to_all.57 = f32[8,48,128]{2,1,0:T(8,128)S(1)} all-to-all(f32[8,48,128]{2,1,0:T(8,128)S(1)} %broadcast_in_dim.15), channel_id=1, replica_groups={{0,8,16,24,32,40,48,56},{2,10,18,26,34,42,50,58},{4,12,20,28,36,44,52,6..., dimensions={0} | all-to-all | bytes 393216 | tf_op jit(solution)/shard_map/all_to_all | solution.py:273
  130.1 12.2 %all_to_all.58 = f32[8,48,128]{2,1,0:T(8,128)S(1)} all-to-all(f32[8,48,128]{2,1,0:T(8,128)S(1)} %broadcast_in_dim.16), channel_id=1, replica_groups={{0,64,128,192,256,320,384,448},{2,66,130,194,258,322,386,450},{4,68,132..., dimensions={0} | all-to-all | bytes 393216 | tf_op jit(solution)/shard_map/all_to_all | solution.py:273
  142.3 9.2 %all_to_all.59 = f32[8,48,128]{2,1,0:T(8,128)S(1)} all-to-all(f32[8,48,128]{2,1,0:T(8,128)S(1)} %broadcast_in_dim.17), channel_id=1, replica_groups=mesh['y'=8,'z'=8,'x'=4,'core'=2] {'x','core'}, dimensions={0} | all-to-all | bytes 393216 | tf_op jit(solution)/shard_map/all_to_all | solution.py:273
  151.5 185.2 %factor.1 = (f32[192,256]{1,0:T(8,128)}, f32[256,256]{1,0:T(8,128)}) custom-call(f32[384,128]{1,0:T(8,128)S(1)} %bitcast.14, f32[192,256]{1,0:T(8,128)S(1)} %get-tuple-element.13.rows_ref), custom_call_target="tpu_custom_call" | custom-call | tf_op jit(solution)/shard_map/factor/pallas_call | solution.py:108
  (19 shorter events, 1.7 us)
Async XLA Ops:
  0.6 1.0 copy-start
  3.6 3.6 %collective-permute-start = (bf16[768,256]{1,0:T(8,128)(2,1)S(1)}, bf16[768,256]{1,0:T(8,128)(2,1)S(1)}, u32[]{:S(2)}, u32[]{:S(2)}) collective-permute-start(bf16[768,256]{1,0:T(8,128)(2,1)S(1)} %get-tuple-element.9), channel_id=1, source_target_pairs={{0,1},{1,0},{2,3},{3,2},{4,5},{5,4},{6,7},{7,6},{8,9},{9,8},{10,11... | collective-permute-start | bytes 1179656 | tf_op jit(solution)/shard_map/ppermute | solution.py:250
  32.5 3.6 %collective-permute-start.1 = (bf16[768,256]{1,0:T(8,128)(2,1)S(1)}, bf16[768,256]{1,0:T(8,128)(2,1)S(1)}, u32[]{:S(2)}, u32[]{:S(2)}) collective-permute-start(bf16[768,256]{1,0:T(8,128)(2,1)S(1)} %bitcast.12), channel_id=1, source_target_pairs={{0,1},{1,0},{2,3},{3,2},{4,5},{5,4},{6,7},{7,6},{8,9},{9,8},{10,11... | collective-permute-start | bytes 1179656 | tf_op jit(solution)/shard_map/ppermute | solution.py:250
  91.2 4.5 %collective-permute-start.2 = (f32[768,256]{1,0:T(8,128)}, f32[768,256]{1,0:T(8,128)}, u32[]{:S(2)}, u32[]{:S(2)}) collective-permute-start(f32[768,256]{1,0:T(8,128)} %half_product.5), channel_id=1, source_target_pairs={{0,1},{1,0},{2,3},{3,2},{4,5},{5,4},{6,7},{7,6},{8,9},{9,8},{10,11... | collective-permute-start | bytes 2359304 | tf_op jit(solution)/shard_map/ppermute | solution.py:250

commit v8 on v7

--- a/solution.py
+++ b/solution.py
@@ -120,106 +120,113 @@
 PARAMS = pltpu.CompilerParams(vmem_limit_bytes=12 * 1024 * 1024)
 
 
-def opening_kernel(which_ref, hidden_ref, right_ref, send_ref, hidden_out, sems):
+def opening_kernel(place_ref, hidden_ref, right_ref, send_ref, hidden_out, right_out, sems):
     rows = send_ref.shape[0]
-    halves = [pl.ds(pl.multiple_of(half * rows, rows), rows) for half in (which_ref[0], 1 - which_ref[0])]
+    halves = [pl.ds(pl.multiple_of(half * rows, rows), rows) for half in (place_ref[OTHER], place_ref[MINE])]
     copies = [
-        pltpu.make_async_copy(hidden_ref.at[half, :], hidden_out.at[half, :], sems.at[i]) for i, half in enumerate(halves)
+        pltpu.make_async_copy(right_ref, right_out, sems.at[0]),
+        pltpu.make_async_copy(hidden_ref.at[halves[0], :], hidden_out.at[halves[0], :], sems.at[1]),
+        pltpu.make_async_copy(hidden_ref.at[halves[1], :], hidden_out.at[halves[1], :], sems.at[2]),
     ]
     for copy in copies:
         copy.start()
     copies[0].wait()
-    send_ref[...] = dot(hidden_out[halves[0], :], right_ref[...]).astype(send_ref.dtype)
     copies[1].wait()
-
-
-def opening(hidden, right, half):
+    send_ref[...] = dot(hidden_out[halves[0], :], right_out[...]).astype(send_ref.dtype)
+    copies[2].wait()
+
+
+def opening(place, hidden, right):
     return pl.pallas_call(
         opening_kernel,
         out_shape=(
-            jax.ShapeDtypeStruct((hidden.shape[0] // 2, K), jnp.bfloat16),
-            jax.ShapeDtypeStruct(hidden.shape, hidden.dtype),
+            pltpu.VMEM((hidden.shape[0] // 2, K), jnp.bfloat16),
+            pltpu.VMEM(hidden.shape, hidden.dtype),
+            pltpu.VMEM(right.shape, right.dtype),
         ),
-        in_specs=[SCALAR, pl.BlockSpec(memory_space=pltpu.HBM), WHOLE],
-        out_specs=(WHOLE, WHOLE),
-        scratch_shapes=[pltpu.SemaphoreType.DMA((2,))],
-        compiler_params=pltpu.CompilerParams(vmem_limit_bytes=49 * 1024 * 1024),
+        in_specs=[SCALAR, *[pl.BlockSpec(memory_space=pltpu.HBM)] * 2],
+        out_specs=(WHOLE, WHOLE, WHOLE),
+        scratch_shapes=[pltpu.SemaphoreType.DMA((3,))],
+        compiler_params=pltpu.CompilerParams(vmem_limit_bytes=12 * 1024 * 1024),
         name="opening",
-    )(half, hidden, right)
+    )(place, pltpu.with_memory_space_constraint(hidden, pltpu.HBM), pltpu.with_memory_space_constraint(right, pltpu.HBM))
 
 
 SCALAR = pl.BlockSpec(memory_space=pltpu.SMEM)
-
-
-def half_kernel(which_ref, hidden_ref, right_ref, out_ref):
+OTHER, MINE, X = range(3)
+
+
+def half_kernel(half, place_ref, hidden_ref, right_ref, out_ref):
     rows = out_ref.shape[0]
-    out_ref[...] = dot(hidden_ref[pl.ds(pl.multiple_of(which_ref[0] * rows, rows), rows), :], right_ref[...])
-
-
-def striped_kernel(which_ref, hidden_ref, back_ref, out_ref):
+    out_ref[...] = dot(hidden_ref[pl.ds(pl.multiple_of(place_ref[half] * rows, rows), rows), :], right_ref[...])
+
+
+def striped_kernel(half, place_ref, hidden_ref, back_ref, out_ref):
     rows = out_ref.shape[0]
     tile = rows // 4
-    blocks = [hidden_ref[pl.ds(pl.multiple_of((2 * i + which_ref[0]) * tile, tile), tile), :] for i in range(4)]
+    blocks = [hidden_ref[pl.ds(pl.multiple_of((2 * i + place_ref[half]) * tile, tile), tile), :] for i in range(4)]
     out_ref[...] = dot(jnp.concatenate(blocks, axis=0), back_ref[...], 1, 1)
 
 
-def half_product(kernel, hidden, right, half):
-    return pl.pallas_call(
-        kernel,
-        out_shape=jax.ShapeDtypeStruct((hidden.shape[0] // 2, K), jnp.float32),
+def half_product(kernel, half, place, hidden, right):
+    return pl.pallas_call(
+        lambda *refs: kernel(half, *refs),
+        out_shape=pltpu.VMEM((hidden.shape[0] // 2, K), jnp.float32),
         in_specs=[SCALAR, WHOLE, WHOLE],
         out_specs=WHOLE,
         compiler_params=PARAMS,
         name="half_product",
-    )(half, hidden, right)
-
-
-def back_kernel(which_ref, hidden_ref, first_ref, *refs):
+    )(place, hidden, right)
+
+
+def back_kernel(half, place_ref, hidden_ref, first_ref, *refs):
     *so_far, out_ref = refs
     rows = first_ref.shape[0]
-    part = dot(first_ref[...], hidden_ref[pl.ds(pl.multiple_of(which_ref[0] * rows, rows), rows), :], 0, 0)
+    part = dot(first_ref[...], hidden_ref[pl.ds(pl.multiple_of(place_ref[half] * rows, rows), rows), :], 0, 0)
     for ref in so_far:
         part = part + ref[...]
     out_ref[...] = part.astype(out_ref.dtype)
 
 
-def half_back(hidden, first, half, dtype, *so_far):
-    return pl.pallas_call(
-        back_kernel,
+def half_back(half, place, hidden, first, dtype, *so_far):
+    return pl.pallas_call(
+        lambda *refs: back_kernel(half, *refs),
         out_shape=jax.ShapeDtypeStruct((K, hidden.shape[1]), dtype),
         in_specs=[SCALAR, *[WHOLE] * (2 + len(so_far))],
         out_specs=WHOLE,
         compiler_params=PARAMS,
         name="half_back",
-    )(half, hidden, first, *so_far)
-
-
-def split_kernel(x_ref, whole_ref, own_ref, pieces_ref):
+    )(place, hidden, first, *so_far)
+
+
+def sum_kernel(place_ref, kept_ref, landed_ref, own_ref, pieces_ref):
     count, tile, _ = pieces_ref.shape
-    own_ref[...] = whole_ref[pl.ds(pl.multiple_of(x_ref[0] * tile, tile), tile), :]
+    own = pl.ds(pl.multiple_of(place_ref[X] * tile, tile), tile)
+    own_ref[...] = kept_ref[own, :] + landed_ref[own, :]
     for i in range(count):
-        pieces_ref[i] = whole_ref[i * tile : (i + 1) * tile, :].astype(pieces_ref.dtype)
-
-
-def own_and_pieces(x, whole, count):
-    tile = whole.shape[0] // count
-    return pl.pallas_call(
-        split_kernel,
+        block = slice(i * tile, (i + 1) * tile)
+        pieces_ref[i] = (kept_ref[block, :] + landed_ref[block, :]).astype(pieces_ref.dtype)
+
+
+def sum_of_halves(place, kept, landed, count):
+    tile = kept.shape[0] // count
+    return pl.pallas_call(
+        sum_kernel,
         out_shape=(
             jax.ShapeDtypeStruct((tile, K), jnp.float32),
             jax.ShapeDtypeStruct((count, tile, K), jnp.bfloat16),
         ),
-        in_specs=[SCALAR, WHOLE],
+        in_specs=[SCALAR, WHOLE, WHOLE],
         out_specs=(WHOLE, WHOLE),
         compiler_params=PARAMS,
-        name="own_and_pieces",
-    )(x, whole)
-
-
-def gram_kernel(scale, x_ref, landed_ref, own_ref, rows_ref, packed_ref):
+        name="sum_of_halves",
+    )(place, kept, pltpu.with_memory_space_constraint(landed, pltpu.VMEM))
+
+
+def gram_kernel(scale, place_ref, landed_ref, own_ref, rows_ref, packed_ref):
     rows = own_ref[...]
     for i in range(landed_ref.shape[0]):
-        rows = rows + jnp.where(x_ref[0] == i, 0.0, landed_ref[i].astype(jnp.float32))
+        rows = rows + jnp.where(place_ref[X] == i, 0.0, landed_ref[i].astype(jnp.float32))
     rows_ref[...] = rows
     left, right = rows[:, :HALF], rows[:, HALF:]
     packed_ref[:HALF, :] = dot(left, left, 0, 0, HIGH) * scale
@@ -227,7 +234,7 @@
     packed_ref[2 * HALF :, :] = dot(right, right, 0, 0, HIGH) * scale
 
 
-def rows_and_gram(x, landed, own, scale):
+def rows_and_gram(place, landed, own, scale):
     return pl.pallas_call(
         lambda *refs: gram_kernel(scale, *refs),
         out_shape=(
@@ -238,11 +245,12 @@
         out_specs=(WHOLE, WHOLE),
         compiler_params=PARAMS,
         name="rows_and_gram",
-    )(x, landed, own)
-
-
-ROW = ("y", "z")
+    )(place, landed, own)
+
+
+ROW = ("y_hi", "y_lo", "z")
 COL = ("x", "core")
+NEAR = ("y_lo", *COL)
 ALL = (*ROW, *COL)
 
 
@@ -288,16 +296,16 @@
     ys, zs, xs = sizes
     total_rows = tok_rows * ys * zs
     core = lax.axis_index("core")
-    mine, other = core.reshape(1), (1 - core).reshape(1)
-
-    send, hidden = opening(hidden, test_matrix, other)
+    place = jnp.stack([1 - core, core, lax.axis_index("x")])
+
+    send, hidden, test_matrix = opening(place, hidden, test_matrix)
     landed = swapped(send)
-    pieces = (half_product(half_kernel, hidden, test_matrix, mine) + landed).astype(bf16).reshape(xs, tile, K)
+    pieces = (half_product(half_kernel, MINE, place, hidden, test_matrix) + landed).astype(bf16).reshape(xs, tile, K)
     my_first = (total(exchanged(pieces, "x")) * (1.0 / math.sqrt(D))).astype(bf16)
     my_half = exchanged(spread(my_first, xs), "x").reshape(tok_rows // 2, K)
     other_half = swapped(my_half)
-    local_back = half_back(hidden, my_half, mine, jnp.float32)
-    local_back = half_back(hidden, other_half, other, bf16, local_back)
+    local_back = half_back(MINE, place, hidden, my_half, jnp.float32)
+    local_back = half_back(OTHER, place, hidden, other_half, bf16, local_back)
 
     lines = ((), ((1, zs),)), (((1, ys),), ())
     this_way, that_way = line_groups(sizes, lines), line_groups(sizes, lines[::-1])
@@ -308,15 +316,15 @@
     my_back = (my_back * (1.0 / total_rows)).astype(bf16)
     back = exchanged(spread(my_back, count), ALL, this_way).reshape(K, width)
 
-    landed = swapped(half_product(striped_kernel, hidden, back, other))
-    whole = half_product(striped_kernel, hidden, back, mine) + landed
-    x = lax.axis_index("x").reshape(1)
-    own, pieces = own_and_pieces(x, whole, xs)
-    my_rows, gram = rows_and_gram(x, exchanged(pieces, "x"), own, 1.0 / total_rows)
-    gram = total(exchanged(gram.reshape(8, 3 * HALF // 8, HALF), COL))
-    for groups in (this_way, that_way):
-        gram = total(exchanged(spread(gram, len(groups[0])), ALL, groups))
-    gram = exchanged(spread(gram, 8), COL).reshape(3 * HALF, HALF)
+    landed = swapped(half_product(striped_kernel, OTHER, place, hidden, back))
+    kept = half_product(striped_kernel, MINE, place, hidden, back)
+    own, pieces = sum_of_halves(place, kept, landed, xs)
+    my_rows, gram = rows_and_gram(place, exchanged(pieces, "x"), own, 1.0 / total_rows)
+    count = 4 * xs
+    gram = total(exchanged(gram.reshape(count, 3 * HALF // count, HALF), NEAR))
+    gram = total(exchanged(spread(gram, zs), "z"))
+    gram = total(exchanged(spread(gram, ys // 2), "y_hi"))
+    gram = exchanged(spread(gram, count), NEAR).reshape(3 * HALF, HALF)
     return factor_call(gram, my_rows)
 
 
@@ -324,7 +332,7 @@
     rows, cols = mesh.devices.shape
     side = math.isqrt(rows)
     sizes = (side, rows // side, cols // 2)
-    grid = Mesh(mesh.devices.reshape(*sizes, 2), ALL)
+    grid = Mesh(mesh.devices.reshape(side // 2, 2, *sizes[1:], 2), ALL)
     in_specs = (P(ROW, COL), P(COL, None))
     out_specs = (P(ALL, None), P())
     return jax.shard_map(

time: 340 us -> 338 us (level)
  no operation moved by 1% of the time
where the time goes in v8:
time: 338 us; the launch traced here: 335 us
  Pallas kernels  195 us (58%)
  blocking collectives  130 us (38%)
  starting transfers between devices  5.75 us (2%)
    pallas_call x1, Pallas kernels, factor_call(): pl.pallas_call(factor_kernel, out_shape=(jax.ShapeDtypeStruct(rows.shape,...  185 us
    all_to_all x10, blocking collectives, exchanged(): return lax.all_to_all(pieces, axis, 0, 0, axis_index_groups=groups)  130 us
  transfers between devices with their start and end apart: 3, of which 3 were waited for; matrix products, arithmetic and copies ran while one was open for 0% of the time, Pallas kernels for 1%

profile of v8, /device:TPU:6, one launch (start us, length us, event | category | flops | bytes accessed | tf_op | source)
XLA Modules:
  0.0 334.7 jit_solution(3122543227934484976)
XLA Ops:
  0.7 2.6 opening.1
  3.4 1.9 collective-permute-start
  5.3 1.1 half_product.3
  6.4 0.6 collective-permute-done
  7.1 14.8 %all_to_all.50 = bf16[4,192,256]{2,1,0:T(8,128)(2,1)S(1)} all-to-all(bf16[4,192,256]{2,1,0:T(8,128)(2,1)S(1)} %bitcast.16), channel_id=1, replica_groups=mesh['y_hi'=4,'y_lo'=2,'z'=8,'x'=4,'core'=2] {'x'}, dimensions={0} | all-to-all | bytes 786432 | tf_op jit(solution)/shard_map/all_to_all | solution.py:281
  22.0 10.2 %all_to_all.51 = bf16[4,192,256]{2,1,0:T(8,128)(2,1)S(1)} all-to-all(bf16[4,192,256]{2,1,0:T(8,128)(2,1)S(1)} %broadcast_in_dim.12), channel_id=1, replica_groups=mesh['y_hi'=4,'y_lo'=2,'z'=8,'x'=4,'core'=2] {'x'}, dimensions={0} | all-to-all | bytes 786432 | tf_op jit(solution)/shard_map/all_to_all | solution.py:281
  32.2 1.9 collective-permute-start.1
  34.1 1.2 half_back.2.refs_3_
  35.8 1.1 half_back.3
  37.0 18.3 %all_to_all.52 = bf16[8,32,896]{2,1,0:T(8,128)(2,1)S(1)} all-to-all(bf16[8,32,896]{2,1,0:T(8,128)(2,1)S(1)} %bitcast.11), channel_id=1, replica_groups={{0,8,16,24,32,40,48,56},{2,10,18,26,34,42,50,58},{4,12,20,28,36,44,52,6..., dimensions={0} | all-to-all | bytes 917504 | tf_op jit(solution)/shard_map/all_to_all | solution.py:281
  55.4 19.5 %all_to_all.53 = bf16[8,32,896]{2,1,0:T(8,128)(2,1)S(1)} all-to-all(bf16[8,32,896]{2,1,0:T(8,128)(2,1)S(1)} %broadcast_in_dim.13), channel_id=1, replica_groups={{0,64,128,192,256,320,384,448},{2,66,130,194,258,322,386,450},{4,68,132..., dimensions={0} | all-to-all | bytes 917504 | tf_op jit(solution)/shard_map/all_to_all | solution.py:281
  75.0 15.0 %all_to_all.54 = bf16[8,32,896]{2,1,0:T(8,128)(2,1)S(1)} all-to-all(bf16[8,32,896]{2,1,0:T(8,128)(2,1)S(1)} %broadcast_in_dim.14), channel_id=1, replica_groups={{0,8,16,24,32,40,48,56},{2,10,18,26,34,42,50,58},{4,12,20,28,36,44,52,6..., dimensions={0} | all-to-all | bytes 917504 | tf_op jit(solution)/shard_map/all_to_all | solution.py:281
  90.0 1.1 half_product.5
  91.2 1.9 collective-permute-start.2
  93.1 1.2 half_product.4.kept_ref
  94.3 1.1 collective-permute-done.2.landed_ref
  95.3 0.6 sum_of_halves.1
  96.0 11.0 %all_to_all.55.refs_1_ = bf16[4,192,256]{2,1,0:T(8,128)(2,1)S(1)} all-to-all(bf16[4,192,256]{2,1,0:T(8,128)(2,1)S(1)} %get-tuple-element.12), channel_id=1, replica_groups=mesh['y_hi'=4,'y_lo'=2,'z'=8,'x'=4,'core'=2] {'x'}, dimensions={0} | all-to-all | bytes 786432 | tf_op jit(solution)/shard_map/all_to_all | solution.py:281
  107.0 1.1 rows_and_gram.1
  108.1 9.7 %all_to_all.56 = f32[16,24,128]{2,1,0:T(8,128)S(1)} all-to-all(f32[16,24,128]{2,1,0:T(8,128)S(1)} %bitcast.15), channel_id=1, replica_groups=mesh['y_hi'=4,'y_lo'=2,'z'=8,'x'=4,'core'=2] {'y_lo','x','core'}, dimensions={0} | all-to-all | bytes 393216 | tf_op jit(solution)/shard_map/all_to_all | solution.py:281
  117.9 11.5 %all_to_all.57 = f32[8,24,128]{2,1,0:T(8,128)S(1)} all-to-all(f32[8,24,128]{2,1,0:T(8,128)S(1)} %broadcast_in_dim.15), channel_id=1, replica_groups=mesh['y_hi'=4,'y_lo'=2,'z'=8,'x'=4,'core'=2] {'z'}, dimensions={0} | all-to-all | bytes 196608 | tf_op jit(solution)/shard_map/all_to_all | solution.py:281
  129.4 10.4 %all_to_all.58 = f32[4,24,128]{2,1,0:T(8,128)S(1)} all-to-all(f32[4,24,128]{2,1,0:T(8,128)S(1)} %broadcast_in_dim.16), channel_id=1, replica_groups=mesh['y_hi'=4,'y_lo'=2,'z'=8,'x'=4,'core'=2] {'y_hi'}, dimensions={0} | all-to-all | bytes 98304 | tf_op jit(solution)/shard_map/all_to_all | solution.py:281
  139.8 9.6 %all_to_all.59 = f32[16,24,128]{2,1,0:T(8,128)S(1)} all-to-all(f32[16,24,128]{2,1,0:T(8,128)S(1)} %broadcast_in_dim.17), channel_id=1, replica_groups=mesh['y_hi'=4,'y_lo'=2,'z'=8,'x'=4,'core'=2] {'y_lo','x','core'}, dimensions={0} | all-to-all | bytes 393216 | tf_op jit(solution)/shard_map/all_to_all | solution.py:281
  149.5 185.2 %factor.1 = (f32[192,256]{1,0:T(8,128)}, f32[256,256]{1,0:T(8,128)}) custom-call(f32[384,128]{1,0:T(8,128)S(1)} %bitcast.14, f32[192,256]{1,0:T(8,128)S(1)} %get-tuple-element.15.rows_ref), custom_call_target="tpu_custom_call" | custom-call | tf_op jit(solution)/shard_map/factor/pallas_call | solution.py:108
  (17 shorter events, 1.1 us)
Async XLA Ops:
  3.4 3.6 %collective-permute-start = (bf16[768,256]{1,0:T(8,128)(2,1)S(1)}, bf16[768,256]{1,0:T(8,128)(2,1)S(1)}, u32[]{:S(2)}, u32[]{:S(2)}) collective-permute-start(bf16[768,256]{1,0:T(8,128)(2,1)S(1)} %get-tuple-element.11), channel_id=1, source_target_pairs={{0,1},{1,0},{2,3},{3,2},{4,5},{5,4},{6,7},{7,6},{8,9},{9,8},{10,11... | collective-permute-start | bytes 1179656 | tf_op jit(solution)/shard_map/ppermute | solution.py:258
  32.2 3.6 %collective-permute-start.1 = (bf16[768,256]{1,0:T(8,128)(2,1)S(1)}, bf16[768,256]{1,0:T(8,128)(2,1)S(1)}, u32[]{:S(2)}, u32[]{:S(2)}) collective-permute-start(bf16[768,256]{1,0:T(8,128)(2,1)S(1)} %bitcast.12), channel_id=1, source_target_pairs={{0,1},{1,0},{2,3},{3,2},{4,5},{5,4},{6,7},{7,6},{8,9},{9,8},{10,11... | collective-permute-start | bytes 1179656 | tf_op jit(solution)/shard_map/ppermute | solution.py:258
  91.2 4.2 %collective-permute-start.2 = (f32[768,256]{1,0:T(8,128)S(1)}, f32[768,256]{1,0:T(8,128)S(1)}, u32[]{:S(2)}, u32[]{:S(2)}) collective-permute-start(f32[768,256]{1,0:T(8,128)S(1)} %half_product.5), channel_id=1, source_target_pairs={{0,1},{1,0},{2,3},{3,2},{4,5},{5,4},{6,7},{7,6},{8,9},{9,8},{10,11... | collective-permute-start | bytes 2359304 | tf_op jit(solution)/shard_map/ppermute | solution.py:258

commit v9 on v8

--- a/solution.py
+++ b/solution.py
@@ -120,9 +120,9 @@
 PARAMS = pltpu.CompilerParams(vmem_limit_bytes=12 * 1024 * 1024)
 
 
-def opening_kernel(place_ref, hidden_ref, right_ref, send_ref, hidden_out, right_out, sems):
+def opening_kernel(half_ref, x_ref, hidden_ref, right_ref, send_ref, hidden_out, right_out, sems):
     rows = send_ref.shape[0]
-    halves = [pl.ds(pl.multiple_of(half * rows, rows), rows) for half in (place_ref[OTHER], place_ref[MINE])]
+    halves = [pl.ds(pl.multiple_of(half * rows, rows), rows) for half in (half_ref[0], 1 - half_ref[0])]
     copies = [
         pltpu.make_async_copy(right_ref, right_out, sems.at[0]),
         pltpu.make_async_copy(hidden_ref.at[halves[0], :], hidden_out.at[halves[0], :], sems.at[1]),
@@ -136,7 +136,7 @@
     copies[2].wait()
 
 
-def opening(place, hidden, right):
+def opening(half, x, hidden, right):
     return pl.pallas_call(
         opening_kernel,
         out_shape=(
@@ -144,71 +144,70 @@
             pltpu.VMEM(hidden.shape, hidden.dtype),
             pltpu.VMEM(right.shape, right.dtype),
         ),
-        in_specs=[SCALAR, *[pl.BlockSpec(memory_space=pltpu.HBM)] * 2],
+        in_specs=[SCALAR, SCALAR, *[pl.BlockSpec(memory_space=pltpu.HBM)] * 2],
         out_specs=(WHOLE, WHOLE, WHOLE),
         scratch_shapes=[pltpu.SemaphoreType.DMA((3,))],
         compiler_params=pltpu.CompilerParams(vmem_limit_bytes=12 * 1024 * 1024),
         name="opening",
-    )(place, pltpu.with_memory_space_constraint(hidden, pltpu.HBM), pltpu.with_memory_space_constraint(right, pltpu.HBM))
+    )(half, x, pltpu.with_memory_space_constraint(hidden, pltpu.HBM), pltpu.with_memory_space_constraint(right, pltpu.HBM))
 
 
 SCALAR = pl.BlockSpec(memory_space=pltpu.SMEM)
-OTHER, MINE, X = range(3)
-
-
-def half_kernel(half, place_ref, hidden_ref, right_ref, out_ref):
+
+
+def half_kernel(half_ref, hidden_ref, right_ref, out_ref):
     rows = out_ref.shape[0]
-    out_ref[...] = dot(hidden_ref[pl.ds(pl.multiple_of(place_ref[half] * rows, rows), rows), :], right_ref[...])
-
-
-def striped_kernel(half, place_ref, hidden_ref, back_ref, out_ref):
+    out_ref[...] = dot(hidden_ref[pl.ds(pl.multiple_of(half_ref[0] * rows, rows), rows), :], right_ref[...])
+
+
+def striped_kernel(half_ref, hidden_ref, back_ref, out_ref):
     rows = out_ref.shape[0]
     tile = rows // 4
-    blocks = [hidden_ref[pl.ds(pl.multiple_of((2 * i + place_ref[half]) * tile, tile), tile), :] for i in range(4)]
+    blocks = [hidden_ref[pl.ds(pl.multiple_of((2 * i + half_ref[0]) * tile, tile), tile), :] for i in range(4)]
     out_ref[...] = dot(jnp.concatenate(blocks, axis=0), back_ref[...], 1, 1)
 
 
-def half_product(kernel, half, place, hidden, right):
-    return pl.pallas_call(
-        lambda *refs: kernel(half, *refs),
+def half_product(kernel, half, hidden, right):
+    return pl.pallas_call(
+        kernel,
         out_shape=pltpu.VMEM((hidden.shape[0] // 2, K), jnp.float32),
         in_specs=[SCALAR, WHOLE, WHOLE],
         out_specs=WHOLE,
         compiler_params=PARAMS,
         name="half_product",
-    )(place, hidden, right)
-
-
-def back_kernel(half, place_ref, hidden_ref, first_ref, *refs):
+    )(half, hidden, right)
+
+
+def back_kernel(half_ref, hidden_ref, first_ref, *refs):
     *so_far, out_ref = refs
     rows = first_ref.shape[0]
-    part = dot(first_ref[...], hidden_ref[pl.ds(pl.multiple_of(place_ref[half] * rows, rows), rows), :], 0, 0)
+    part = dot(first_ref[...], hidden_ref[pl.ds(pl.multiple_of(half_ref[0] * rows, rows), rows), :], 0, 0)
     for ref in so_far:
         part = part + ref[...]
     out_ref[...] = part.astype(out_ref.dtype)
 
 
-def half_back(half, place, hidden, first, dtype, *so_far):
-    return pl.pallas_call(
-        lambda *refs: back_kernel(half, *refs),
+def half_back(half, hidden, first, dtype, *so_far):
+    return pl.pallas_call(
+        back_kernel,
         out_shape=jax.ShapeDtypeStruct((K, hidden.shape[1]), dtype),
         in_specs=[SCALAR, *[WHOLE] * (2 + len(so_far))],
         out_specs=WHOLE,
         compiler_params=PARAMS,
         name="half_back",
-    )(place, hidden, first, *so_far)
-
-
-def sum_kernel(place_ref, kept_ref, landed_ref, own_ref, pieces_ref):
+    )(half, hidden, first, *so_far)
+
+
+def sum_kernel(x_ref, kept_ref, landed_ref, own_ref, pieces_ref):
     count, tile, _ = pieces_ref.shape
-    own = pl.ds(pl.multiple_of(place_ref[X] * tile, tile), tile)
+    own = pl.ds(pl.multiple_of(x_ref[0] * tile, tile), tile)
     own_ref[...] = kept_ref[own, :] + landed_ref[own, :]
     for i in range(count):
         block = slice(i * tile, (i + 1) * tile)
         pieces_ref[i] = (kept_ref[block, :] + landed_ref[block, :]).astype(pieces_ref.dtype)
 
 
-def sum_of_halves(place, kept, landed, count):
+def sum_of_halves(x, kept, landed, count):
     tile = kept.shape[0] // count
     return pl.pallas_call(
         sum_kernel,
@@ -220,13 +219,13 @@
         out_specs=(WHOLE, WHOLE),
         compiler_params=PARAMS,
         name="sum_of_halves",
-    )(place, kept, pltpu.with_memory_space_constraint(landed, pltpu.VMEM))
-
-
-def gram_kernel(scale, place_ref, landed_ref, own_ref, rows_ref, packed_ref):
+    )(x, kept, pltpu.with_memory_space_constraint(landed, pltpu.VMEM))
+
+
+def gram_kernel(scale, x_ref, landed_ref, own_ref, rows_ref, packed_ref):
     rows = own_ref[...]
     for i in range(landed_ref.shape[0]):
-        rows = rows + jnp.where(place_ref[X] == i, 0.0, landed_ref[i].astype(jnp.float32))
+        rows = rows + jnp.where(x_ref[0] == i, 0.0, landed_ref[i].astype(jnp.float32))
     rows_ref[...] = rows
     left, right = rows[:, :HALF], rows[:, HALF:]
     packed_ref[:HALF, :] = dot(left, left, 0, 0, HIGH) * scale
@@ -234,7 +233,7 @@
     packed_ref[2 * HALF :, :] = dot(right, right, 0, 0, HIGH) * scale
 
 
-def rows_and_gram(place, landed, own, scale):
+def rows_and_gram(x, landed, own, scale):
     return pl.pallas_call(
         lambda *refs: gram_kernel(scale, *refs),
         out_shape=(
@@ -245,7 +244,7 @@
         out_specs=(WHOLE, WHOLE),
         compiler_params=PARAMS,
         name="rows_and_gram",
-    )(place, landed, own)
+    )(x, landed, own)
 
 
 ROW = ("y_hi", "y_lo", "z")
@@ -296,16 +295,16 @@
     ys, zs, xs = sizes
     total_rows = tok_rows * ys * zs
     core = lax.axis_index("core")
-    place = jnp.stack([1 - core, core, lax.axis_index("x")])
-
-    send, hidden, test_matrix = opening(place, hidden, test_matrix)
+    mine, other, x = core.reshape(1), (1 - core).reshape(1), lax.axis_index("x").reshape(1)
+
+    send, hidden, test_matrix = opening(other, x, hidden, test_matrix)
     landed = swapped(send)
-    pieces = (half_product(half_kernel, MINE, place, hidden, test_matrix) + landed).astype(bf16).reshape(xs, tile, K)
+    pieces = (half_product(half_kernel, mine, hidden, test_matrix) + landed).astype(bf16).reshape(xs, tile, K)
     my_first = (total(exchanged(pieces, "x")) * (1.0 / math.sqrt(D))).astype(bf16)
     my_half = exchanged(spread(my_first, xs), "x").reshape(tok_rows // 2, K)
     other_half = swapped(my_half)
-    local_back = half_back(MINE, place, hidden, my_half, jnp.float32)
-    local_back = half_back(OTHER, place, hidden, other_half, bf16, local_back)
+    local_back = half_back(mine, hidden, my_half, jnp.float32)
+    local_back = half_back(other, hidden, other_half, bf16, local_back)
 
     lines = ((), ((1, zs),)), (((1, ys),), ())
     this_way, that_way = line_groups(sizes, lines), line_groups(sizes, lines[::-1])
@@ -316,10 +315,10 @@
     my_back = (my_back * (1.0 / total_rows)).astype(bf16)
     back = exchanged(spread(my_back, count), ALL, this_way).reshape(K, width)
 
-    landed = swapped(half_product(striped_kernel, OTHER, place, hidden, back))
-    kept = half_product(striped_kernel, MINE, place, hidden, back)
-    own, pieces = sum_of_halves(place, kept, landed, xs)
-    my_rows, gram = rows_and_gram(place, exchanged(pieces, "x"), own, 1.0 / total_rows)
+    landed = swapped(half_product(striped_kernel, other, hidden, back))
+    kept = half_product(striped_kernel, mine, hidden, back)
+    own, pieces = sum_of_halves(x, kept, landed, xs)
+    my_rows, gram = rows_and_gram(x, exchanged(pieces, "x"), own, 1.0 / total_rows)
     count = 4 * xs
     gram = total(exchanged(gram.reshape(count, 3 * HALF // count, HALF), NEAR))
     gram = total(exchanged(spread(gram, zs), "z"))

time: 338 us -> 335 us (level)
  Pallas kernels: 195 us -> 191 us
where the time goes in v9:
time: 335 us; the launch traced here: 332 us
  Pallas kernels  191 us (57%)
  blocking collectives  130 us (39%)
  starting transfers between devices  5.75 us (2%)
  waiting for transfers between devices  3.81 us (1%)
    pallas_call x1, Pallas kernels, factor_call(): pl.pallas_call(factor_kernel, out_shape=(jax.ShapeDtypeStruct(rows.shape,...  185 us
    all_to_all x10, blocking collectives, exchanged(): return lax.all_to_all(pieces, axis, 0, 0, axis_index_groups=groups)  130 us
  transfers between devices with their start and end apart: 3, of which 3 were waited for; matrix products, arithmetic and copies ran while one was open for 0% of the time, Pallas kernels for 1%

profile of v9, /device:TPU:6, one launch (start us, length us, event | category | flops | bytes accessed | tf_op | source)
XLA Modules:
  0.0 331.9 jit_solution(3638028210746293684)
XLA Ops:
  0.6 2.1 opening.1
  2.7 1.9 collective-permute-start
  4.7 0.6 half_product.3
  5.2 1.1 collective-permute-done
  6.5 14.8 %all_to_all.50 = bf16[4,192,256]{2,1,0:T(8,128)(2,1)S(1)} all-to-all(bf16[4,192,256]{2,1,0:T(8,128)(2,1)S(1)} %bitcast.16), channel_id=1, replica_groups=mesh['y_hi'=4,'y_lo'=2,'z'=8,'x'=4,'core'=2] {'x'}, dimensions={0} | all-to-all | bytes 786432 | tf_op jit(solution)/shard_map/all_to_all | solution.py:280
  21.4 10.2 %all_to_all.51 = bf16[4,192,256]{2,1,0:T(8,128)(2,1)S(1)} all-to-all(bf16[4,192,256]{2,1,0:T(8,128)(2,1)S(1)} %broadcast_in_dim.12), channel_id=1, replica_groups=mesh['y_hi'=4,'y_lo'=2,'z'=8,'x'=4,'core'=2] {'x'}, dimensions={0} | all-to-all | bytes 786432 | tf_op jit(solution)/shard_map/all_to_all | solution.py:280
  31.6 1.9 collective-permute-start.1
  33.5 0.6 half_back.2.refs_0_
  34.2 1.1 collective-permute-done.1.first_ref
  35.2 0.6 half_back.3
  35.9 18.3 %all_to_all.52 = bf16[8,32,896]{2,1,0:T(8,128)(2,1)S(1)} all-to-all(bf16[8,32,896]{2,1,0:T(8,128)(2,1)S(1)} %bitcast.11), channel_id=1, replica_groups={{0,8,16,24,32,40,48,56},{2,10,18,26,34,42,50,58},{4,12,20,28,36,44,52,6..., dimensions={0} | all-to-all | bytes 917504 | tf_op jit(solution)/shard_map/all_to_all | solution.py:280
  54.3 19.5 %all_to_all.53 = bf16[8,32,896]{2,1,0:T(8,128)(2,1)S(1)} all-to-all(bf16[8,32,896]{2,1,0:T(8,128)(2,1)S(1)} %broadcast_in_dim.13), channel_id=1, replica_groups={{0,64,128,192,256,320,384,448},{2,66,130,194,258,322,386,450},{4,68,132..., dimensions={0} | all-to-all | bytes 917504 | tf_op jit(solution)/shard_map/all_to_all | solution.py:280
  73.9 15.0 %all_to_all.54 = bf16[8,32,896]{2,1,0:T(8,128)(2,1)S(1)} all-to-all(bf16[8,32,896]{2,1,0:T(8,128)(2,1)S(1)} %broadcast_in_dim.14), channel_id=1, replica_groups={{0,8,16,24,32,40,48,56},{2,10,18,26,34,42,50,58},{4,12,20,28,36,44,52,6..., dimensions={0} | all-to-all | bytes 917504 | tf_op jit(solution)/shard_map/all_to_all | solution.py:280
  88.9 0.6 half_product.5
  89.5 1.9 collective-permute-start.2
  91.4 0.6 half_product.4.kept_ref
  92.0 1.6 collective-permute-done.2.landed_ref
  93.8 11.0 %all_to_all.55.refs_1_ = bf16[4,192,256]{2,1,0:T(8,128)(2,1)S(1)} all-to-all(bf16[4,192,256]{2,1,0:T(8,128)(2,1)S(1)} %get-tuple-element.12), channel_id=1, replica_groups=mesh['y_hi'=4,'y_lo'=2,'z'=8,'x'=4,'core'=2] {'x'}, dimensions={0} | all-to-all | bytes 786432 | tf_op jit(solution)/shard_map/all_to_all | solution.py:280
  104.8 0.5 rows_and_gram.1
  105.3 9.7 %all_to_all.56 = f32[16,24,128]{2,1,0:T(8,128)S(1)} all-to-all(f32[16,24,128]{2,1,0:T(8,128)S(1)} %bitcast.15), channel_id=1, replica_groups=mesh['y_hi'=4,'y_lo'=2,'z'=8,'x'=4,'core'=2] {'y_lo','x','core'}, dimensions={0} | all-to-all | bytes 393216 | tf_op jit(solution)/shard_map/all_to_all | solution.py:280
  115.1 11.5 %all_to_all.57 = f32[8,24,128]{2,1,0:T(8,128)S(1)} all-to-all(f32[8,24,128]{2,1,0:T(8,128)S(1)} %broadcast_in_dim.15), channel_id=1, replica_groups=mesh['y_hi'=4,'y_lo'=2,'z'=8,'x'=4,'core'=2] {'z'}, dimensions={0} | all-to-all | bytes 196608 | tf_op jit(solution)/shard_map/all_to_all | solution.py:280
  126.6 10.4 %all_to_all.58 = f32[4,24,128]{2,1,0:T(8,128)S(1)} all-to-all(f32[4,24,128]{2,1,0:T(8,128)S(1)} %broadcast_in_dim.16), channel_id=1, replica_groups=mesh['y_hi'=4,'y_lo'=2,'z'=8,'x'=4,'core'=2] {'y_hi'}, dimensions={0} | all-to-all | bytes 98304 | tf_op jit(solution)/shard_map/all_to_all | solution.py:280
  137.1 9.6 %all_to_all.59 = f32[16,24,128]{2,1,0:T(8,128)S(1)} all-to-all(f32[16,24,128]{2,1,0:T(8,128)S(1)} %broadcast_in_dim.17), channel_id=1, replica_groups=mesh['y_hi'=4,'y_lo'=2,'z'=8,'x'=4,'core'=2] {'y_lo','x','core'}, dimensions={0} | all-to-all | bytes 393216 | tf_op jit(solution)/shard_map/all_to_all | solution.py:280
  146.7 185.2 %factor.1 = (f32[192,256]{1,0:T(8,128)}, f32[256,256]{1,0:T(8,128)}) custom-call(f32[384,128]{1,0:T(8,128)S(1)} %bitcast.14, f32[192,256]{1,0:T(8,128)S(1)} %get-tuple-element.15.rows_ref), custom_call_target="tpu_custom_call" | custom-call | tf_op jit(solution)/shard_map/factor/pallas_call | solution.py:108
  (16 shorter events, 0.6 us)
Async XLA Ops:
  2.7 3.6 %collective-permute-start = (bf16[768,256]{1,0:T(8,128)(2,1)S(1)}, bf16[768,256]{1,0:T(8,128)(2,1)S(1)}, u32[]{:S(2)}, u32[]{:S(2)}) collective-permute-start(bf16[768,256]{1,0:T(8,128)(2,1)S(1)} %get-tuple-element.11), channel_id=1, source_target_pairs={{0,1},{1,0},{2,3},{3,2},{4,5},{5,4},{6,7},{7,6},{8,9},{9,8},{10,11... | collective-permute-start | bytes 1179656 | tf_op jit(solution)/shard_map/ppermute | solution.py:257
  31.6 3.6 %collective-permute-start.1 = (bf16[768,256]{1,0:T(8,128)(2,1)S(1)}, bf16[768,256]{1,0:T(8,128)(2,1)S(1)}, u32[]{:S(2)}, u32[]{:S(2)}) collective-permute-start(bf16[768,256]{1,0:T(8,128)(2,1)S(1)} %bitcast.12), channel_id=1, source_target_pairs={{0,1},{1,0},{2,3},{3,2},{4,5},{5,4},{6,7},{7,6},{8,9},{9,8},{10,11... | collective-permute-start | bytes 1179656 | tf_op jit(solution)/shard_map/ppermute | solution.py:257
  89.5 4.2 %collective-permute-start.2 = (f32[768,256]{1,0:T(8,128)S(1)}, f32[768,256]{1,0:T(8,128)S(1)}, u32[]{:S(2)}, u32[]{:S(2)}) collective-permute-start(f32[768,256]{1,0:T(8,128)S(1)} %half_product.5), channel_id=1, source_target_pairs={{0,1},{1,0},{2,3},{3,2},{4,5},{5,4},{6,7},{7,6},{8,9},{9,8},{10,11... | collective-permute-start | bytes 2359304 | tf_op jit(solution)/shard_map/ppermute | solution.py:257

commit v10 on v9

--- a/solution.py
+++ b/solution.py
@@ -120,131 +120,143 @@
 PARAMS = pltpu.CompilerParams(vmem_limit_bytes=12 * 1024 * 1024)
 
 
-def opening_kernel(half_ref, x_ref, hidden_ref, right_ref, send_ref, hidden_out, right_out, sems):
-    rows = send_ref.shape[0]
-    halves = [pl.ds(pl.multiple_of(half * rows, rows), rows) for half in (half_ref[0], 1 - half_ref[0])]
-    copies = [
-        pltpu.make_async_copy(right_ref, right_out, sems.at[0]),
-        pltpu.make_async_copy(hidden_ref.at[halves[0], :], hidden_out.at[halves[0], :], sems.at[1]),
-        pltpu.make_async_copy(hidden_ref.at[halves[1], :], hidden_out.at[halves[1], :], sems.at[2]),
-    ]
+SCALAR = pl.BlockSpec(memory_space=pltpu.SMEM)
+STEPS = 8
+
+
+def opening_kernel(core_ref, me_ref, hidden_ref, right_ref, send_ref, keep_ref, hidden_out, right_buf, sems):
+    rows = hidden_out.shape[0] // STEPS
+    blocks = [slice(i * rows, (i + 1) * rows) for i in range(STEPS)]
+    copies = [pltpu.make_async_copy(right_ref, right_buf, sems.at[STEPS])]
+    for i, block in enumerate(blocks):
+        copies.append(pltpu.make_async_copy(hidden_ref.at[block, :], hidden_out.at[block, :], sems.at[i]))
     for copy in copies:
         copy.start()
-    copies[0].wait()
-    copies[1].wait()
-    send_ref[...] = dot(hidden_out[halves[0], :], right_out[...]).astype(send_ref.dtype)
-    copies[2].wait()
-
-
-def opening(half, x, hidden, right):
+    for copy in copies:
+        copy.wait()
+    first = dot(hidden_out[...], right_buf[...])
+    left, right = first[:, :HALF], first[:, HALF:]
+    send_ref[...] = jnp.where(core_ref[0] == 0, right, left).astype(send_ref.dtype)
+    keep_ref[...] = jnp.where(core_ref[0] == 0, left, right)
+
+
+def opening(core, me, hidden, right):
+    rows = hidden.shape[0]
+    in_hbm = pl.BlockSpec(memory_space=pltpu.HBM)
     return pl.pallas_call(
         opening_kernel,
         out_shape=(
-            pltpu.VMEM((hidden.shape[0] // 2, K), jnp.bfloat16),
-            pltpu.VMEM(hidden.shape, hidden.dtype),
-            pltpu.VMEM(right.shape, right.dtype),
+            jax.ShapeDtypeStruct((rows, HALF), jnp.bfloat16),
+            jax.ShapeDtypeStruct((rows, HALF), jnp.float32),
+            jax.ShapeDtypeStruct(hidden.shape, hidden.dtype),
         ),
-        in_specs=[SCALAR, SCALAR, *[pl.BlockSpec(memory_space=pltpu.HBM)] * 2],
+        in_specs=[SCALAR, SCALAR, in_hbm, in_hbm],
         out_specs=(WHOLE, WHOLE, WHOLE),
-        scratch_shapes=[pltpu.SemaphoreType.DMA((3,))],
-        compiler_params=pltpu.CompilerParams(vmem_limit_bytes=12 * 1024 * 1024),
+        scratch_shapes=[pltpu.VMEM(right.shape, right.dtype), pltpu.SemaphoreType.DMA((STEPS + 1,))],
+        compiler_params=PARAMS,
         name="opening",
-    )(half, x, pltpu.with_memory_space_constraint(hidden, pltpu.HBM), pltpu.with_memory_space_constraint(right, pltpu.HBM))
-
-
-SCALAR = pl.BlockSpec(memory_space=pltpu.SMEM)
-
-
-def half_kernel(half_ref, hidden_ref, right_ref, out_ref):
-    rows = out_ref.shape[0]
-    out_ref[...] = dot(hidden_ref[pl.ds(pl.multiple_of(half_ref[0] * rows, rows), rows), :], right_ref[...])
-
-
-def striped_kernel(half_ref, hidden_ref, back_ref, out_ref):
-    rows = out_ref.shape[0]
-    tile = rows // 4
-    blocks = [hidden_ref[pl.ds(pl.multiple_of((2 * i + half_ref[0]) * tile, tile), tile), :] for i in range(4)]
-    out_ref[...] = dot(jnp.concatenate(blocks, axis=0), back_ref[...], 1, 1)
-
-
-def half_product(kernel, half, hidden, right):
-    return pl.pallas_call(
-        kernel,
-        out_shape=pltpu.VMEM((hidden.shape[0] // 2, K), jnp.float32),
-        in_specs=[SCALAR, WHOLE, WHOLE],
-        out_specs=WHOLE,
-        compiler_params=PARAMS,
-        name="half_product",
-    )(half, hidden, right)
-
-
-def back_kernel(half_ref, hidden_ref, first_ref, *refs):
-    *so_far, out_ref = refs
-    rows = first_ref.shape[0]
-    part = dot(first_ref[...], hidden_ref[pl.ds(pl.multiple_of(half_ref[0] * rows, rows), rows), :], 0, 0)
-    for ref in so_far:
-        part = part + ref[...]
-    out_ref[...] = part.astype(out_ref.dtype)
-
-
-def half_back(half, hidden, first, dtype, *so_far):
-    return pl.pallas_call(
-        back_kernel,
-        out_shape=jax.ShapeDtypeStruct((K, hidden.shape[1]), dtype),
-        in_specs=[SCALAR, *[WHOLE] * (2 + len(so_far))],
-        out_specs=WHOLE,
-        compiler_params=PARAMS,
-        name="half_back",
-    )(half, hidden, first, *so_far)
-
-
-def sum_kernel(x_ref, kept_ref, landed_ref, own_ref, pieces_ref):
+    )(
+        core,
+        me,
+        pltpu.with_memory_space_constraint(hidden, pltpu.HBM),
+        pltpu.with_memory_space_constraint(right, pltpu.HBM),
+    )
+
+
+def pieces_kernel(own_ref, landed_ref, hidden_ref, pieces_ref, _):
     count, tile, _ = pieces_ref.shape
-    own = pl.ds(pl.multiple_of(x_ref[0] * tile, tile), tile)
-    own_ref[...] = kept_ref[own, :] + landed_ref[own, :]
     for i in range(count):
         block = slice(i * tile, (i + 1) * tile)
-        pieces_ref[i] = (kept_ref[block, :] + landed_ref[block, :]).astype(pieces_ref.dtype)
-
-
-def sum_of_halves(x, kept, landed, count):
-    tile = kept.shape[0] // count
-    return pl.pallas_call(
-        sum_kernel,
+        pieces_ref[i] = (own_ref[block, :] + landed_ref[block, :].astype(jnp.float32)).astype(pieces_ref.dtype)
+
+
+def first_pieces(own, landed, hidden, count):
+    return pl.pallas_call(
+        pieces_kernel,
         out_shape=(
-            jax.ShapeDtypeStruct((tile, K), jnp.float32),
-            jax.ShapeDtypeStruct((count, tile, K), jnp.bfloat16),
+            jax.ShapeDtypeStruct((count, own.shape[0] // count, HALF), jnp.bfloat16),
+            jax.ShapeDtypeStruct(hidden.shape, hidden.dtype),
         ),
-        in_specs=[SCALAR, WHOLE, WHOLE],
+        in_specs=[WHOLE] * 3,
         out_specs=(WHOLE, WHOLE),
-        compiler_params=PARAMS,
-        name="sum_of_halves",
-    )(x, kept, pltpu.with_memory_space_constraint(landed, pltpu.VMEM))
-
-
-def gram_kernel(scale, x_ref, landed_ref, own_ref, rows_ref, packed_ref):
-    rows = own_ref[...]
-    for i in range(landed_ref.shape[0]):
-        rows = rows + jnp.where(x_ref[0] == i, 0.0, landed_ref[i].astype(jnp.float32))
-    rows_ref[...] = rows
-    left, right = rows[:, :HALF], rows[:, HALF:]
+        input_output_aliases={2: 1},
+        compiler_params=PARAMS,
+        name="first_pieces",
+    )(own, landed, hidden)
+
+
+def back_kernel(first_ref, own_ref, pair_ref, out_ref):
+    first = first_ref[...]
+    out_ref[:HALF, :] = dot(first, own_ref[...], 0, 0).astype(out_ref.dtype)
+    out_ref[HALF:, :] = dot(first, pair_ref[...], 0, 0).astype(out_ref.dtype)
+
+
+def local_backs(first, own, pair):
+    return pl.pallas_call(
+        back_kernel,
+        out_shape=jax.ShapeDtypeStruct((K, own.shape[1]), jnp.bfloat16),
+        in_specs=[WHOLE] * 3,
+        out_specs=WHOLE,
+        compiler_params=PARAMS,
+        name="local_backs",
+    )(first, own, pair)
+
+
+def sketch_kernel(me_ref, own_ref, pair_ref, back_ref, mine_ref, pieces_ref):
+    count, tile, _ = pieces_ref.shape
+    sketch = dot(own_ref[...], back_ref[:HALF, :], 1, 1) + dot(pair_ref[...], back_ref[HALF:, :], 1, 1)
+    for i in range(count):
+        block = sketch[i * tile : (i + 1) * tile, :]
+        pieces_ref[i] = block.astype(pieces_ref.dtype)
+
+        @pl.when(me_ref[0] == i)
+        def _():
+            mine_ref[...] = block
+
+
+def sketch_pieces(me, own, pair, back, count):
+    tile = own.shape[0] // count
+    return pl.pallas_call(
+        sketch_kernel,
+        out_shape=(
+            jax.ShapeDtypeStruct((tile, HALF), jnp.float32),
+            jax.ShapeDtypeStruct((count, tile, HALF), jnp.bfloat16),
+        ),
+        in_specs=[SCALAR, WHOLE, WHOLE, WHOLE],
+        out_specs=(WHOLE, WHOLE),
+        compiler_params=PARAMS,
+        name="sketch_pieces",
+    )(me, own, pair, back)
+
+
+def gram_kernel(scale, me_ref, landed_ref, own_ref, rows_ref, packed_ref):
+    halves = []
+    for half in range(2):
+        parts = [
+            jnp.where(me_ref[0] == i, own_ref[...], landed_ref[i].astype(jnp.float32))
+            for i in range(half, landed_ref.shape[0], 2)
+        ]
+        halves.append(sum(parts[1:], parts[0]))
+    left, right = halves
+    rows_ref[:, :HALF] = left
+    rows_ref[:, HALF:] = right
     packed_ref[:HALF, :] = dot(left, left, 0, 0, HIGH) * scale
     packed_ref[HALF : 2 * HALF, :] = dot(left, right, 0, 0, HIGH) * scale
     packed_ref[2 * HALF :, :] = dot(right, right, 0, 0, HIGH) * scale
 
 
-def rows_and_gram(x, landed, own, scale):
+def rows_and_gram(me, landed, own, scale):
     return pl.pallas_call(
         lambda *refs: gram_kernel(scale, *refs),
         out_shape=(
-            jax.ShapeDtypeStruct(landed.shape[1:], jnp.float32),
+            jax.ShapeDtypeStruct((own.shape[0], K), jnp.float32),
             jax.ShapeDtypeStruct((3 * HALF, HALF), jnp.float32),
         ),
         in_specs=[SCALAR, WHOLE, WHOLE],
         out_specs=(WHOLE, WHOLE),
         compiler_params=PARAMS,
         name="rows_and_gram",
-    )(x, landed, own)
+    )(me, landed, own)
 
 
 ROW = ("y_hi", "y_lo", "z")
@@ -291,20 +303,16 @@
 def body(sizes, hidden, test_matrix):
     bf16 = jnp.bfloat16
     tok_rows, width = hidden.shape
-    tile = tok_rows // 8
     ys, zs, xs = sizes
     total_rows = tok_rows * ys * zs
-    core = lax.axis_index("core")
-    mine, other, x = core.reshape(1), (1 - core).reshape(1), lax.axis_index("x").reshape(1)
-
-    send, hidden, test_matrix = opening(other, x, hidden, test_matrix)
-    landed = swapped(send)
-    pieces = (half_product(half_kernel, mine, hidden, test_matrix) + landed).astype(bf16).reshape(xs, tile, K)
-    my_first = (total(exchanged(pieces, "x")) * (1.0 / math.sqrt(D))).astype(bf16)
-    my_half = exchanged(spread(my_first, xs), "x").reshape(tok_rows // 2, K)
-    other_half = swapped(my_half)
-    local_back = half_back(mine, hidden, my_half, jnp.float32)
-    local_back = half_back(other, hidden, other_half, bf16, local_back)
+    core, me = (lax.axis_index(axis).reshape(1) for axis in ("core", COL))
+
+    send, keep, hidden = opening(core, me, hidden, test_matrix)
+    pieces, hidden = first_pieces(keep, swapped(send), hidden, xs)
+    pair = swapped(hidden)
+    first = (total(exchanged(pieces, "x")) * (1.0 / math.sqrt(D))).astype(bf16)
+    first = exchanged(spread(first, xs), "x").reshape(tok_rows, HALF)
+    local_back = local_backs(first, hidden, pair)
 
     lines = ((), ((1, zs),)), (((1, ys),), ())
     this_way, that_way = line_groups(sizes, lines), line_groups(sizes, lines[::-1])
@@ -315,10 +323,8 @@
     my_back = (my_back * (1.0 / total_rows)).astype(bf16)
     back = exchanged(spread(my_back, count), ALL, this_way).reshape(K, width)
 
-    landed = swapped(half_product(striped_kernel, other, hidden, back))
-    kept = half_product(striped_kernel, mine, hidden, back)
-    own, pieces = sum_of_halves(x, kept, landed, xs)
-    my_rows, gram = rows_and_gram(x, exchanged(pieces, "x"), own, 1.0 / total_rows)
+    own, pieces = sketch_pieces(me, hidden, pair, back, 2 * xs)
+    my_rows, gram = rows_and_gram(me, exchanged(pieces, COL), own, 1.0 / total_rows)
     count = 4 * xs
     gram = total(exchanged(gram.reshape(count, 3 * HALF // count, HALF), NEAR))
     gram = total(exchanged(spread(gram, zs), "z"))

time: 335 us -> 333 us (level)
  transfers between devices with their start and end apart: 3 -> 2, of which waited for: 3 -> 1; matrix products, arithmetic and copies ran while one was open for 0% -> 0% of each run, Pallas kernels for 1% -> 0%
where the time goes in v10:
time: 333 us; the launch traced here: 330 us
  Pallas kernels  191 us (57%)
  blocking collectives  131 us (39%)
  starting transfers between devices  3.97 us (1%)
    pallas_call x1, Pallas kernels, factor_call(): pl.pallas_call(factor_kernel, out_shape=(jax.ShapeDtypeStruct(rows.shape,...  185 us
    all_to_all x10, blocking collectives, exchanged(): return lax.all_to_all(pieces, axis, 0, 0, axis_index_groups=groups)  131 us
  transfers between devices with their start and end apart: 2, of which 1 were waited for; matrix products, arithmetic and copies ran while one was open for 0% of the time, Pallas kernels for 0%

profile of v10, /device:TPU:6, one launch (start us, length us, event | category | flops | bytes accessed | tf_op | source)
XLA Modules:
  0.0 329.9 jit_solution(14245841227927649949)
XLA Ops:
  0.6 2.9 opening.1
  3.5 1.9 collective-permute-start
  5.5 1.7 collective-permute-done.landed_ref
  7.2 0.1 first_pieces.1
  7.2 2.0 collective-permute-start.1
  9.3 15.1 %all_to_all.50 = bf16[4,384,128]{2,1,0:T(8,128)(2,1)S(1)} all-to-all(bf16[4,384,128]{2,1,0:T(8,128)(2,1)S(1)} %get-tuple-element.15), channel_id=1, replica_groups=mesh['y_hi'=4,'y_lo'=2,'z'=8,'x'=4,'core'=2] {'x'}, dimensions={0} | all-to-all | bytes 786432 | tf_op jit(solution)/shard_map/all_to_all | solution.py:292
  24.4 0.1 broadcast_in_dim.12
  24.5 10.2 %all_to_all.51 = bf16[4,384,128]{2,1,0:T(8,128)(2,1)S(1)} all-to-all(bf16[4,384,128]{2,1,0:T(8,128)(2,1)S(1)} %broadcast_in_dim.12), channel_id=1, replica_groups=mesh['y_hi'=4,'y_lo'=2,'z'=8,'x'=4,'core'=2] {'x'}, dimensions={0} | all-to-all | bytes 786432 | tf_op jit(solution)/shard_map/all_to_all | solution.py:292
  34.7 0.0 collective-permute-done.1.pair_ref
  34.7 1.0 local_backs.1
  35.7 0.5 copy-done
  36.2 18.7 %all_to_all.52 = bf16[8,32,896]{2,1,0:T(8,128)(2,1)S(1)} all-to-all(bf16[8,32,896]{2,1,0:T(8,128)(2,1)S(1)} %bitcast.8), channel_id=1, replica_groups={{0,8,16,24,32,40,48,56},{2,10,18,26,34,42,50,58},{4,12,20,28,36,44,52,6..., dimensions={0} | all-to-all | bytes 917504 | tf_op jit(solution)/shard_map/all_to_all | solution.py:292
  54.9 0.1 reduce_sum.58
  55.1 19.6 %all_to_all.53 = bf16[8,32,896]{2,1,0:T(8,128)(2,1)S(1)} all-to-all(bf16[8,32,896]{2,1,0:T(8,128)(2,1)S(1)} %broadcast_in_dim.13), channel_id=1, replica_groups={{0,64,128,192,256,320,384,448},{2,66,130,194,258,322,386,450},{4,68,132..., dimensions={0} | all-to-all | bytes 917504 | tf_op jit(solution)/shard_map/all_to_all | solution.py:292
  74.7 0.1 convert_reduce_fusion
  74.8 15.0 %all_to_all.54 = bf16[8,32,896]{2,1,0:T(8,128)(2,1)S(1)} all-to-all(bf16[8,32,896]{2,1,0:T(8,128)(2,1)S(1)} %broadcast_in_dim.14), channel_id=1, replica_groups={{0,8,16,24,32,40,48,56},{2,10,18,26,34,42,50,58},{4,12,20,28,36,44,52,6..., dimensions={0} | all-to-all | bytes 917504 | tf_op jit(solution)/shard_map/all_to_all | solution.py:292
  89.8 1.7 sketch_pieces.1
  91.5 11.3 %all_to_all.55.refs_1_ = bf16[8,192,128]{2,1,0:T(8,128)(2,1)S(1)} all-to-all(bf16[8,192,128]{2,1,0:T(8,128)(2,1)S(1)} %get-tuple-element.16), channel_id=1, replica_groups=mesh['y_hi'=4,'y_lo'=2,'z'=8,'x'=4,'core'=2] {'x','core'}, dimensions={0} | all-to-all | bytes 786432 | tf_op jit(solution)/shard_map/all_to_all | solution.py:292
  102.8 0.5 rows_and_gram.1
  103.3 9.7 %all_to_all.56 = f32[16,24,128]{2,1,0:T(8,128)S(1)} all-to-all(f32[16,24,128]{2,1,0:T(8,128)S(1)} %bitcast.11), channel_id=1, replica_groups=mesh['y_hi'=4,'y_lo'=2,'z'=8,'x'=4,'core'=2] {'y_lo','x','core'}, dimensions={0} | all-to-all | bytes 393216 | tf_op jit(solution)/shard_map/all_to_all | solution.py:292
  113.1 11.5 %all_to_all.57 = f32[8,24,128]{2,1,0:T(8,128)S(1)} all-to-all(f32[8,24,128]{2,1,0:T(8,128)S(1)} %broadcast_in_dim.15), channel_id=1, replica_groups=mesh['y_hi'=4,'y_lo'=2,'z'=8,'x'=4,'core'=2] {'z'}, dimensions={0} | all-to-all | bytes 196608 | tf_op jit(solution)/shard_map/all_to_all | solution.py:292
  124.6 10.4 %all_to_all.58 = f32[4,24,128]{2,1,0:T(8,128)S(1)} all-to-all(f32[4,24,128]{2,1,0:T(8,128)S(1)} %broadcast_in_dim.16), channel_id=1, replica_groups=mesh['y_hi'=4,'y_lo'=2,'z'=8,'x'=4,'core'=2] {'y_hi'}, dimensions={0} | all-to-all | bytes 98304 | tf_op jit(solution)/shard_map/all_to_all | solution.py:292
  135.1 9.6 %all_to_all.59 = f32[16,24,128]{2,1,0:T(8,128)S(1)} all-to-all(f32[16,24,128]{2,1,0:T(8,128)S(1)} %broadcast_in_dim.17), channel_id=1, replica_groups=mesh['y_hi'=4,'y_lo'=2,'z'=8,'x'=4,'core'=2] {'y_lo','x','core'}, dimensions={0} | all-to-all | bytes 393216 | tf_op jit(solution)/shard_map/all_to_all | solution.py:292
  144.7 185.2 %factor.1 = (f32[192,256]{1,0:T(8,128)}, f32[256,256]{1,0:T(8,128)}) custom-call(f32[384,128]{1,0:T(8,128)S(1)} %bitcast.10, f32[192,256]{1,0:T(8,128)S(1)} %get-tuple-element.19.rows_ref), custom_call_target="tpu_custom_call" | custom-call | tf_op jit(solution)/shard_map/factor/pallas_call | solution.py:108
  (14 shorter events, 0.2 us)
Async XLA Ops:
  3.5 3.6 %collective-permute-start = (bf16[1536,128]{1,0:T(8,128)(2,1)S(1)}, bf16[1536,128]{1,0:T(8,128)(2,1)S(1)}, u32[]{:S(2)}, u32[]{:S(2)}) collective-permute-start(bf16[1536,128]{1,0:T(8,128)(2,1)S(1)} %get-tuple-element.12), channel_id=1, source_target_pairs={{0,1},{1,0},{2,3},{3,2},{4,5},{5,4},{6,7},{7,6},{8,9},{9,8},{10,11... | collective-permute-start | bytes 1179656 | tf_op jit(solution)/shard_map/ppermute | solution.py:269
  7.2 27.4 %collective-permute-start.1 = (bf16[1536,896]{1,0:T(8,128)(2,1)S(1)}, bf16[1536,896]{1,0:T(8,128)(2,1)S(1)}, u32[]{:S(2)}, u32[]{:S(2)}) collective-permute-start(bf16[1536,896]{1,0:T(8,128)(2,1)S(1)} %get-tuple-element.14.own_ref), channel_id=1, source_target_pairs={{0,1},{1,0},{2,3},{3,2},{4,5},{5,4},{6,7},{7,6},{8,9},{9,8},{10,11... | collective-permute-start | bytes 8257544 | tf_op jit(solution)/shard_map/ppermute | solution.py:269
  34.7 1.6 copy-start
  55.0 34.8 %copy-start.1 = (bf16[1536,896]{1,0:T(8,128)(2,1)S(1)}, bf16[1536,896]{1,0:T(8,128)(2,1)}, u32[]{:S(2)}) copy-start(bf16[1536,896]{1,0:T(8,128)(2,1)} %copy-done) | copy-start | bytes 8257540

commit v11 on v10

--- a/solution.py
+++ b/solution.py
@@ -89,7 +89,8 @@
         def eliminate(k, carry):
             line = work_ref[pl.ds(k, 1), :]
             pivot = jnp.sum(jnp.where(lane == k, line, 0.0), axis=1, keepdims=True)
-            line = line * lax.rsqrt(pivot)
+            scale = lax.rsqrt(pivot)
+            line = line * (scale * (1.5 - 0.5 * pivot * scale * scale))
             coef = jnp.where(lane[:, :K] > k, line[:, :K], 0.0)
             work_ref[...] = work_ref[...] - dot(coef, line, 0, 0, HIGH)
             work_ref[pl.ds(k, 1), :] = line
@@ -124,7 +125,11 @@
 STEPS = 8
 
 
-def opening_kernel(core_ref, me_ref, hidden_ref, right_ref, send_ref, keep_ref, hidden_out, right_buf, sems):
+def half_columns(core_ref):
+    return pl.ds(pl.multiple_of(core_ref[0] * HALF, HALF), HALF)
+
+
+def opening_kernel(core_ref, me_ref, hidden_ref, right_ref, first_ref, hidden_out, right_buf, sems):
     rows = hidden_out.shape[0] // STEPS
     blocks = [slice(i * rows, (i + 1) * rows) for i in range(STEPS)]
     copies = [pltpu.make_async_copy(right_ref, right_buf, sems.at[STEPS])]
@@ -134,24 +139,19 @@
         copy.start()
     for copy in copies:
         copy.wait()
-    first = dot(hidden_out[...], right_buf[...])
-    left, right = first[:, :HALF], first[:, HALF:]
-    send_ref[...] = jnp.where(core_ref[0] == 0, right, left).astype(send_ref.dtype)
-    keep_ref[...] = jnp.where(core_ref[0] == 0, left, right)
+    first_ref[...] = dot(hidden_out[...], right_buf[:, half_columns(core_ref)])
 
 
 def opening(core, me, hidden, right):
-    rows = hidden.shape[0]
     in_hbm = pl.BlockSpec(memory_space=pltpu.HBM)
     return pl.pallas_call(
         opening_kernel,
         out_shape=(
-            jax.ShapeDtypeStruct((rows, HALF), jnp.bfloat16),
-            jax.ShapeDtypeStruct((rows, HALF), jnp.float32),
+            jax.ShapeDtypeStruct((hidden.shape[0], HALF), jnp.float32),
             jax.ShapeDtypeStruct(hidden.shape, hidden.dtype),
         ),
         in_specs=[SCALAR, SCALAR, in_hbm, in_hbm],
-        out_specs=(WHOLE, WHOLE, WHOLE),
+        out_specs=(WHOLE, WHOLE),
         scratch_shapes=[pltpu.VMEM(right.shape, right.dtype), pltpu.SemaphoreType.DMA((STEPS + 1,))],
         compiler_params=PARAMS,
         name="opening",
@@ -163,26 +163,22 @@
     )
 
 
-def pieces_kernel(own_ref, landed_ref, hidden_ref, pieces_ref, _):
+def pieces_kernel(core_ref, own_ref, pair_ref, right_ref, pieces_ref):
     count, tile, _ = pieces_ref.shape
+    first = own_ref[...] + dot(pair_ref[...], right_ref[:, half_columns(core_ref)])
     for i in range(count):
-        block = slice(i * tile, (i + 1) * tile)
-        pieces_ref[i] = (own_ref[block, :] + landed_ref[block, :].astype(jnp.float32)).astype(pieces_ref.dtype)
-
-
-def first_pieces(own, landed, hidden, count):
+        pieces_ref[i] = first[i * tile : (i + 1) * tile, :].astype(pieces_ref.dtype)
+
+
+def first_pieces(core, own, pair, right, count):
     return pl.pallas_call(
         pieces_kernel,
-        out_shape=(
-            jax.ShapeDtypeStruct((count, own.shape[0] // count, HALF), jnp.bfloat16),
-            jax.ShapeDtypeStruct(hidden.shape, hidden.dtype),
-        ),
-        in_specs=[WHOLE] * 3,
-        out_specs=(WHOLE, WHOLE),
-        input_output_aliases={2: 1},
+        out_shape=jax.ShapeDtypeStruct((count, own.shape[0] // count, HALF), jnp.bfloat16),
+        in_specs=[SCALAR, WHOLE, WHOLE, WHOLE],
+        out_specs=WHOLE,
         compiler_params=PARAMS,
         name="first_pieces",
-    )(own, landed, hidden)
+    )(core, own, pair, right)
 
 
 def back_kernel(first_ref, own_ref, pair_ref, out_ref):
@@ -307,9 +303,9 @@
     total_rows = tok_rows * ys * zs
     core, me = (lax.axis_index(axis).reshape(1) for axis in ("core", COL))
 
-    send, keep, hidden = opening(core, me, hidden, test_matrix)
-    pieces, hidden = first_pieces(keep, swapped(send), hidden, xs)
-    pair = swapped(hidden)
+    pair, right = swapped(hidden), swapped(test_matrix)
+    own, hidden = opening(core, me, hidden, test_matrix)
+    pieces = first_pieces(core, own, pair, right, xs)
     first = (total(exchanged(pieces, "x")) * (1.0 / math.sqrt(D))).astype(bf16)
     first = exchanged(spread(first, xs), "x").reshape(tok_rows, HALF)
     local_back = local_backs(first, hidden, pair)

time: 333 us -> 333 us (level)
  transfers between devices with their start and end apart: 2 -> 2, of which waited for: 1 -> 1; matrix products, arithmetic and copies ran while one was open for 0% -> 0% of each run, Pallas kernels for 0% -> 1%
where the time goes in v11:
time: 333 us; the launch traced here: 330 us
  Pallas kernels  193 us (58%)
  blocking collectives  131 us (39%)
  starting transfers between devices  4.33 us (1%)
    pallas_call x1, Pallas kernels, factor_call(): pl.pallas_call(factor_kernel, out_shape=(jax.ShapeDtypeStruct(rows.shape,...  186 us
    all_to_all x10, blocking collectives, exchanged(): return lax.all_to_all(pieces, axis, 0, 0, axis_index_groups=groups)  131 us
  transfers between devices with their start and end apart: 2, of which 1 were waited for; matrix products, arithmetic and copies ran while one was open for 0% of the time, Pallas kernels for 1%

profile of v11, /device:TPU:6, one launch (start us, length us, event | category | flops | bytes accessed | tf_op | source)
XLA Modules:
  0.0 330.2 jit_solution(645786882059624496)
XLA Ops:
  0.6 1.9 collective-permute-start
  2.6 2.4 collective-permute-start.1
  5.0 2.8 opening.1
  7.8 0.0 copy-start
  7.8 0.7 collective-permute-done.1.right_ref
  8.5 0.0 collective-permute-done.pair_ref
  8.5 0.9 first_pieces.1
  9.4 14.8 %all_to_all.50 = bf16[4,384,128]{2,1,0:T(8,128)(2,1)S(1)} all-to-all(bf16[4,384,128]{2,1,0:T(8,128)(2,1)S(1)} %first_pieces.1), channel_id=1, replica_groups=mesh['y_hi'=4,'y_lo'=2,'z'=8,'x'=4,'core'=2] {'x'}, dimensions={0} | all-to-all | bytes 786432 | tf_op jit(solution)/shard_map/all_to_all | solution.py:288
  24.3 0.1 broadcast_in_dim.12
  24.4 10.2 %all_to_all.51 = bf16[4,384,128]{2,1,0:T(8,128)(2,1)S(1)} all-to-all(bf16[4,384,128]{2,1,0:T(8,128)(2,1)S(1)} %broadcast_in_dim.12), channel_id=1, replica_groups=mesh['y_hi'=4,'y_lo'=2,'z'=8,'x'=4,'core'=2] {'x'}, dimensions={0} | all-to-all | bytes 786432 | tf_op jit(solution)/shard_map/all_to_all | solution.py:288
  34.6 1.0 local_backs.1
  35.6 18.3 %all_to_all.52 = bf16[8,32,896]{2,1,0:T(8,128)(2,1)S(1)} all-to-all(bf16[8,32,896]{2,1,0:T(8,128)(2,1)S(1)} %bitcast.8), channel_id=1, replica_groups={{0,8,16,24,32,40,48,56},{2,10,18,26,34,42,50,58},{4,12,20,28,36,44,52,6..., dimensions={0} | all-to-all | bytes 917504 | tf_op jit(solution)/shard_map/all_to_all | solution.py:288
  53.9 0.1 reduce_sum.58
  54.0 19.6 %all_to_all.53 = bf16[8,32,896]{2,1,0:T(8,128)(2,1)S(1)} all-to-all(bf16[8,32,896]{2,1,0:T(8,128)(2,1)S(1)} %broadcast_in_dim.13), channel_id=1, replica_groups={{0,64,128,192,256,320,384,448},{2,66,130,194,258,322,386,450},{4,68,132..., dimensions={0} | all-to-all | bytes 917504 | tf_op jit(solution)/shard_map/all_to_all | solution.py:288
  73.7 0.1 convert_reduce_fusion
  73.8 15.0 %all_to_all.54 = bf16[8,32,896]{2,1,0:T(8,128)(2,1)S(1)} all-to-all(bf16[8,32,896]{2,1,0:T(8,128)(2,1)S(1)} %broadcast_in_dim.14), channel_id=1, replica_groups={{0,8,16,24,32,40,48,56},{2,10,18,26,34,42,50,58},{4,12,20,28,36,44,52,6..., dimensions={0} | all-to-all | bytes 917504 | tf_op jit(solution)/shard_map/all_to_all | solution.py:288
  88.8 1.7 sketch_pieces.1
  90.5 11.3 %all_to_all.55.refs_1_ = bf16[8,192,128]{2,1,0:T(8,128)(2,1)S(1)} all-to-all(bf16[8,192,128]{2,1,0:T(8,128)(2,1)S(1)} %get-tuple-element.10), channel_id=1, replica_groups=mesh['y_hi'=4,'y_lo'=2,'z'=8,'x'=4,'core'=2] {'x','core'}, dimensions={0} | all-to-all | bytes 786432 | tf_op jit(solution)/shard_map/all_to_all | solution.py:288
  101.8 0.5 rows_and_gram.1
  102.3 9.7 %all_to_all.56 = f32[16,24,128]{2,1,0:T(8,128)S(1)} all-to-all(f32[16,24,128]{2,1,0:T(8,128)S(1)} %bitcast.11), channel_id=1, replica_groups=mesh['y_hi'=4,'y_lo'=2,'z'=8,'x'=4,'core'=2] {'y_lo','x','core'}, dimensions={0} | all-to-all | bytes 393216 | tf_op jit(solution)/shard_map/all_to_all | solution.py:288
  112.1 11.5 %all_to_all.57 = f32[8,24,128]{2,1,0:T(8,128)S(1)} all-to-all(f32[8,24,128]{2,1,0:T(8,128)S(1)} %broadcast_in_dim.15), channel_id=1, replica_groups=mesh['y_hi'=4,'y_lo'=2,'z'=8,'x'=4,'core'=2] {'z'}, dimensions={0} | all-to-all | bytes 196608 | tf_op jit(solution)/shard_map/all_to_all | solution.py:288
  123.6 10.4 %all_to_all.58 = f32[4,24,128]{2,1,0:T(8,128)S(1)} all-to-all(f32[4,24,128]{2,1,0:T(8,128)S(1)} %broadcast_in_dim.16), channel_id=1, replica_groups=mesh['y_hi'=4,'y_lo'=2,'z'=8,'x'=4,'core'=2] {'y_hi'}, dimensions={0} | all-to-all | bytes 98304 | tf_op jit(solution)/shard_map/all_to_all | solution.py:288
  134.1 9.6 %all_to_all.59 = f32[16,24,128]{2,1,0:T(8,128)S(1)} all-to-all(f32[16,24,128]{2,1,0:T(8,128)S(1)} %broadcast_in_dim.17), channel_id=1, replica_groups=mesh['y_hi'=4,'y_lo'=2,'z'=8,'x'=4,'core'=2] {'y_lo','x','core'}, dimensions={0} | all-to-all | bytes 393216 | tf_op jit(solution)/shard_map/all_to_all | solution.py:288
  143.7 186.5 %factor.1 = (f32[192,256]{1,0:T(8,128)}, f32[256,256]{1,0:T(8,128)}) custom-call(f32[384,128]{1,0:T(8,128)S(1)} %bitcast.10, f32[192,256]{1,0:T(8,128)S(1)} %get-tuple-element.13.rows_ref), custom_call_target="tpu_custom_call" | custom-call | tf_op jit(solution)/shard_map/factor/pallas_call | solution.py:109
  (14 shorter events, 0.2 us)
Async XLA Ops:
  0.6 7.9 %collective-permute-start = (bf16[1536,896]{1,0:T(8,128)(2,1)}, bf16[1536,896]{1,0:T(8,128)(2,1)S(1)}, u32[]{:S(2)}, u32[]{:S(2)}) collective-permute-start(bf16[1536,896]{1,0:T(8,128)(2,1)} %hidden_ref.1), channel_id=1, source_target_pairs={{0,1},{1,0},{2,3},{3,2},{4,5},{5,4},{6,7},{7,6},{8,9},{9,8},{10,11... | collective-permute-start | bytes 8257544 | tf_op jit(solution)/shard_map/ppermute | solution.py:265
  2.6 5.9 %collective-permute-start.1 = (bf16[896,256]{1,0:T(8,128)(2,1)}, bf16[896,256]{1,0:T(8,128)(2,1)S(1)}, u32[]{:S(2)}, u32[]{:S(2)}) collective-permute-start(bf16[896,256]{1,0:T(8,128)(2,1)} %right_ref.1), channel_id=1, source_target_pairs={{0,1},{1,0},{2,3},{3,2},{4,5},{5,4},{6,7},{7,6},{8,9},{9,8},{10,11... | collective-permute-start | bytes 1376264 | tf_op jit(solution)/shard_map/ppermute | solution.py:265
  7.8 26.8 %copy-start = (bf16[1536,896]{1,0:T(8,128)(2,1)}, bf16[1536,896]{1,0:T(8,128)(2,1)S(1)}, u32[]{:S(2)}) copy-start(bf16[1536,896]{1,0:T(8,128)(2,1)S(1)} %get-tuple-element.8.own_ref) | copy-start | bytes 8257540
  54.0 34.8 %copy-start.1 = (bf16[1536,896]{1,0:T(8,128)(2,1)S(1)}, bf16[1536,896]{1,0:T(8,128)(2,1)}, u32[]{:S(2)}) copy-start(bf16[1536,896]{1,0:T(8,128)(2,1)} %copy-done) | copy-start | bytes 8257540

commit v12 on v11

--- a/solution.py
+++ b/solution.py
@@ -129,7 +129,7 @@
     return pl.ds(pl.multiple_of(core_ref[0] * HALF, HALF), HALF)
 
 
-def opening_kernel(core_ref, me_ref, hidden_ref, right_ref, first_ref, hidden_out, right_buf, sems):
+def opening_kernel(core_ref, hidden_ref, right_ref, first_ref, hidden_out, right_buf, sems):
     rows = hidden_out.shape[0] // STEPS
     blocks = [slice(i * rows, (i + 1) * rows) for i in range(STEPS)]
     copies = [pltpu.make_async_copy(right_ref, right_buf, sems.at[STEPS])]
@@ -142,7 +142,7 @@
     first_ref[...] = dot(hidden_out[...], right_buf[:, half_columns(core_ref)])
 
 
-def opening(core, me, hidden, right):
+def opening(core, hidden, right):
     in_hbm = pl.BlockSpec(memory_space=pltpu.HBM)
     return pl.pallas_call(
         opening_kernel,
@@ -150,14 +150,13 @@
             jax.ShapeDtypeStruct((hidden.shape[0], HALF), jnp.float32),
             jax.ShapeDtypeStruct(hidden.shape, hidden.dtype),
         ),
-        in_specs=[SCALAR, SCALAR, in_hbm, in_hbm],
+        in_specs=[SCALAR, in_hbm, in_hbm],
         out_specs=(WHOLE, WHOLE),
         scratch_shapes=[pltpu.VMEM(right.shape, right.dtype), pltpu.SemaphoreType.DMA((STEPS + 1,))],
         compiler_params=PARAMS,
         name="opening",
     )(
         core,
-        me,
         pltpu.with_memory_space_constraint(hidden, pltpu.HBM),
         pltpu.with_memory_space_constraint(right, pltpu.HBM),
     )
@@ -198,40 +197,25 @@
     )(first, own, pair)
 
 
-def sketch_kernel(me_ref, own_ref, pair_ref, back_ref, mine_ref, pieces_ref):
-    count, tile, _ = pieces_ref.shape
-    sketch = dot(own_ref[...], back_ref[:HALF, :], 1, 1) + dot(pair_ref[...], back_ref[HALF:, :], 1, 1)
-    for i in range(count):
-        block = sketch[i * tile : (i + 1) * tile, :]
-        pieces_ref[i] = block.astype(pieces_ref.dtype)
-
-        @pl.when(me_ref[0] == i)
-        def _():
-            mine_ref[...] = block
-
-
-def sketch_pieces(me, own, pair, back, count):
-    tile = own.shape[0] // count
+def sketch_kernel(own_ref, pair_ref, back_ref, out_ref):
+    out_ref[...] = dot(own_ref[...], back_ref[:HALF, :], 1, 1) + dot(pair_ref[...], back_ref[HALF:, :], 1, 1)
+
+
+def partial_sketch(own, pair, back):
     return pl.pallas_call(
         sketch_kernel,
-        out_shape=(
-            jax.ShapeDtypeStruct((tile, HALF), jnp.float32),
-            jax.ShapeDtypeStruct((count, tile, HALF), jnp.bfloat16),
-        ),
-        in_specs=[SCALAR, WHOLE, WHOLE, WHOLE],
-        out_specs=(WHOLE, WHOLE),
-        compiler_params=PARAMS,
-        name="sketch_pieces",
-    )(me, own, pair, back)
-
-
-def gram_kernel(scale, me_ref, landed_ref, own_ref, rows_ref, packed_ref):
+        out_shape=jax.ShapeDtypeStruct((own.shape[0], HALF), jnp.float32),
+        in_specs=[WHOLE] * 3,
+        out_specs=WHOLE,
+        compiler_params=PARAMS,
+        name="partial_sketch",
+    )(own, pair, back)
+
+
+def gram_kernel(scale, landed_ref, rows_ref, packed_ref):
     halves = []
     for half in range(2):
-        parts = [
-            jnp.where(me_ref[0] == i, own_ref[...], landed_ref[i].astype(jnp.float32))
-            for i in range(half, landed_ref.shape[0], 2)
-        ]
+        parts = [landed_ref[i] for i in range(half, landed_ref.shape[0], 2)]
         halves.append(sum(parts[1:], parts[0]))
     left, right = halves
     rows_ref[:, :HALF] = left
@@ -241,18 +225,18 @@
     packed_ref[2 * HALF :, :] = dot(right, right, 0, 0, HIGH) * scale
 
 
-def rows_and_gram(me, landed, own, scale):
+def rows_and_gram(landed, scale):
     return pl.pallas_call(
         lambda *refs: gram_kernel(scale, *refs),
         out_shape=(
-            jax.ShapeDtypeStruct((own.shape[0], K), jnp.float32),
+            jax.ShapeDtypeStruct((landed.shape[1], K), jnp.float32),
             jax.ShapeDtypeStruct((3 * HALF, HALF), jnp.float32),
         ),
-        in_specs=[SCALAR, WHOLE, WHOLE],
+        in_specs=[WHOLE],
         out_specs=(WHOLE, WHOLE),
         compiler_params=PARAMS,
         name="rows_and_gram",
-    )(me, landed, own)
+    )(landed)
 
 
 ROW = ("y_hi", "y_lo", "z")
@@ -301,10 +285,10 @@
     tok_rows, width = hidden.shape
     ys, zs, xs = sizes
     total_rows = tok_rows * ys * zs
-    core, me = (lax.axis_index(axis).reshape(1) for axis in ("core", COL))
+    core = lax.axis_index("core").reshape(1)
 
     pair, right = swapped(hidden), swapped(test_matrix)
-    own, hidden = opening(core, me, hidden, test_matrix)
+    own, hidden = opening(core, hidden, test_matrix)
     pieces = first_pieces(core, own, pair, right, xs)
     first = (total(exchanged(pieces, "x")) * (1.0 / math.sqrt(D))).astype(bf16)
     first = exchanged(spread(first, xs), "x").reshape(tok_rows, HALF)
@@ -319,8 +303,8 @@
     my_back = (my_back * (1.0 / total_rows)).astype(bf16)
     back = exchanged(spread(my_back, count), ALL, this_way).reshape(K, width)
 
-    own, pieces = sketch_pieces(me, hidden, pair, back, 2 * xs)
-    my_rows, gram = rows_and_gram(me, exchanged(pieces, COL), own, 1.0 / total_rows)
+    pieces = partial_sketch(hidden, pair, back).reshape(2 * xs, tok_rows // (2 * xs), HALF)
+    my_rows, gram = rows_and_gram(exchanged(pieces, COL), 1.0 / total_rows)
     count = 4 * xs
     gram = total(exchanged(gram.reshape(count, 3 * HALF // count, HALF), NEAR))
     gram = total(exchanged(spread(gram, zs), "z"))

time: 333 us -> 337 us (1.012)
  blocking collectives: 131 us -> 135 us
    all_to_all x10, blocking collectives: 131 us -> 135 us  [exchanged(): return lax.all_to_all(pieces, axis, 0, 0, axis_index_groups=groups)]
where the time goes in v12:
time: 337 us; the launch traced here: 334 us
  Pallas kernels  193 us (57%)
  blocking collectives  135 us (40%)
  starting transfers between devices  4.33 us (1%)
    pallas_call x1, Pallas kernels, factor_call(): pl.pallas_call(factor_kernel, out_shape=(jax.ShapeDtypeStruct(rows.shape,...  186 us
    all_to_all x10, blocking collectives, exchanged(): return lax.all_to_all(pieces, axis, 0, 0, axis_index_groups=groups)  135 us
  transfers between devices with their start and end apart: 2, of which 1 were waited for; matrix products, arithmetic and copies ran while one was open for 0% of the time, Pallas kernels for 1%

profile of v12, /device:TPU:6, one launch (start us, length us, event | category | flops | bytes accessed | tf_op | source)
XLA Modules:
  0.0 334.4 jit_solution(11294014278230157264)
XLA Ops:
  0.6 1.9 collective-permute-start
  2.6 2.4 collective-permute-start.1
  5.0 2.8 opening.1
  7.8 0.7 collective-permute-done.1.right_ref
  8.5 0.0 collective-permute-done.pair_ref
  8.5 0.9 first_pieces.1
  9.4 14.8 %all_to_all.50 = bf16[4,384,128]{2,1,0:T(8,128)(2,1)S(1)} all-to-all(bf16[4,384,128]{2,1,0:T(8,128)(2,1)S(1)} %first_pieces.1), channel_id=1, replica_groups=mesh['y_hi'=4,'y_lo'=2,'z'=8,'x'=4,'core'=2] {'x'}, dimensions={0} | all-to-all | bytes 786432 | tf_op jit(solution)/shard_map/all_to_all | solution.py:272
  24.3 0.1 broadcast_in_dim.12
  24.4 10.2 %all_to_all.51 = bf16[4,384,128]{2,1,0:T(8,128)(2,1)S(1)} all-to-all(bf16[4,384,128]{2,1,0:T(8,128)(2,1)S(1)} %broadcast_in_dim.12), channel_id=1, replica_groups=mesh['y_hi'=4,'y_lo'=2,'z'=8,'x'=4,'core'=2] {'x'}, dimensions={0} | all-to-all | bytes 786432 | tf_op jit(solution)/shard_map/all_to_all | solution.py:272
  34.6 0.0 copy-done
  34.6 1.0 local_backs.1
  35.6 18.3 %all_to_all.52 = bf16[8,32,896]{2,1,0:T(8,128)(2,1)S(1)} all-to-all(bf16[8,32,896]{2,1,0:T(8,128)(2,1)S(1)} %bitcast.9), channel_id=1, replica_groups={{0,8,16,24,32,40,48,56},{2,10,18,26,34,42,50,58},{4,12,20,28,36,44,52,6..., dimensions={0} | all-to-all | bytes 917504 | tf_op jit(solution)/shard_map/all_to_all | solution.py:272
  53.9 0.1 reduce_sum.58
  54.0 19.6 %all_to_all.53 = bf16[8,32,896]{2,1,0:T(8,128)(2,1)S(1)} all-to-all(bf16[8,32,896]{2,1,0:T(8,128)(2,1)S(1)} %broadcast_in_dim.13), channel_id=1, replica_groups={{0,64,128,192,256,320,384,448},{2,66,130,194,258,322,386,450},{4,68,132..., dimensions={0} | all-to-all | bytes 917504 | tf_op jit(solution)/shard_map/all_to_all | solution.py:272
  73.7 0.1 convert_reduce_fusion
  73.8 15.0 %all_to_all.54 = bf16[8,32,896]{2,1,0:T(8,128)(2,1)S(1)} all-to-all(bf16[8,32,896]{2,1,0:T(8,128)(2,1)S(1)} %broadcast_in_dim.14), channel_id=1, replica_groups={{0,8,16,24,32,40,48,56},{2,10,18,26,34,42,50,58},{4,12,20,28,36,44,52,6..., dimensions={0} | all-to-all | bytes 917504 | tf_op jit(solution)/shard_map/all_to_all | solution.py:272
  88.8 1.6 partial_sketch.1
  90.4 15.7 %all_to_all.55.refs_0_ = f32[8,192,128]{2,1,0:T(8,128)S(1)} all-to-all(f32[8,192,128]{2,1,0:T(8,128)S(1)} %bitcast.7), channel_id=1, replica_groups=mesh['y_hi'=4,'y_lo'=2,'z'=8,'x'=4,'core'=2] {'x','core'}, dimensions={0} | all-to-all | bytes 1572864 | tf_op jit(solution)/shard_map/all_to_all | solution.py:272
  106.1 0.5 rows_and_gram.1
  106.6 9.7 %all_to_all.56 = f32[16,24,128]{2,1,0:T(8,128)S(1)} all-to-all(f32[16,24,128]{2,1,0:T(8,128)S(1)} %bitcast.12), channel_id=1, replica_groups=mesh['y_hi'=4,'y_lo'=2,'z'=8,'x'=4,'core'=2] {'y_lo','x','core'}, dimensions={0} | all-to-all | bytes 393216 | tf_op jit(solution)/shard_map/all_to_all | solution.py:272
  116.4 11.5 %all_to_all.57 = f32[8,24,128]{2,1,0:T(8,128)S(1)} all-to-all(f32[8,24,128]{2,1,0:T(8,128)S(1)} %broadcast_in_dim.15), channel_id=1, replica_groups=mesh['y_hi'=4,'y_lo'=2,'z'=8,'x'=4,'core'=2] {'z'}, dimensions={0} | all-to-all | bytes 196608 | tf_op jit(solution)/shard_map/all_to_all | solution.py:272
  127.9 10.4 %all_to_all.58 = f32[4,24,128]{2,1,0:T(8,128)S(1)} all-to-all(f32[4,24,128]{2,1,0:T(8,128)S(1)} %broadcast_in_dim.16), channel_id=1, replica_groups=mesh['y_hi'=4,'y_lo'=2,'z'=8,'x'=4,'core'=2] {'y_hi'}, dimensions={0} | all-to-all | bytes 98304 | tf_op jit(solution)/shard_map/all_to_all | solution.py:272
  138.3 9.6 %all_to_all.59 = f32[16,24,128]{2,1,0:T(8,128)S(1)} all-to-all(f32[16,24,128]{2,1,0:T(8,128)S(1)} %broadcast_in_dim.17), channel_id=1, replica_groups=mesh['y_hi'=4,'y_lo'=2,'z'=8,'x'=4,'core'=2] {'y_lo','x','core'}, dimensions={0} | all-to-all | bytes 393216 | tf_op jit(solution)/shard_map/all_to_all | solution.py:272
  147.9 186.5 %factor.1 = (f32[192,256]{1,0:T(8,128)}, f32[256,256]{1,0:T(8,128)}) custom-call(f32[384,128]{1,0:T(8,128)S(1)} %bitcast.11, f32[192,256]{1,0:T(8,128)S(1)} %get-tuple-element.9.rows_ref), custom_call_target="tpu_custom_call" | custom-call | tf_op jit(solution)/shard_map/factor/pallas_call | solution.py:109
  (14 shorter events, 0.2 us)
Async XLA Ops:
  0.6 7.9 %collective-permute-start = (bf16[1536,896]{1,0:T(8,128)(2,1)}, bf16[1536,896]{1,0:T(8,128)(2,1)S(1)}, u32[]{:S(2)}, u32[]{:S(2)}) collective-permute-start(bf16[1536,896]{1,0:T(8,128)(2,1)} %hidden_ref.1), channel_id=1, source_target_pairs={{0,1},{1,0},{2,3},{3,2},{4,5},{5,4},{6,7},{7,6},{8,9},{9,8},{10,11... | collective-permute-start | bytes 8257544 | tf_op jit(solution)/shard_map/ppermute | solution.py:249
  2.6 5.9 %collective-permute-start.1 = (bf16[896,256]{1,0:T(8,128)(2,1)}, bf16[896,256]{1,0:T(8,128)(2,1)S(1)}, u32[]{:S(2)}, u32[]{:S(2)}) collective-permute-start(bf16[896,256]{1,0:T(8,128)(2,1)} %right_ref.1), channel_id=1, source_target_pairs={{0,1},{1,0},{2,3},{3,2},{4,5},{5,4},{6,7},{7,6},{8,9},{9,8},{10,11... | collective-permute-start | bytes 1376264 | tf_op jit(solution)/shard_map/ppermute | solution.py:249
  7.8 26.8 %copy-start = (bf16[1536,896]{1,0:T(8,128)(2,1)}, bf16[1536,896]{1,0:T(8,128)(2,1)S(1)}, u32[]{:S(2)}) copy-start(bf16[1536,896]{1,0:T(8,128)(2,1)S(1)} %get-tuple-element.6.own_ref) | copy-start | bytes 8257540
  54.0 34.8 %copy-start.1 = (bf16[1536,896]{1,0:T(8,128)(2,1)S(1)}, bf16[1536,896]{1,0:T(8,128)(2,1)}, u32[]{:S(2)}) copy-start(bf16[1536,896]{1,0:T(8,128)(2,1)} %copy-done) | copy-start | bytes 8257540

commit v13 on v11

--- a/solution.py
+++ b/solution.py
@@ -78,7 +78,11 @@
     def _():
         x = x_ref[...]
         last = ((g_ref[...] - eye) * upper).astype(bf16)
-        x_ref[...] = x - dot(x.astype(bf16), last)
+        x = jnp.where(row <= col, x - dot(x.astype(bf16), last), 0.0)
+        (x_high, x_low), (r_high, r_low), (g_high, g_low) = terms(x), terms(rows_ref[...]), terms(gram_ref[...])
+        basis_ref[...] = dot(r_high, x_high) + (dot(r_high, x_low) + dot(r_low, x_high))
+        factor = dot(x_high, g_high, 0) + (dot(x_high, g_low, 0) + dot(x_low, g_high, 0))
+        factor_ref[...] = jnp.where(row <= col, factor, 0.0)
 
     @pl.when(jnp.logical_not(ok))
     def _():
@@ -97,11 +101,9 @@
             return carry
 
         lax.fori_loop(0, K, eliminate, 0)
-        x_ref[...] = work_ref[:, K:].T
-
-    x = jnp.where(row <= col, x_ref[...], 0.0)
-    basis_ref[...] = dot(rows_ref[...], x, precision=HIGH)
-    factor_ref[...] = jnp.where(row <= col, dot(x, gram_ref[...], 0, 0, HIGH), 0.0)
+        x = jnp.where(row <= col, work_ref[:, K:].T, 0.0)
+        basis_ref[...] = dot(rows_ref[...], x, precision=HIGH)
+        factor_ref[...] = jnp.where(row <= col, work_ref[:, :K], 0.0)
 
 
 def factor_call(packed, rows):

time: 333 us -> 333 us (level)
  no operation moved by 1% of the time
where the time goes in v13:
time: 333 us; the launch traced here: 330 us
  Pallas kernels  193 us (58%)
  blocking collectives  131 us (39%)
  starting transfers between devices  4.33 us (1%)
    pallas_call x1, Pallas kernels, factor_call(): pl.pallas_call(factor_kernel, out_shape=(jax.ShapeDtypeStruct(rows.shape,...  186 us
    all_to_all x10, blocking collectives, exchanged(): return lax.all_to_all(pieces, axis, 0, 0, axis_index_groups=groups)  131 us
  transfers between devices with their start and end apart: 2, of which 1 were waited for; matrix products, arithmetic and copies ran while one was open for 0% of the time, Pallas kernels for 1%

profile of v13, /device:TPU:6, one launch (start us, length us, event | category | flops | bytes accessed | tf_op | source)
XLA Modules:
  0.0 329.9 jit_solution(12108371485798155338)
XLA Ops:
  0.6 1.9 collective-permute-start
  2.6 2.4 collective-permute-start.1
  5.0 2.8 opening.1
  7.8 0.7 collective-permute-done.1.right_ref
  8.5 0.0 collective-permute-done.pair_ref
  8.5 0.9 first_pieces.1
  9.4 14.8 %all_to_all.50 = bf16[4,384,128]{2,1,0:T(8,128)(2,1)S(1)} all-to-all(bf16[4,384,128]{2,1,0:T(8,128)(2,1)S(1)} %first_pieces.1), channel_id=1, replica_groups=mesh['y_hi'=4,'y_lo'=2,'z'=8,'x'=4,'core'=2] {'x'}, dimensions={0} | all-to-all | bytes 786432 | tf_op jit(solution)/shard_map/all_to_all | solution.py:290
  24.3 0.1 broadcast_in_dim.12
  24.4 10.2 %all_to_all.51 = bf16[4,384,128]{2,1,0:T(8,128)(2,1)S(1)} all-to-all(bf16[4,384,128]{2,1,0:T(8,128)(2,1)S(1)} %broadcast_in_dim.12), channel_id=1, replica_groups=mesh['y_hi'=4,'y_lo'=2,'z'=8,'x'=4,'core'=2] {'x'}, dimensions={0} | all-to-all | bytes 786432 | tf_op jit(solution)/shard_map/all_to_all | solution.py:290
  34.6 0.0 copy-done
  34.6 1.0 local_backs.1
  35.6 18.3 %all_to_all.52 = bf16[8,32,896]{2,1,0:T(8,128)(2,1)S(1)} all-to-all(bf16[8,32,896]{2,1,0:T(8,128)(2,1)S(1)} %bitcast.8), channel_id=1, replica_groups={{0,8,16,24,32,40,48,56},{2,10,18,26,34,42,50,58},{4,12,20,28,36,44,52,6..., dimensions={0} | all-to-all | bytes 917504 | tf_op jit(solution)/shard_map/all_to_all | solution.py:290
  53.9 0.1 reduce_sum.58
  54.0 19.6 %all_to_all.53 = bf16[8,32,896]{2,1,0:T(8,128)(2,1)S(1)} all-to-all(bf16[8,32,896]{2,1,0:T(8,128)(2,1)S(1)} %broadcast_in_dim.13), channel_id=1, replica_groups={{0,64,128,192,256,320,384,448},{2,66,130,194,258,322,386,450},{4,68,132..., dimensions={0} | all-to-all | bytes 917504 | tf_op jit(solution)/shard_map/all_to_all | solution.py:290
  73.7 0.1 convert_reduce_fusion
  73.8 15.0 %all_to_all.54 = bf16[8,32,896]{2,1,0:T(8,128)(2,1)S(1)} all-to-all(bf16[8,32,896]{2,1,0:T(8,128)(2,1)S(1)} %broadcast_in_dim.14), channel_id=1, replica_groups={{0,8,16,24,32,40,48,56},{2,10,18,26,34,42,50,58},{4,12,20,28,36,44,52,6..., dimensions={0} | all-to-all | bytes 917504 | tf_op jit(solution)/shard_map/all_to_all | solution.py:290
  88.8 1.7 sketch_pieces.1
  90.5 11.3 %all_to_all.55.refs_1_ = bf16[8,192,128]{2,1,0:T(8,128)(2,1)S(1)} all-to-all(bf16[8,192,128]{2,1,0:T(8,128)(2,1)S(1)} %get-tuple-element.10), channel_id=1, replica_groups=mesh['y_hi'=4,'y_lo'=2,'z'=8,'x'=4,'core'=2] {'x','core'}, dimensions={0} | all-to-all | bytes 786432 | tf_op jit(solution)/shard_map/all_to_all | solution.py:290
  101.8 0.5 rows_and_gram.1
  102.3 9.7 %all_to_all.56 = f32[16,24,128]{2,1,0:T(8,128)S(1)} all-to-all(f32[16,24,128]{2,1,0:T(8,128)S(1)} %bitcast.11), channel_id=1, replica_groups=mesh['y_hi'=4,'y_lo'=2,'z'=8,'x'=4,'core'=2] {'y_lo','x','core'}, dimensions={0} | all-to-all | bytes 393216 | tf_op jit(solution)/shard_map/all_to_all | solution.py:290
  112.1 11.5 %all_to_all.57 = f32[8,24,128]{2,1,0:T(8,128)S(1)} all-to-all(f32[8,24,128]{2,1,0:T(8,128)S(1)} %broadcast_in_dim.15), channel_id=1, replica_groups=mesh['y_hi'=4,'y_lo'=2,'z'=8,'x'=4,'core'=2] {'z'}, dimensions={0} | all-to-all | bytes 196608 | tf_op jit(solution)/shard_map/all_to_all | solution.py:290
  123.6 10.4 %all_to_all.58 = f32[4,24,128]{2,1,0:T(8,128)S(1)} all-to-all(f32[4,24,128]{2,1,0:T(8,128)S(1)} %broadcast_in_dim.16), channel_id=1, replica_groups=mesh['y_hi'=4,'y_lo'=2,'z'=8,'x'=4,'core'=2] {'y_hi'}, dimensions={0} | all-to-all | bytes 98304 | tf_op jit(solution)/shard_map/all_to_all | solution.py:290
  134.1 9.6 %all_to_all.59 = f32[16,24,128]{2,1,0:T(8,128)S(1)} all-to-all(f32[16,24,128]{2,1,0:T(8,128)S(1)} %broadcast_in_dim.17), channel_id=1, replica_groups=mesh['y_hi'=4,'y_lo'=2,'z'=8,'x'=4,'core'=2] {'y_lo','x','core'}, dimensions={0} | all-to-all | bytes 393216 | tf_op jit(solution)/shard_map/all_to_all | solution.py:290
  143.7 186.2 %factor.1 = (f32[192,256]{1,0:T(8,128)}, f32[256,256]{1,0:T(8,128)}) custom-call(f32[384,128]{1,0:T(8,128)S(1)} %bitcast.10, f32[192,256]{1,0:T(8,128)S(1)} %get-tuple-element.13.rows_ref), custom_call_target="tpu_custom_call" | custom-call | tf_op jit(solution)/shard_map/factor/pallas_call | solution.py:111
  (14 shorter events, 0.2 us)
Async XLA Ops:
  0.6 7.9 %collective-permute-start = (bf16[1536,896]{1,0:T(8,128)(2,1)}, bf16[1536,896]{1,0:T(8,128)(2,1)S(1)}, u32[]{:S(2)}, u32[]{:S(2)}) collective-permute-start(bf16[1536,896]{1,0:T(8,128)(2,1)} %hidden_ref.1), channel_id=1, source_target_pairs={{0,1},{1,0},{2,3},{3,2},{4,5},{5,4},{6,7},{7,6},{8,9},{9,8},{10,11... | collective-permute-start | bytes 8257544 | tf_op jit(solution)/shard_map/ppermute | solution.py:267
  2.6 5.9 %collective-permute-start.1 = (bf16[896,256]{1,0:T(8,128)(2,1)}, bf16[896,256]{1,0:T(8,128)(2,1)S(1)}, u32[]{:S(2)}, u32[]{:S(2)}) collective-permute-start(bf16[896,256]{1,0:T(8,128)(2,1)} %right_ref.1), channel_id=1, source_target_pairs={{0,1},{1,0},{2,3},{3,2},{4,5},{5,4},{6,7},{7,6},{8,9},{9,8},{10,11... | collective-permute-start | bytes 1376264 | tf_op jit(solution)/shard_map/ppermute | solution.py:267
  7.8 26.8 %copy-start = (bf16[1536,896]{1,0:T(8,128)(2,1)}, bf16[1536,896]{1,0:T(8,128)(2,1)S(1)}, u32[]{:S(2)}) copy-start(bf16[1536,896]{1,0:T(8,128)(2,1)S(1)} %get-tuple-element.8.own_ref) | copy-start | bytes 8257540
  54.0 34.8 %copy-start.1 = (bf16[1536,896]{1,0:T(8,128)(2,1)S(1)}, bf16[1536,896]{1,0:T(8,128)(2,1)}, u32[]{:S(2)}) copy-start(bf16[1536,896]{1,0:T(8,128)(2,1)} %copy-done) | copy-start | bytes 8257540
